TPU v7x, 32 devices: a whole 2x2x4 slice. The times are simulated.
32 devices in a mesh: tm: 8 (over z, y), patch: 4 (over x, core).
Axes of the slice: x: 2, y: 2, z: 4, core: 2. Of those that a mesh axis runs over, the one named last changes fastest.
Arguments:
- tokens: bfloat16 [64, 256, 768], P('tm', 'patch'), may hold values from -5 to 5
- time_gain: float32 [768], replicated, may hold values from 0.25 to 1.75
- time_proj: bfloat16 [768, 2304], replicated, may hold values from -1 to 1
- time_out: bfloat16 [768, 768], replicated, may hold values from -0.375 to 0.375
- time_scale: float32 [12], replicated, may hold values from 2 to 260
- space_gain: float32 [768], replicated, may hold values from 0.25 to 1.75
- space_proj: bfloat16 [768, 2304], replicated, may hold values from -1 to 1
- space_out: bfloat16 [768, 768], replicated, may hold values from -0.375 to 0.375
- space_scale: float32 [12], replicated, may hold values from 2 to 260
Outputs:
- block_out: bfloat16 [64, 256, 768], P('tm', 'patch')
All inputs are finite; a program needn't handle non-finite values.
Results may differ from a plain program's by a relative error of at most 0.012.
The roundings to bfloat16 on the way count: a program that leaves them out, or rounds other values in their place, can miss the bound.
Values may be sent and summed in bfloat16 or wider, within the bound.
No kernel may reach another device: no remote copies, remote signals or barrier semaphores. Data moves between devices by JAX's collectives and lax.ppermute only.
A program may use at most 128 MiB of HBM per device.

v0:
```python
import jax
import jax.numpy as jnp
from jax import lax
from jax.sharding import PartitionSpec as P

HEADS = 12
HEAD_DIM = 64


EPSILON = 1e-06


def layer_norm(values, gain_vector):
    widened = values.astype(jnp.float32)
    centred = widened - jnp.mean(widened, axis=-1, keepdims=True)
    spread = jnp.mean(centred * centred, axis=-1, keepdims=True)
    return (centred * lax.rsqrt(spread + EPSILON) * gain_vector).astype(jnp.bfloat16)


def project(normed, weight):
    flat = normed.reshape(-1, normed.shape[-1])
    fields = jnp.dot(flat, weight, preferred_element_type=jnp.float32)
    pieces = fields.reshape(fields.shape[:-1] + (3, HEADS, HEAD_DIM))
    paired = pieces[:, :2]
    paired = paired * lax.rsqrt(jnp.sum(paired * paired, axis=-1, keepdims=True) + EPSILON)
    joined = jnp.concatenate([paired, pieces[:, 2:]], axis=1)
    return joined.reshape(normed.shape[:-1] + (3 * HEADS * HEAD_DIM,)).astype(jnp.bfloat16)


def softmax_mix(scores, values, pattern):
    largest = jnp.max(scores, axis=-1, keepdims=True)
    powers = jnp.exp(scores - largest)
    totals = jnp.sum(powers, axis=-1, keepdims=True)
    attended = jnp.einsum(
        pattern, powers.astype(jnp.bfloat16), values, preferred_element_type=jnp.float32
    )
    return (attended, totals)


def attend_time(packed, scales):
    frames, item_count = (packed.shape[0], packed.shape[1])
    pieces = packed.reshape(frames, item_count, 3, HEADS, HEAD_DIM)
    key_rows = pieces[:, :, 1]
    value_rows = pieces[:, :, 2]
    block_rows = min(frames, 512)
    queries = pieces[:, :, 0].reshape(frames // block_rows, block_rows, item_count, HEADS, HEAD_DIM)

    def single(query_rows):
        scores = jnp.einsum(
            "qihd,kihd->ihqk", query_rows, key_rows, preferred_element_type=jnp.float32
        )
        scores = scores * scales[None, :, None, None]
        attended, totals = softmax_mix(scores, value_rows, "ihqk,kihd->qihd")
        return (attended / jnp.transpose(totals, (2, 0, 1, 3))).astype(jnp.bfloat16)

    result = lax.map(single, queries)
    return result.reshape(frames, item_count, HEADS * HEAD_DIM)


def attend_space(queries, key_rows, values, scales):
    scores = jnp.einsum("fqhd,fkhd->fhqk", queries, key_rows, preferred_element_type=jnp.float32)
    scores = scores * scales[None, :, None, None]
    attended, totals = softmax_mix(scores, values, "fhqk,fkhd->fqhd")
    averaged = attended / jnp.swapaxes(totals, 1, 2)
    return averaged.astype(jnp.bfloat16).reshape(queries.shape[0], queries.shape[1], -1)


def per_device(
    tokens,
    time_gain,
    time_proj,
    time_out,
    time_scale,
    space_gain,
    space_proj,
    space_out,
    space_scale,
):
    frames, local_count = (tokens.shape[0], tokens.shape[1])
    peers = lax.axis_size("tm")
    model_width = HEADS * HEAD_DIM
    normed = layer_norm(tokens, time_gain)
    packed = project(normed, time_proj)
    outgoing = packed.reshape(frames, peers, local_count // peers, packed.shape[-1])
    attended = attend_time(
        lax.all_to_all(outgoing, "tm", split_axis=1, concat_axis=0, tiled=True)[:, 0], time_scale
    )[:, None]
    attended = lax.all_to_all(attended, "tm", split_axis=0, concat_axis=1, tiled=True)
    update = jnp.dot(
        attended.reshape(-1, model_width), time_out, preferred_element_type=jnp.float32
    )
    stream = (tokens.astype(jnp.float32) + update.reshape(tokens.shape)).astype(jnp.bfloat16)
    fields = project(layer_norm(stream, space_gain), space_proj)
    queries = fields[..., :model_width].reshape(frames, local_count, HEADS, HEAD_DIM)
    key_values = lax.all_gather(fields[..., model_width:], "patch", axis=1, tiled=True)
    all_patches = key_values.shape[1]
    shaped = key_values.reshape(frames, all_patches, 2, HEADS, HEAD_DIM)
    mixed_rows = attend_space(queries, shaped[:, :, 0], shaped[:, :, 1], space_scale)
    update = jnp.dot(
        mixed_rows.reshape(-1, model_width), space_out, preferred_element_type=jnp.float32
    )
    return (stream.astype(jnp.float32) + update.reshape(stream.shape)).astype(jnp.bfloat16)


def solution(mesh):
    in_specs = (P("tm", "patch", None), P(), P(), P(), P(), P(), P(), P(), P())
    out_specs = P("tm", "patch", None)
    return jax.shard_map(
        per_device, mesh=mesh, in_specs=in_specs, out_specs=out_specs, check_vma=False
    )
```

profile of v0, /device:TPU:0, one launch (start us, length us, event | category | flops | bytes accessed | tf_op | source)
XLA Modules:
  0.0 234.8 jit_solution(6751911498519850920)
XLA Ops:
  6.5 1.4 convert_reduce_fusion.1
  8.0 1.5 fusion.18
  9.5 5.8 %copy.32 = bf16[768,2304]{0,1:T(8,128)(2,1)} copy(bf16[768,2304]{1,0:T(8,128)(2,1)} %param.11) | data formatting | bytes 7077888 | tf_op args[2]
  15.6 4.1 %fusion.36 = f32[512,3,12,64]{0,3,2,1:T(8,128)S(1)} fusion(bf16[512,768,1,1]{1,0,3,2:T(8,128)(2,1)S(1)} %bitcast.106, bf16[3,12,64,768]{3,2,1,0:T(8,128)(2,1)} %bitcast.102), kind=kOutput, calls=%fused_computation.62 | convolution fusion | flops 1811939328 | bytes 9043968 | tf_op jit(solution)/shard_map/dot_general | solution.py:22
  19.8 0.5 multiply_reduce_fusion.2
  20.4 0.5 multiply_convert_fusion.1
  21.1 6.8 %copy.33 = bf16[512,3,12,64]{3,2,1,0:T(8,128)(2,1)} copy(bf16[512,3,12,64]{0,3,2,1:T(8,128)(2,1)S(1)} %pad_maximum_fusion) | data formatting | bytes 4718592 | tf_op jit(solution)/shard_map/concatenate | solution.py:26
  27.9 7.2 %convert_element_type.45 = bf16[8,8,8,2304]{3,2,1,0:T(8,128)(2,1)S(1)} reshape(bf16[512,3,12,64]{3,2,1,0:T(8,128)(2,1)} %copy.33) | data formatting | bytes 4718592 | tf_op jit(solution)/shard_map/convert_element_type | solution.py:27
  35.3 60.9 %all_to_all.30 = bf16[8,8,8,2304]{3,2,0,1:T(8,128)(2,1)S(1)} all-to-all(bf16[8,8,8,2304]{3,2,0,1:T(8,128)(2,1)S(1)} %copy.34), channel_id=1, replica_groups=mesh['tm'=8,'patch'=4] {'tm'}, dimensions={1} | all-to-all | bytes 4718592 | tf_op jit(solution)/shard_map/all_to_all | solution.py:86
  96.3 6.0 %reshape_squeeze.4 = bf16[64,8,3,12,64]{4,3,2,1,0:T(8,128)(2,1)} reshape(bf16[8,8,1,8,2304]{4,3,1,0,2:T(8,128)(2,1)S(1)} %bitcast.100) | data formatting | bytes 4718592 | tf_op jit(solution)/shard_map/reshape;squeeze | solution.py:42
  102.3 7.2 %fusion.35 = (bf16[64,8,1,12,64]{4,3,2,1,0:T(8,128)(2,1)S(1)}, bf16[64,8,1,12,64]{4,3,2,1,0:T(8,128)(2,1)}, bf16[64,8,1,12,64]{4,3,2,1,0:T(8,128)(2,1)}) fusion(bf16[64,8,3,12,64]{4,3,2,1,0:T(8,128)(2,1)} %reshape_squeeze.4), kind=kLoop, calls=%fused_computation.61 | loop fusion | bytes 4718592 | tf_op jit(solution)/shard_map/slice | solution.py:44
  109.4 3.0 %copy.55 = bf16[64,8,1,12,64]{0,4,3,1,2:T(8,128)(2,1)} copy(bf16[64,8,1,12,64]{4,3,2,1,0:T(8,128)(2,1)S(1)} %get-tuple-element.15) | data formatting | bytes 1572864
  112.4 4.7 %multiply_reduce_fusion.3 = (f32[8,12,64]{2,1,0:T(8,128)S(1)}, f32[8,12,64,64]{2,3,1,0:T(8,128)S(1)}) fusion(f32[12]{0:T(128)S(1)} %copy-done.13, bf16[64,8,1,12,64]{4,3,2,1,0:T(8,128)(2,1)} %get-tuple-element.16, bf16[64,8,1,12,64]{4,3,2,1,0:T(8,128)(2,1)} %get-tuple-element.17), kind=kOutput, calls=%fused_computation.19 | convolution fusion | flops 51111936 | bytes 3170352 | tf_op jit(solution)/shard_map/while/body/eval_jaxpr/qihd,kihd->ihqk/dot_general | solution.py:49
  117.2 1.0 fusion.9
  118.6 0.9 fusion.6
  119.5 1.6 copy.39
  121.0 3.6 %all-to-all-start.1 = ((bf16[64,1,8,768]{3,2,1,0:T(8,128)(2,1)}), bf16[64,1,8,768]{3,2,1,0:T(8,128)(2,1)S(1)}, u32[]{:S(2)}, u32[]{:S(2)}) async-start(bf16[64,1,8,768]{3,2,1,0:T(8,128)(2,1)} %copy.39), calls=%async_computation.1 | async-start | bytes 1572864 | tf_op jit(solution)/shard_map/all_to_all | solution.py:88
  124.9 5.8 %copy.41 = bf16[768,2304]{0,1:T(8,128)(2,1)} copy(bf16[768,2304]{1,0:T(8,128)(2,1)} %param.15) | data formatting | bytes 7077888 | tf_op args[6]
  130.6 13.9 %all-to-all-done.1 = bf16[64,1,8,768]{3,2,1,0:T(8,128)(2,1)S(1)} async-done(((bf16[64,1,8,768]{3,2,1,0:T(8,128)(2,1)}), bf16[64,1,8,768]{3,2,1,0:T(8,128)(2,1)S(1)}, u32[]{:S(2)}, u32[]{:S(2)}) %all-to-all-start.1) | async-done | bytes 786464 | tf_op jit(solution)/shard_map/all_to_all | solution.py:88
  144.5 0.9 convert_reduce_fusion
  146.3 0.5 copy-done.7
  146.8 2.0 fusion.37
  149.5 0.5 multiply_convert_fusion
  150.2 4.3 %convert_element_type.51 = bf16[8,64,2304]{1,0,2:T(8,128)(2,1)} reshape(bf16[512,3,12,64]{0,3,2,1:T(8,128)(2,1)S(1)} %pad_maximum_fusion.1) | data formatting | bytes 4718592 | tf_op jit(solution)/shard_map/convert_element_type | solution.py:27
  154.5 3.2 %slice.53 = bf16[8,64,1536]{1,0,2:T(8,128)(2,1)} slice(bf16[8,64,2304]{1,0,2:T(8,128)(2,1)} %convert_element_type.51), slice={[0:8], [0:64], [768:2304]} | slice | bytes 3145728 | tf_op jit(solution)/shard_map/slice | solution.py:95
  157.7 5.7 %copy.42 = bf16[8,64,1536]{2,0,1:T(8,128)(2,1)} copy(bf16[8,64,1536]{1,0,2:T(8,128)(2,1)} %slice.53) | data formatting | bytes 3145728 | tf_op jit(solution)/shard_map/slice | solution.py:95
  163.4 45.4 %all-gather.2.cloned.1.call-done = bf16[8,256,1536]{2,0,1:T(8,128)(2,1)} async-done(((bf16[8,64,1536]{2,0,1:T(8,128)(2,1)}), bf16[8,256,1536]{2,0,1:T(8,128)(2,1)}) %all-gather.2.cloned.1.call-update) | async-done | bytes 6291472 | tf_op jit(solution)/shard_map/all_gather | solution.py:95
  208.9 9.1 %copy.43 = bf16[8,256,1536]{1,2,0:T(8,128)(2,1)} copy(bf16[8,256,1536]{2,0,1:T(8,128)(2,1)} %all-gather.2.cloned.1.call-done) | data formatting | bytes 12582912 | tf_op jit(solution)/shard_map/all_gather | solution.py:95
  218.0 3.5 %multiply_reduce_fusion = (f32[8,12,64]{2,1,0:T(8,128)S(1)}, f32[8,12,64,256]{3,2,1,0:T(8,128)S(1)}) fusion(f32[12]{0:T(128)S(1)} %copy-done.12, bf16[8,256,2,12,64]{1,4,3,2,0:T(8,128)(2,1)} %bitcast.98, bf16[8,64,12,64]{1,0,3,2:T(8,128)(2,1)S(1)} %bitcast.97), kind=kOutput, calls=%fused_computation.1 | convolution fusion | flops 204466176 | bytes 10248240 | tf_op jit(solution)/shard_map/fqhd,fkhd->fhqk/dot_general | solution.py:61
  221.5 2.3 fusion
  224.3 1.8 fusion.5
  226.2 1.8 fusion.22
  (46 shorter events, 3.6 us)
Async XLA Ops:
  6.5 138.0 %copy-start = (bf16[768,768]{1,0:T(8,128)(2,1)S(1)}, bf16[768,768]{1,0:T(8,128)(2,1)}, u32[]{:S(2)}) copy-start(bf16[768,768]{1,0:T(8,128)(2,1)} %param.12) | copy-start | bytes 3538948
  9.5 5.8 %copy-start.3 = (bf16[8,64,768]{2,1,0:T(8,128)(2,1)S(1)}, bf16[8,64,768]{2,1,0:T(8,128)(2,1)}, u32[]{:S(2)}) copy-start(bf16[8,64,768]{2,1,0:T(8,128)(2,1)} %param.9) | copy-start | bytes 2359300
  9.5 5.8 %copy-start.10 = (f32[768]{0:T(1024)S(1)}, f32[768]{0:T(1024)}, u32[]{:S(2)}) copy-start(f32[768]{0:T(1024)} %param.10) | copy-start | bytes 9220
  109.4 3.0 %copy-start.13 = (f32[12]{0:T(128)S(1)}, f32[12]{0:T(128)}, u32[]{:S(2)}) copy-start(f32[12]{0:T(128)} %param.13) | copy-start | bytes 148
  117.1 1.4 copy-start.8
  121.0 23.5 %all-to-all-start.1 = ((bf16[64,1,8,768]{3,2,1,0:T(8,128)(2,1)}), bf16[64,1,8,768]{3,2,1,0:T(8,128)(2,1)S(1)}, u32[]{:S(2)}, u32[]{:S(2)}) async-start(bf16[64,1,8,768]{3,2,1,0:T(8,128)(2,1)} %copy.39), calls=%async_computation.1 | async-start | bytes 1572864 | tf_op jit(solution)/shard_map/all_to_all | solution.py:88
  124.6 19.9 %copy-start.4 = (bf16[8,64,768]{2,1,0:T(8,128)(2,1)S(1)}, bf16[8,64,768]{2,1,0:T(8,128)(2,1)}, u32[]{:S(2)}) copy-start(bf16[8,64,768]{2,1,0:T(8,128)(2,1)} %param.9) | copy-start | bytes 2359300
  124.6 84.2 %all-gather.2.cloned.1.call-start = ((), (), s32[]{:S(2)}) async-start(), calls=%async_computation.2 | async-start | bytes 7864320 | tf_op jit(solution)/shard_map/all_gather | solution.py:95
  144.5 1.3 copy-start.11
  144.5 2.3 copy-start.7
  145.4 0.9 copy-start.5
  163.4 54.6 %slice-start = ((bf16[8,64,2304]{1,0,2:T(8,128)(2,1)}), bf16[8,64,768]{1,0,2:T(8,128)(2,1)S(1)}, s32[]{:S(2)}) async-start(bf16[8,64,2304]{1,0,2:T(8,128)(2,1)} %convert_element_type.51), calls=%async_computation.3 | async-start | bytes 3145728 | tf_op jit(solution)/shard_map/slice | solution.py:94
  163.4 54.6 %copy-start.12 = (f32[12]{0:T(128)S(1)}, f32[12]{0:T(128)}, u32[]{:S(2)}) copy-start(f32[12]{0:T(128)} %param.17) | copy-start | bytes 148
  221.5 2.8 %copy-start.2 = (bf16[8,256,1536]{1,2,0:T(8,128)(2,1)S(1)}, bf16[8,256,1536]{1,2,0:T(8,128)(2,1)}, u32[]{:S(2)}) copy-start(bf16[8,256,1536]{1,2,0:T(8,128)(2,1)} %copy.43) | copy-start | bytes 18874372
  224.3 1.9 copy-start.6
  224.3 1.9 copy-start.9
  224.3 3.6 %copy-start.1 = (bf16[768,768]{1,0:T(8,128)(2,1)S(1)}, bf16[768,768]{1,0:T(8,128)(2,1)}, u32[]{:S(2)}) copy-start(bf16[768,768]{1,0:T(8,128)(2,1)} %param.12) | copy-start | bytes 3538948
Sparse Core Ops, SparseCore 0:
  163.5 45.2 all-gather.1
where the time goes:
time: 236 us; the launch traced here: 235 us
  local copies, waits for them, and re-layouts  67.7 us (29%)
  blocking collectives  60.9 us (26%)
  waiting for transfers between devices  59.3 us (25%)
  matrix products  19.7 us (8%)
  between operations  13.7 us (6%)
  other arithmetic  9.53 us (4%)
  starting transfers between devices  3.85 us (2%)
    all_to_all x1, blocking collectives, per_device(): lax.all_to_all(outgoing, 'tm', split_axis=1, concat_axis=0, tiled=True)  60.9 us
    all_gather x1, waiting for transfers between devices, per_device(): lax.all_gather(fields[..., model_width:], 'patch', axis=1, tiled=True)  45.4 us
    unnamed x31, local copies, waits for them, and re-layouts  16.2 us
    all_to_all x1, waiting for transfers between devices, per_device(): lax.all_to_all(attended, 'tm', split_axis=0, concat_axis=1, tiled=True)  13.9 us
    convert_element_type x3, local copies, waits for them, and re-layouts, project(): joined.reshape(normed.shape[:-1] + (3 * HEADS * HEAD_DIM,))  11.7 us
    all_gather x1, local copies, waits for them, and re-layouts, per_device(): lax.all_gather(fields[..., model_width:], 'patch', axis=1, tiled=True)  9.15 us
    slice x2, local copies, waits for them, and re-layouts, per_device(): fields[..., model_width:]  8.86 us
    slice x1, local copies, waits for them, and re-layouts, attend_time(): value_rows = pieces[:, :, 2]  7.19 us
  transfers between devices with their start and end apart: 2, of which 2 were waited for; matrix products, arithmetic and copies ran while one was open for 2% of the time, Pallas kernels for 0%

commit v1 on v0

v1 whole, which is shorter than its diff:
```python
import functools
import math

import jax
import jax.numpy as jnp
from jax import lax
from jax.experimental import pallas as pl
from jax.experimental.pallas import tpu as pltpu
from jax.sharding import PartitionSpec as P

HEADS = 12
HEAD_DIM = 64
WIDTH = HEADS * HEAD_DIM
EPSILON = 1e-06
LOG2_E = math.log2(math.e)
LANES = 128
GROUP = 256

NT = (((1,), (1,)), ((), ()))
TN = (((0,), (0,)), ((), ()))


def dot(left, right, dims=(((1,), (0,)), ((), ()))):
    return lax.dot_general(left, right, dims, preferred_element_type=jnp.float32)


def layer_norm(values, gain):
    centred = values - jnp.mean(values, axis=-1, keepdims=True)
    spread = jnp.mean(centred * centred, axis=-1, keepdims=True)
    return (centred * lax.rsqrt(spread + EPSILON) * gain).astype(jnp.bfloat16)


def unit_rows(fields):
    squares = jnp.sum(fields * fields, axis=0, keepdims=True)
    return (fields * lax.rsqrt(squares + EPSILON)).astype(jnp.bfloat16)


def hold(held, values):
    for part in range(held.shape[0]):
        held[part] = values[:, part * LANES : (part + 1) * LANES].astype(jnp.float32)


def pick(held, start, count, step):
    return jnp.concatenate(
        [held[part, pl.ds(start, count, stride=step), :] for part in range(held.shape[0])], axis=1
    )


def attend(keys, queries, values, factor, packed):
    scores = dot(keys, queries, TN)
    columns = scores.shape[1]
    if packed == 1:
        powers = jnp.exp2((scores - jnp.max(scores, axis=0, keepdims=True)) * factor)
        totals = jnp.sum(powers, axis=0, keepdims=True)
        weights = powers.astype(jnp.bfloat16)
    else:
        length = columns // packed
        owner = lax.broadcasted_iota(jnp.int32, (length, columns), 1) // length
        own = scores[:length]
        for item in range(1, packed):
            own = jnp.where(owner == item, scores[item * length : (item + 1) * length], own)
        powers = jnp.exp2((own - jnp.max(own, axis=0, keepdims=True)) * factor)
        totals = jnp.sum(powers, axis=0, keepdims=True)
        weights = jnp.concatenate(
            [jnp.where(owner == item, powers, 0.0).astype(jnp.bfloat16) for item in range(packed)], axis=0
        )
    return (dot(values, weights) * (1.0 / totals)).astype(jnp.bfloat16)


def attend_heads(normed, proj_ref, scale_ref, mixed_ref, span, packed):
    rows = normed.shape[0]
    for head in range(HEADS):
        low = head * HEAD_DIM
        queries = unit_rows(dot(proj_ref[low : low + HEAD_DIM], normed, NT))
        keys = unit_rows(dot(proj_ref[WIDTH + low : WIDTH + low + HEAD_DIM], normed, NT))
        values = dot(proj_ref[2 * WIDTH + low : 2 * WIDTH + low + HEAD_DIM], normed, NT).astype(jnp.bfloat16)
        factor = scale_ref[head] * LOG2_E
        for start in range(0, rows, span):
            cut = slice(start, start + span)
            mixed_ref[low : low + HEAD_DIM, cut] = attend(
                keys[:, cut], queries[:, cut], values[:, cut], factor, packed
            )


def time_kernel(frames, scale_ref, tokens_ref, gain_ref, proj_ref, out_ref, stream_ref, held, result, mixed):
    rows = tokens_ref.shape[0]
    patches = rows // frames
    together = max(1, min(patches, GROUP // frames))
    packed = max(1, min(together, LANES // frames))
    hold(held, tokens_ref)
    for first in range(0, patches, together):
        tokens = jnp.concatenate(
            [pick(held, first + item, frames, patches) for item in range(together)], axis=0
        )
        normed = layer_norm(tokens, gain_ref[...])
        attend_heads(normed, proj_ref, scale_ref, mixed, packed * frames, packed)
        stream = tokens + dot(mixed[...], out_ref[...], TN)
        for item in range(together):
            for part in range(result.shape[0]):
                result[part, pl.ds(first + item, frames, stride=patches), :] = stream[
                    item * frames : (item + 1) * frames, part * LANES : (part + 1) * LANES
                ]
    for part in range(result.shape[0]):
        stream_ref[:, part * LANES : (part + 1) * LANES] = result[part].astype(jnp.bfloat16)


def space_kernel(senders, sides, scale_ref, stream_ref, gain_ref, proj_ref, out_ref, block_ref, held, mixed):
    rows = stream_ref.shape[0]
    frames, all_patches = block_ref.shape[1], sides * block_ref.shape[2]
    piece = rows // senders // frames
    hold(held, stream_ref)
    for frame in range(frames):
        parts = []
        for side in range(sides):
            if piece % 8:
                start = (side * frames + frame) * piece
                parts.append(pick(held, start, senders // sides, sides * frames))
            else:
                for sender in range(side, senders, sides):
                    parts.append(pick(held, (sender * frames + frame) * piece, piece, 1))
        stream = jnp.concatenate(parts, axis=0)
        normed = layer_norm(stream, gain_ref[...])
        attend_heads(normed, proj_ref, scale_ref, mixed, all_patches, 1)
        block = (stream + dot(mixed[...], out_ref[...], TN)).astype(jnp.bfloat16)
        for side in range(sides):
            block_ref[side, frame] = block[side * (all_patches // sides) : (side + 1) * (all_patches // sides)]


def call(kernel, out_shape, scratch, scale, rows, gain, proj, out):
    whole = pl.BlockSpec(memory_space=pltpu.VMEM)
    return pl.pallas_call(
        kernel,
        out_shape=jax.ShapeDtypeStruct(out_shape, jnp.bfloat16),
        in_specs=[pl.BlockSpec(memory_space=pltpu.SMEM)] + [whole] * 4,
        out_specs=whole,
        scratch_shapes=scratch,
        compiler_params=pltpu.CompilerParams(vmem_limit_bytes=40 * 1024 * 1024),
        cost_estimate=pl.CostEstimate(flops=3 * 10**9, bytes_accessed=7 * 10**6, transcendentals=10**6),
    )(scale, rows, gain.reshape(1, -1), proj, out)


def per_device(
    tokens,
    time_gain,
    time_proj,
    time_out,
    time_scale,
    space_gain,
    space_proj,
    space_out,
    space_scale,
):
    frames, local_count, width = tokens.shape
    peers, sides = lax.axis_size("tm"), lax.axis_size("patch")
    rows = frames * local_count
    all_frames = frames * peers
    time_rows = max(GROUP, all_frames)
    outgoing = tokens.reshape(frames, peers, local_count // peers, width)
    outgoing = jnp.swapaxes(outgoing, 0, 1).reshape(peers, rows // peers, width)
    arrived = lax.all_to_all(outgoing, "tm", split_axis=0, concat_axis=0, tiled=True).reshape(rows, width)
    stream = call(
        functools.partial(time_kernel, all_frames),
        (rows, width),
        [
            pltpu.VMEM((width // LANES, rows, LANES), jnp.float32),
            pltpu.VMEM((width // LANES, rows, LANES), jnp.float32),
            pltpu.VMEM((width, time_rows), jnp.bfloat16),
        ],
        time_scale, arrived, time_gain, time_proj.T, time_out,
    )
    senders = peers * sides
    stream = lax.all_to_all(
        stream.reshape(senders, rows // senders, width), ("tm", "patch"), split_axis=0, concat_axis=0, tiled=True
    ).reshape(rows, width)
    block = call(
        functools.partial(space_kernel, senders, sides),
        (sides, frames // sides, local_count, width),
        [pltpu.VMEM((width // LANES, rows, LANES), jnp.float32), pltpu.VMEM((width, sides * local_count), jnp.bfloat16)],
        space_scale, stream, space_gain, space_proj.T, space_out,
    )
    block = lax.all_to_all(block, "patch", split_axis=0, concat_axis=0, tiled=True)
    return block.reshape(frames, local_count, width)


def solution(mesh):
    in_specs = (P("tm", "patch", None), P(), P(), P(), P(), P(), P(), P(), P())
    out_specs = P("tm", "patch", None)
    return jax.shard_map(
        per_device, mesh=mesh, in_specs=in_specs, out_specs=out_specs, check_vma=False
    )
```

time: 236 us -> 111 us (0.47)
  local copies, waits for them, and re-layouts: 67.7 us -> 19.4 us
  blocking collectives: 60.9 us -> 14.2 us
  Pallas kernels: 0 us -> 37.8 us
  waiting for transfers between devices: 59.3 us -> 28.2 us
  matrix products: 19.7 us -> 0 us
  between operations: 13.7 us -> 0.06 us
  other arithmetic: 9.53 us -> 0 us
  starting transfers between devices: 3.85 us -> 11 us
    all_to_all x1, blocking collectives: 60.9 us -> 14.2 us  [per_device(): lax.all_to_all(block, 'patch', split_axis=0, concat_axis=0, tiled=True)]
    all_gather x1 -> x0, waiting for transfers between devices: 45.4 us -> none  [per_device(): lax.all_gather(fields[..., model_width:], 'patch', axis=1, tiled=True)]
    pallas_call x0 -> x2, Pallas kernels: none -> 37.8 us  [call(): pl.pallas_call(kernel, out_shape=jax.ShapeDtypeStruct(out_shape, jnp.bflo...]
    dot_general x8 -> x0, matrix products: 19.7 us -> none  [the longest x2 6.17 us: project(): fields = jnp.dot(flat, weight, preferred_element_type=jnp.float32)]
    slice x7 -> x0, local copies, waits for them, and re-layouts: 16.3 us -> none  [the longest x2 8.86 us: per_device(): fields[..., model_width:]]
    all_to_all x1 -> x2, waiting for transfers between devices: 13.9 us -> 28.2 us  [the longest x1 14.5 us: per_device(): lax.all_to_all(stream.reshape(senders, rows // senders, width), ('tm', 'p...]
    convert_element_type x3 -> x0, local copies, waits for them, and re-layouts: 11.7 us -> none  [project(): joined.reshape(normed.shape[:-1] + (3 * HEADS * HEAD_DIM,))]
    all_gather x1 -> x0, local copies, waits for them, and re-layouts: 9.15 us -> none  [per_device(): lax.all_gather(fields[..., model_width:], 'patch', axis=1, tiled=True)]
  transfers between devices with their start and end apart: 2 -> 2, of which waited for: 2 -> 2; matrix products, arithmetic and copies ran while one was open for 2% -> 11% of each run, Pallas kernels for 0% -> 0%
where the time goes in v1:
time: 111 us
  Pallas kernels  37.8 us (34%)
  waiting for transfers between devices  28.2 us (25%)
  local copies, waits for them, and re-layouts  19.4 us (17%)
  blocking collectives  14.2 us (13%)
  starting transfers between devices  11 us (10%)
    pallas_call x2, Pallas kernels, call(): pl.pallas_call(kernel, out_shape=jax.ShapeDtypeStruct(out_shape, jnp.bflo...  37.8 us
    unnamed x19, local copies, waits for them, and re-layouts  17.7 us
    all_to_all x1, waiting for transfers between devices, per_device(): lax.all_to_all(stream.reshape(senders, rows // senders, width), ('tm', 'p...  14.5 us
    all_to_all x1, blocking collectives, per_device(): lax.all_to_all(block, 'patch', split_axis=0, concat_axis=0, tiled=True)  14.2 us
    all_to_all x1, waiting for transfers between devices, per_device(): lax.all_to_all(outgoing, 'tm', split_axis=0, concat_axis=0, tiled=True)  13.6 us
    all_to_all x1, starting transfers between devices, per_device(): lax.all_to_all(outgoing, 'tm', split_axis=0, concat_axis=0, tiled=True)  7.28 us
    all_to_all x1, starting transfers between devices, per_device(): lax.all_to_all(stream.reshape(senders, rows // senders, width), ('tm', 'p...  3.76 us
  transfers between devices with their start and end apart: 2, of which 2 were waited for; matrix products, arithmetic and copies ran while one was open for 11% of the time, Pallas kernels for 0%

profile of v1, /device:TPU:0, one launch (start us, length us, event | category | flops | bytes accessed | tf_op | source)
XLA Modules:
  0.0 110.6 jit_solution(11908784674397562686)
XLA Ops:
  0.0 0.0 copy-start
  0.0 1.1 %copy-done = bf16[8,64,768]{2,1,0:T(8,128)(2,1)S(1)} copy-done((bf16[8,64,768]{2,1,0:T(8,128)(2,1)S(1)}, bf16[8,64,768]{2,1,0:T(8,128)(2,1)}, u32[]{:S(2)}) %copy-start) | copy-done | bytes 786456
  1.1 0.9 copy_bitcast_fusion
  2.1 7.3 %all-to-all-start = ((bf16[8,64,768]{2,1,0:T(8,128)(2,1)}), bf16[8,64,768]{2,1,0:T(8,128)(2,1)S(1)}, u32[]{:S(2)}, u32[]{:S(2)}) async-start(bf16[8,64,768]{2,1,0:T(8,128)(2,1)} %copy_bitcast_fusion), calls=%async_computation | async-start | bytes 1572864 | tf_op jit(solution)/shard_map/all_to_all | solution.py:160
  9.4 0.7 reshape.27.gain_ref
  10.0 0.0 copy-start.3
  10.0 0.0 copy-start.5
  10.0 5.9 %copy.11 = bf16[768,2304]{0,1:T(8,128)(2,1)} copy(bf16[768,2304]{1,0:T(8,128)(2,1)} %param.11) | data formatting | bytes 7077888 | tf_op args[2]
  15.9 13.6 %all-to-all-done = bf16[8,64,768]{2,1,0:T(8,128)(2,1)S(1)} async-done(((bf16[8,64,768]{2,1,0:T(8,128)(2,1)}), bf16[8,64,768]{2,1,0:T(8,128)(2,1)S(1)}, u32[]{:S(2)}, u32[]{:S(2)}) %all-to-all-start) | async-done | bytes 786464 | tf_op jit(solution)/shard_map/all_to_all | solution.py:160
  29.5 0.0 copy-done.3
  29.5 0.0 copy-done.5
  29.5 0.0 copy-start.1
  29.5 2.0 %copy-done.1 = bf16[768,2304]{0,1:T(8,128)(2,1)S(1)} copy-done((bf16[768,2304]{0,1:T(8,128)(2,1)S(1)}, bf16[768,2304]{0,1:T(8,128)(2,1)}, u32[]{:S(2)}) %copy-start.1) | copy-done | bytes 3538968
  31.5 0.0 copy-start.7
  31.5 20.6 %shard_map.91 = bf16[512,768]{1,0:T(8,128)(2,1)} custom-call(f32[12]{0:T(128)S(1)} %copy-done.5, bf16[512,768]{1,0:T(8,128)(2,1)S(1)} %bitcast.15, f32[1,768]{1,0:T(1,128)S(1)} %reshape.27.gain_ref, bf16[2304,768]{1,0:T(8,128)(2,1)S(1)} %bitcast.13, bf16[768,768]{1,0:T(8,128)(2,1)S(1)} %copy-done.3), custom_call_target="tpu_custom_call" | custom-call | flops 3000000000 | bytes 7000000 | tf_op jit(solution)/shard_map/pallas_call | solution.py:131
  52.1 3.8 %all-to-all-start.1 = ((bf16[32,16,768]{2,1,0:T(8,128)(2,1)}), bf16[32,16,768]{2,1,0:T(8,128)(2,1)S(1)}, u32[]{:S(2)}, u32[]{:S(2)}) async-start(bf16[32,16,768]{2,1,0:T(8,128)(2,1)} %bitcast.5), calls=%async_computation.1 | async-start | bytes 1572864 | tf_op jit(solution)/shard_map/all_to_all | solution.py:172
  55.9 0.0 copy-done.7
  55.9 0.0 copy-start.4
  55.9 0.0 copy-start.6
  56.0 5.9 %copy.12 = bf16[768,2304]{0,1:T(8,128)(2,1)} copy(bf16[768,2304]{1,0:T(8,128)(2,1)} %param.15) | data formatting | bytes 7077888 | tf_op args[6]
  61.8 14.5 %all-to-all-done.1 = bf16[32,16,768]{2,1,0:T(8,128)(2,1)S(1)} async-done(((bf16[32,16,768]{2,1,0:T(8,128)(2,1)}), bf16[32,16,768]{2,1,0:T(8,128)(2,1)S(1)}, u32[]{:S(2)}, u32[]{:S(2)}) %all-to-all-start.1) | async-done | bytes 786464 | tf_op jit(solution)/shard_map/all_to_all | solution.py:172
  76.3 0.0 copy-done.4
  76.3 0.0 copy-done.6
  76.3 0.0 copy-start.2
  76.4 2.0 %copy-done.2 = bf16[768,2304]{0,1:T(8,128)(2,1)S(1)} copy-done((bf16[768,2304]{0,1:T(8,128)(2,1)S(1)}, bf16[768,2304]{0,1:T(8,128)(2,1)}, u32[]{:S(2)}) %copy-start.2) | copy-done | bytes 3538968
  78.4 17.2 %shard_map.92 = bf16[4,2,64,768]{3,2,1,0:T(8,128)(2,1)S(1)} custom-call(f32[12]{0:T(128)S(1)} %copy-done.6, bf16[512,768]{1,0:T(8,128)(2,1)S(1)} %bitcast.16, f32[1,768]{1,0:T(1,128)S(1)} %reshape.30.gain_ref, bf16[2304,768]{1,0:T(8,128)(2,1)S(1)} %bitcast.14, bf16[768,768]{1,0:T(8,128)(2,1)S(1)} %copy-done.4), custom_call_target="tpu_custom_call" | custom-call | flops 3000000000 | bytes 7000000 | tf_op jit(solution)/shard_map/pallas_call | solution.py:131
  95.5 14.2 %all_to_all.15 = bf16[4,2,64,768]{3,2,1,0:T(8,128)(2,1)S(1)} all-to-all(bf16[4,2,64,768]{3,2,1,0:T(8,128)(2,1)S(1)} %shard_map.92), channel_id=1, replica_groups=mesh['tm'=8,'patch'=4] {'patch'}, dimensions={0} | all-to-all | bytes 1572864 | tf_op jit(solution)/shard_map/all_to_all | solution.py:181
  109.7 0.9 copy.15
  (1 shorter events, 0.0 us)
Async XLA Ops:
  0.0 1.1 %copy-start = (bf16[8,64,768]{2,1,0:T(8,128)(2,1)S(1)}, bf16[8,64,768]{2,1,0:T(8,128)(2,1)}, u32[]{:S(2)}) copy-start(bf16[8,64,768]{2,1,0:T(8,128)(2,1)} %param.9) | copy-start | bytes 2359300
  2.1 27.5 %all-to-all-start = ((bf16[8,64,768]{2,1,0:T(8,128)(2,1)}), bf16[8,64,768]{2,1,0:T(8,128)(2,1)S(1)}, u32[]{:S(2)}, u32[]{:S(2)}) async-start(bf16[8,64,768]{2,1,0:T(8,128)(2,1)} %copy_bitcast_fusion), calls=%async_computation | async-start | bytes 1572864 | tf_op jit(solution)/shard_map/all_to_all | solution.py:160
  10.0 19.5 %copy-start.3 = (bf16[768,768]{1,0:T(8,128)(2,1)S(1)}, bf16[768,768]{1,0:T(8,128)(2,1)}, u32[]{:S(2)}) copy-start(bf16[768,768]{1,0:T(8,128)(2,1)} %out_ref.2) | copy-start | bytes 3538948
  10.0 19.5 %copy-start.5 = (f32[12]{0:T(128)S(1)}, f32[12]{0:T(128)}, u32[]{:S(2)}) copy-start(f32[12]{0:T(128)} %scale_ref.2) | copy-start | bytes 148
  29.5 2.0 %copy-start.1 = (bf16[768,2304]{0,1:T(8,128)(2,1)S(1)}, bf16[768,2304]{0,1:T(8,128)(2,1)}, u32[]{:S(2)}) copy-start(bf16[768,2304]{0,1:T(8,128)(2,1)} %copy.11) | copy-start | bytes 10616836
  31.5 24.4 %copy-start.7 = (f32[768]{0:T(1024)S(1)}, f32[768]{0:T(1024)}, u32[]{:S(2)}) copy-start(f32[768]{0:T(1024)} %param.14) | copy-start | bytes 9220
  52.1 24.2 %all-to-all-start.1 = ((bf16[32,16,768]{2,1,0:T(8,128)(2,1)}), bf16[32,16,768]{2,1,0:T(8,128)(2,1)S(1)}, u32[]{:S(2)}, u32[]{:S(2)}) async-start(bf16[32,16,768]{2,1,0:T(8,128)(2,1)} %bitcast.5), calls=%async_computation.1 | async-start | bytes 1572864 | tf_op jit(solution)/shard_map/all_to_all | solution.py:172
  55.9 20.4 %copy-start.4 = (bf16[768,768]{1,0:T(8,128)(2,1)S(1)}, bf16[768,768]{1,0:T(8,128)(2,1)}, u32[]{:S(2)}) copy-start(bf16[768,768]{1,0:T(8,128)(2,1)} %out_ref.3) | copy-start | bytes 3538948
  55.9 20.4 %copy-start.6 = (f32[12]{0:T(128)S(1)}, f32[12]{0:T(128)}, u32[]{:S(2)}) copy-start(f32[12]{0:T(128)} %scale_ref.3) | copy-start | bytes 148
  76.3 2.0 %copy-start.2 = (bf16[768,2304]{0,1:T(8,128)(2,1)S(1)}, bf16[768,2304]{0,1:T(8,128)(2,1)}, u32[]{:S(2)}) copy-start(bf16[768,2304]{0,1:T(8,128)(2,1)} %copy.12) | copy-start | bytes 10616836

commit v2 on v1

v2 whole, which is shorter than its diff:
```python
import functools
import math

import jax
import jax.numpy as jnp
from jax import lax
from jax.experimental import pallas as pl
from jax.experimental.pallas import tpu as pltpu
from jax.sharding import PartitionSpec as P

HEADS = 12
HEAD_DIM = 64
WIDTH = HEADS * HEAD_DIM
EPSILON = 1e-06
LOG2_E = math.log2(math.e)
LANES = 128

TN = (((0,), (0,)), ((), ()))
TT = (((0,), (1,)), ((), ()))


def dot(left, right, dims=(((1,), (0,)), ((), ()))):
    return lax.dot_general(left, right, dims, preferred_element_type=jnp.float32)


def layer_norm(values, gain):
    centred = values - jnp.mean(values, axis=-1, keepdims=True)
    spread = jnp.mean(centred * centred, axis=-1, keepdims=True)
    return (centred * lax.rsqrt(spread + EPSILON) * gain).astype(jnp.bfloat16)


def unit_columns(fields):
    heads = fields.reshape(HEADS, HEAD_DIM, fields.shape[1])
    squares = jnp.sum(heads * heads, axis=1, keepdims=True)
    return (heads * lax.rsqrt(squares + EPSILON)).reshape(fields.shape)


def project(normed, proj_ref, fields_ref):
    for part in range(3):
        cut = slice(part * WIDTH, (part + 1) * WIDTH)
        fields = dot(proj_ref[:, cut], normed, TT)
        if part < 2:
            fields = unit_columns(fields)
        fields_ref[cut] = fields.astype(jnp.bfloat16)


def hold(held, values):
    for part in range(held.shape[0]):
        held[part] = values[:, part * LANES : (part + 1) * LANES].astype(jnp.float32)


def pick(held, start, count, step):
    return jnp.concatenate(
        [held[part, pl.ds(start, count, stride=step), :] for part in range(held.shape[0])], axis=1
    )


def head_rows(part, head):
    return slice(part * WIDTH + head * HEAD_DIM, part * WIDTH + (head + 1) * HEAD_DIM)


def attend(fields_ref, scale_ref, mixed_ref, scores_ref, weights_ref, totals_ref, span, packed):
    length = span // packed
    owner = lax.broadcasted_iota(jnp.int32, (length, span), 1) // length
    for start in range(0, fields_ref.shape[1], span):
        cut = slice(start, start + span)
        for head in range(HEADS):
            scores_ref[head] = dot(fields_ref[head_rows(1, head), cut], fields_ref[head_rows(0, head), cut], TN)
        for head in range(HEADS):
            factor = scale_ref[head] * LOG2_E
            for low in range(0, span, LANES):
                lanes = slice(low, low + LANES)
                mine = owner[:, lanes]
                items = range(low // length, (low + LANES - 1) // length + 1) if packed > 1 else range(1)
                scores = scores_ref[head, items[0] * length : (items[0] + 1) * length, lanes]
                for item in items[1:]:
                    scores = jnp.where(mine == item, scores_ref[head, item * length : (item + 1) * length, lanes], scores)
                powers = jnp.exp2((scores - jnp.max(scores, axis=0, keepdims=True)) * factor)
                totals_ref[head, :, lanes] = 1.0 / jnp.sum(powers, axis=0, keepdims=True)
                for item in range(packed):
                    part = powers if packed == 1 else jnp.where(mine == item, powers, 0.0)
                    weights_ref[head, item * length : (item + 1) * length, lanes] = part.astype(jnp.bfloat16)
        for head in range(HEADS):
            mixed = dot(fields_ref[head_rows(2, head), cut], weights_ref[head]) * totals_ref[head]
            mixed_ref[head_rows(0, head), cut] = mixed.astype(jnp.bfloat16)


def time_kernel(
    frames, scale_ref, tokens_ref, gain_ref, proj_ref, out_ref, stream_ref, held, result, fields, mixed, *work
):
    patches = tokens_ref.shape[0] // frames
    span, packed = time_span(frames, patches)
    hold(held, tokens_ref)
    tokens = jnp.concatenate([pick(held, patch, frames, patches) for patch in range(patches)], axis=0)
    project(layer_norm(tokens, gain_ref[...]), proj_ref, fields)
    attend(fields, scale_ref, mixed, *work, span, packed)
    update = dot(mixed[...], out_ref[...], TN)
    for patch in range(patches):
        stream = pick(held, patch, frames, patches) + update[patch * frames : (patch + 1) * frames]
        for part in range(result.shape[0]):
            result[part, pl.ds(patch, frames, stride=patches), :] = stream[:, part * LANES : (part + 1) * LANES]
    for part in range(result.shape[0]):
        stream_ref[:, part * LANES : (part + 1) * LANES] = result[part].astype(jnp.bfloat16)


def space_kernel(
    senders, sides, scale_ref, stream_ref, gain_ref, proj_ref, out_ref, block_ref, held, fields, mixed, *work
):
    frames, side_patches = block_ref.shape[1:3]
    piece = stream_ref.shape[0] // senders // frames
    hold(held, stream_ref)

    def ordered():
        parts = []
        for frame in range(frames):
            for side in range(sides):
                if piece % 8:
                    start = (side * frames + frame) * piece
                    parts.append(pick(held, start, senders // sides, sides * frames))
                else:
                    for sender in range(side, senders, sides):
                        parts.append(pick(held, (sender * frames + frame) * piece, piece, 1))
        return jnp.concatenate(parts, axis=0)

    project(layer_norm(ordered(), gain_ref[...]), proj_ref, fields)
    attend(fields, scale_ref, mixed, *work, sides * side_patches, 1)
    block = (ordered() + dot(mixed[...], out_ref[...], TN)).astype(jnp.bfloat16)
    for frame in range(frames):
        for side in range(sides):
            start = (frame * sides + side) * side_patches
            block_ref[side, frame] = block[start : start + side_patches]


def time_span(frames, patches):
    packed = max(1, min(patches, LANES // frames))
    return packed * frames, packed


def work_space(rows, span):
    return [
        pltpu.VMEM((3 * WIDTH, rows), jnp.bfloat16),
        pltpu.VMEM((WIDTH, rows), jnp.bfloat16),
        pltpu.VMEM((HEADS, span, span), jnp.float32),
        pltpu.VMEM((HEADS, span, span), jnp.bfloat16),
        pltpu.VMEM((HEADS, 1, span), jnp.float32),
    ]


def call(kernel, out_shape, scratch, scale, rows, gain, proj, out):
    whole = pl.BlockSpec(memory_space=pltpu.VMEM)
    return pl.pallas_call(
        kernel,
        out_shape=jax.ShapeDtypeStruct(out_shape, jnp.bfloat16),
        in_specs=[pl.BlockSpec(memory_space=pltpu.SMEM)] + [whole] * 4,
        out_specs=whole,
        scratch_shapes=scratch,
        compiler_params=pltpu.CompilerParams(vmem_limit_bytes=40 * 1024 * 1024),
        cost_estimate=pl.CostEstimate(flops=3 * 10**9, bytes_accessed=7 * 10**6, transcendentals=10**6),
    )(scale, rows, gain.reshape(1, -1), proj, out)


def per_device(
    tokens,
    time_gain,
    time_proj,
    time_out,
    time_scale,
    space_gain,
    space_proj,
    space_out,
    space_scale,
):
    frames, local_count, width = tokens.shape
    peers, sides = lax.axis_size("tm"), lax.axis_size("patch")
    rows = frames * local_count
    all_frames = frames * peers
    outgoing = tokens.reshape(frames, peers, local_count // peers, width)
    outgoing = jnp.swapaxes(outgoing, 0, 1).reshape(peers, rows // peers, width)
    arrived = lax.all_to_all(outgoing, "tm", split_axis=0, concat_axis=0, tiled=True).reshape(rows, width)
    held = pltpu.VMEM((width // LANES, rows, LANES), jnp.float32)
    stream = call(
        functools.partial(time_kernel, all_frames),
        (rows, width),
        [held, held] + work_space(rows, time_span(all_frames, local_count // peers)[0]),
        time_scale, arrived, time_gain, time_proj, time_out,
    )
    senders = peers * sides
    stream = lax.all_to_all(
        stream.reshape(senders, rows // senders, width), ("tm", "patch"), split_axis=0, concat_axis=0, tiled=True
    ).reshape(rows, width)
    block = call(
        functools.partial(space_kernel, senders, sides),
        (sides, frames // sides, local_count, width),
        [held] + work_space(rows, sides * local_count),
        space_scale, stream, space_gain, space_proj, space_out,
    )
    block = lax.all_to_all(block, "patch", split_axis=0, concat_axis=0, tiled=True)
    return block.reshape(frames, local_count, width)


def solution(mesh):
    in_specs = (P("tm", "patch", None), P(), P(), P(), P(), P(), P(), P(), P())
    out_specs = P("tm", "patch", None)
    return jax.shard_map(
        per_device, mesh=mesh, in_specs=in_specs, out_specs=out_specs, check_vma=False
    )
```

time: 111 us -> 87.9 us (0.79)
  Pallas kernels: 37.8 us -> 12.6 us
  waiting for transfers between devices: 28.2 us -> 40.1 us
  local copies, waits for them, and re-layouts: 19.4 us -> 9.58 us
    pallas_call x2, Pallas kernels: 37.8 us -> 12.6 us  [call(): pl.pallas_call(kernel, out_shape=jax.ShapeDtypeStruct(out_shape, jnp.bflo...]
    unnamed x19 -> x17, local copies, waits for them, and re-layouts: 17.7 us -> 7.95 us
    all_to_all x1, waiting for transfers between devices: 14.5 us -> 20.6 us  [per_device(): lax.all_to_all(stream.reshape(senders, rows // senders, width), ('tm', 'p...]
    all_to_all x1, waiting for transfers between devices: 13.6 us -> 19.5 us  [per_device(): lax.all_to_all(outgoing, 'tm', split_axis=0, concat_axis=0, tiled=True)]
  transfers between devices with their start and end apart: 2 -> 2, of which waited for: 2 -> 2; matrix products, arithmetic and copies ran while one was open for 11% -> 1% of each run, Pallas kernels for 0% -> 0%
where the time goes in v2:
time: 87.9 us; the launch traced here: 87.4 us
  waiting for transfers between devices  40.1 us (46%)
  blocking collectives  14.2 us (16%)
  Pallas kernels  12.6 us (14%)
  starting transfers between devices  10.9 us (12%)
  local copies, waits for them, and re-layouts  9.58 us (11%)
    all_to_all x1, waiting for transfers between devices, per_device(): lax.all_to_all(stream.reshape(senders, rows // senders, width), ('tm', 'p...  20.6 us
    all_to_all x1, waiting for transfers between devices, per_device(): lax.all_to_all(outgoing, 'tm', split_axis=0, concat_axis=0, tiled=True)  19.5 us
    all_to_all x1, blocking collectives, per_device(): lax.all_to_all(block, 'patch', split_axis=0, concat_axis=0, tiled=True)  14.2 us
    pallas_call x2, Pallas kernels, call(): pl.pallas_call(kernel, out_shape=jax.ShapeDtypeStruct(out_shape, jnp.bflo...  12.6 us
    unnamed x17, local copies, waits for them, and re-layouts  7.95 us
    all_to_all x1, starting transfers between devices, per_device(): lax.all_to_all(outgoing, 'tm', split_axis=0, concat_axis=0, tiled=True)  7.28 us
    all_to_all x1, starting transfers between devices, per_device(): lax.all_to_all(stream.reshape(senders, rows // senders, width), ('tm', 'p...  3.57 us
  transfers between devices with their start and end apart: 2, of which 2 were waited for; matrix products, arithmetic and copies ran while one was open for 1% of the time, Pallas kernels for 0%

profile of v2, /device:TPU:0, one launch (start us, length us, event | category | flops | bytes accessed | tf_op | source)
XLA Modules:
  0.0 87.4 jit_solution(11725620530534547139)
XLA Ops:
  0.0 0.0 copy-start
  0.0 1.1 %copy-done = bf16[8,64,768]{2,1,0:T(8,128)(2,1)S(1)} copy-done((bf16[8,64,768]{2,1,0:T(8,128)(2,1)S(1)}, bf16[8,64,768]{2,1,0:T(8,128)(2,1)}, u32[]{:S(2)}) %copy-start) | copy-done | bytes 786456
  1.1 0.9 %copy_bitcast_fusion = bf16[8,64,768]{2,1,0:T(8,128)(2,1)} fusion(bf16[8,64,768]{2,1,0:T(8,128)(2,1)S(1)} %copy-done), kind=kLoop, calls=%fused_computation | loop fusion | bytes 1572864 | tf_op jit(solution)/shard_map/reshape | solution.py:178
  2.1 7.3 %all-to-all-start = ((bf16[8,64,768]{2,1,0:T(8,128)(2,1)}), bf16[8,64,768]{2,1,0:T(8,128)(2,1)S(1)}, u32[]{:S(2)}, u32[]{:S(2)}) async-start(bf16[8,64,768]{2,1,0:T(8,128)(2,1)} %copy_bitcast_fusion), calls=%async_computation | async-start | bytes 1572864 | tf_op jit(solution)/shard_map/all_to_all | solution.py:179
  9.4 0.7 reshape.27.gain_ref
  10.0 19.5 %all-to-all-done = bf16[8,64,768]{2,1,0:T(8,128)(2,1)S(1)} async-done(((bf16[8,64,768]{2,1,0:T(8,128)(2,1)}), bf16[8,64,768]{2,1,0:T(8,128)(2,1)S(1)}, u32[]{:S(2)}, u32[]{:S(2)}) %all-to-all-start) | async-done | bytes 786464 | tf_op jit(solution)/shard_map/all_to_all | solution.py:179
  29.5 0.0 copy-start.1
  29.5 2.0 %copy-done.1 = bf16[768,2304]{1,0:T(8,128)(2,1)S(1)} copy-done((bf16[768,2304]{1,0:T(8,128)(2,1)S(1)}, bf16[768,2304]{1,0:T(8,128)(2,1)}, u32[]{:S(2)}) %copy-start.1) | copy-done | bytes 3538968
  31.5 0.0 copy-start.3
  31.5 1.3 %copy-done.3 = bf16[768,768]{1,0:T(8,128)(2,1)S(1)} copy-done((bf16[768,768]{1,0:T(8,128)(2,1)S(1)}, bf16[768,768]{1,0:T(8,128)(2,1)}, u32[]{:S(2)}) %copy-start.3) | copy-done | bytes 1179672
  32.8 0.0 copy-start.5
  32.8 0.7 copy-done.5
  33.5 0.0 copy-start.7
  33.5 0.0 copy-start.4
  33.5 0.0 copy-start.6
  33.5 6.7 %shard_map.91 = bf16[512,768]{1,0:T(8,128)(2,1)} custom-call(f32[12]{0:T(128)S(1)} %copy-done.5, bf16[512,768]{1,0:T(8,128)(2,1)S(1)} %bitcast.11, f32[1,768]{1,0:T(1,128)S(1)} %reshape.27.gain_ref, bf16[768,2304]{1,0:T(8,128)(2,1)S(1)} %copy-done.1, bf16[768,768]{1,0:T(8,128)(2,1)S(1)} %copy-done.3), custom_call_target="tpu_custom_call" | custom-call | flops 3000000000 | bytes 7000000 | tf_op jit(solution)/shard_map/pallas_call | solution.py:151
  40.2 3.6 %all-to-all-start.1 = ((bf16[32,16,768]{2,1,0:T(8,128)(2,1)}), bf16[32,16,768]{2,1,0:T(8,128)(2,1)S(1)}, u32[]{:S(2)}, u32[]{:S(2)}) async-start(bf16[32,16,768]{2,1,0:T(8,128)(2,1)} %bitcast.4), calls=%async_computation.1 | async-start | bytes 1572864 | tf_op jit(solution)/shard_map/all_to_all | solution.py:188
  43.8 0.0 copy-done.7
  43.8 20.6 %all-to-all-done.1 = bf16[32,16,768]{2,1,0:T(8,128)(2,1)S(1)} async-done(((bf16[32,16,768]{2,1,0:T(8,128)(2,1)}), bf16[32,16,768]{2,1,0:T(8,128)(2,1)S(1)}, u32[]{:S(2)}, u32[]{:S(2)}) %all-to-all-start.1) | async-done | bytes 786464 | tf_op jit(solution)/shard_map/all_to_all | solution.py:188
  64.4 0.0 copy-done.4
  64.4 0.0 copy-done.6
  64.4 0.0 copy-start.2
  64.4 2.0 %copy-done.2 = bf16[768,2304]{1,0:T(8,128)(2,1)S(1)} copy-done((bf16[768,2304]{1,0:T(8,128)(2,1)S(1)}, bf16[768,2304]{1,0:T(8,128)(2,1)}, u32[]{:S(2)}) %copy-start.2) | copy-done | bytes 3538968
  66.4 5.9 %shard_map.92 = bf16[4,2,64,768]{3,2,1,0:T(8,128)(2,1)S(1)} custom-call(f32[12]{0:T(128)S(1)} %copy-done.6, bf16[512,768]{1,0:T(8,128)(2,1)S(1)} %bitcast.12, f32[1,768]{1,0:T(1,128)S(1)} %reshape.30.gain_ref, bf16[768,2304]{1,0:T(8,128)(2,1)S(1)} %copy-done.2, bf16[768,768]{1,0:T(8,128)(2,1)S(1)} %copy-done.4), custom_call_target="tpu_custom_call" | custom-call | flops 3000000000 | bytes 7000000 | tf_op jit(solution)/shard_map/pallas_call | solution.py:151
  72.3 14.2 %all_to_all.15 = bf16[4,2,64,768]{3,2,1,0:T(8,128)(2,1)S(1)} all-to-all(bf16[4,2,64,768]{3,2,1,0:T(8,128)(2,1)S(1)} %shard_map.92), channel_id=1, replica_groups=mesh['tm'=8,'patch'=4] {'patch'}, dimensions={0} | all-to-all | bytes 1572864 | tf_op jit(solution)/shard_map/all_to_all | solution.py:197
  86.5 0.9 %copy.13 = bf16[8,64,768]{2,1,0:T(8,128)(2,1)} copy(bf16[8,64,768]{2,1,0:T(8,128)(2,1)S(1)} %bitcast.13) | data formatting | bytes 1572864
  (1 shorter events, 0.0 us)
Async XLA Ops:
  0.0 1.1 %copy-start = (bf16[8,64,768]{2,1,0:T(8,128)(2,1)S(1)}, bf16[8,64,768]{2,1,0:T(8,128)(2,1)}, u32[]{:S(2)}) copy-start(bf16[8,64,768]{2,1,0:T(8,128)(2,1)} %param.9) | copy-start | bytes 2359300
  2.1 27.5 %all-to-all-start = ((bf16[8,64,768]{2,1,0:T(8,128)(2,1)}), bf16[8,64,768]{2,1,0:T(8,128)(2,1)S(1)}, u32[]{:S(2)}, u32[]{:S(2)}) async-start(bf16[8,64,768]{2,1,0:T(8,128)(2,1)} %copy_bitcast_fusion), calls=%async_computation | async-start | bytes 1572864 | tf_op jit(solution)/shard_map/all_to_all | solution.py:179
  29.5 2.0 %copy-start.1 = (bf16[768,2304]{1,0:T(8,128)(2,1)S(1)}, bf16[768,2304]{1,0:T(8,128)(2,1)}, u32[]{:S(2)}) copy-start(bf16[768,2304]{1,0:T(8,128)(2,1)} %proj_ref.2) | copy-start | bytes 10616836
  31.5 1.3 %copy-start.3 = (bf16[768,768]{1,0:T(8,128)(2,1)S(1)}, bf16[768,768]{1,0:T(8,128)(2,1)}, u32[]{:S(2)}) copy-start(bf16[768,768]{1,0:T(8,128)(2,1)} %out_ref.2) | copy-start | bytes 3538948
  32.8 0.7 copy-start.5
  33.5 10.3 %copy-start.7 = (f32[768]{0:T(1024)S(1)}, f32[768]{0:T(1024)}, u32[]{:S(2)}) copy-start(f32[768]{0:T(1024)} %param.14) | copy-start | bytes 9220
  33.5 31.0 %copy-start.4 = (bf16[768,768]{1,0:T(8,128)(2,1)S(1)}, bf16[768,768]{1,0:T(8,128)(2,1)}, u32[]{:S(2)}) copy-start(bf16[768,768]{1,0:T(8,128)(2,1)} %out_ref.3) | copy-start | bytes 3538948
  33.5 31.0 %copy-start.6 = (f32[12]{0:T(128)S(1)}, f32[12]{0:T(128)}, u32[]{:S(2)}) copy-start(f32[12]{0:T(128)} %scale_ref.3) | copy-start | bytes 148
  40.2 24.2 %all-to-all-start.1 = ((bf16[32,16,768]{2,1,0:T(8,128)(2,1)}), bf16[32,16,768]{2,1,0:T(8,128)(2,1)S(1)}, u32[]{:S(2)}, u32[]{:S(2)}) async-start(bf16[32,16,768]{2,1,0:T(8,128)(2,1)} %bitcast.4), calls=%async_computation.1 | async-start | bytes 1572864 | tf_op jit(solution)/shard_map/all_to_all | solution.py:188
  64.4 2.0 %copy-start.2 = (bf16[768,2304]{1,0:T(8,128)(2,1)S(1)}, bf16[768,2304]{1,0:T(8,128)(2,1)}, u32[]{:S(2)}) copy-start(bf16[768,2304]{1,0:T(8,128)(2,1)} %proj_ref.3) | copy-start | bytes 10616836

commit v3 on v2

--- a/solution.py
+++ b/solution.py
@@ -14,6 +14,7 @@
 EPSILON = 1e-06
 LOG2_E = math.log2(math.e)
 LANES = 128
+VMEM_BYTES = 24 * 1024 * 1024
 
 TN = (((0,), (0,)), ((), ()))
 TT = (((0,), (1,)), ((), ()))
@@ -67,7 +68,7 @@
         for head in range(HEADS):
             scores_ref[head] = dot(fields_ref[head_rows(1, head), cut], fields_ref[head_rows(0, head), cut], TN)
         for head in range(HEADS):
-            factor = scale_ref[head] * LOG2_E
+            factor = scale_ref[head : head + 1]
             for low in range(0, span, LANES):
                 lanes = slice(low, low + LANES)
                 mine = owner[:, lanes]
@@ -85,12 +86,30 @@
             mixed_ref[head_rows(0, head), cut] = mixed.astype(jnp.bfloat16)
 
 
-def time_kernel(
-    frames, scale_ref, tokens_ref, gain_ref, proj_ref, out_ref, stream_ref, held, result, fields, mixed, *work
-):
-    patches = tokens_ref.shape[0] // frames
+def pack_kernel(tokens_ref, *refs):
+    pieces, held = refs[:-1], refs[-1]
+    frames, patches = tokens_ref.shape[0], tokens_ref.shape[1] // len(pieces)
+    me = lax.axis_index("tm")
+    for frame in range(frames):
+        for part in range(held.shape[0]):
+            held[part, frame] = tokens_ref[frame, :, part * LANES : (part + 1) * LANES].astype(jnp.float32)
+    for index, piece in enumerate(pieces):
+        start = pl.multiple_of((me ^ index) * patches, patches)
+        for part in range(held.shape[0]):
+            rows = [held[part, frame, pl.ds(start, patches)] for frame in range(frames)]
+            piece[:, part * LANES : (part + 1) * LANES] = jnp.concatenate(rows, axis=0).astype(jnp.bfloat16)
+
+
+def time_kernel(frames, count, scale_ref, gain_ref, proj_ref, out_ref, *refs):
+    pieces, (stream_ref, held, result, fields, mixed, *work) = refs[:count], refs[count:]
+    patches = stream_ref.shape[0] // frames
     span, packed = time_span(frames, patches)
-    hold(held, tokens_ref)
+    me = lax.axis_index("tm")
+    for index, piece in enumerate(pieces):
+        size = piece.shape[0]
+        start = 0 if count == 1 else pl.multiple_of((me ^ index) * size, size)
+        for part in range(held.shape[0]):
+            held[part, pl.ds(start, size)] = piece[:, part * LANES : (part + 1) * LANES].astype(jnp.float32)
     tokens = jnp.concatenate([pick(held, patch, frames, patches) for patch in range(patches)], axis=0)
     project(layer_norm(tokens, gain_ref[...]), proj_ref, fields)
     attend(fields, scale_ref, mixed, *work, span, packed)
@@ -103,10 +122,9 @@
         stream_ref[:, part * LANES : (part + 1) * LANES] = result[part].astype(jnp.bfloat16)
 
 
-def space_kernel(
-    senders, sides, scale_ref, stream_ref, gain_ref, proj_ref, out_ref, block_ref, held, fields, mixed, *work
-):
-    frames, side_patches = block_ref.shape[1:3]
+def space_kernel(senders, sides, scale_ref, gain_ref, proj_ref, out_ref, stream_ref, *refs):
+    pieces, (block, held, fields, mixed, *work) = refs[:sides], refs[sides:]
+    frames, side_patches = pieces[0].shape[:2]
     piece = stream_ref.shape[0] // senders // frames
     hold(held, stream_ref)
 
@@ -124,11 +142,29 @@
 
     project(layer_norm(ordered(), gain_ref[...]), proj_ref, fields)
     attend(fields, scale_ref, mixed, *work, sides * side_patches, 1)
-    block = (ordered() + dot(mixed[...], out_ref[...], TN)).astype(jnp.bfloat16)
+    stream = ordered() + dot(mixed[...], out_ref[...], TN)
     for frame in range(frames):
         for side in range(sides):
             start = (frame * sides + side) * side_patches
-            block_ref[side, frame] = block[start : start + side_patches]
+            block[side, frame] = stream[start : start + side_patches].astype(jnp.bfloat16)
+    me = lax.axis_index("patch")
+    for index in range(sides):
+        pieces[index][...] = block[me ^ index]
+
+
+def place_kernel(*refs):
+    count = len(refs) // 2
+    pieces, whole, sems = refs[:count], refs[count], refs[count + 1 :]
+    frames = pieces[0].shape[0]
+    me = lax.axis_index("patch")
+    copies = [
+        pltpu.make_async_copy(piece, whole.at[pl.ds((me ^ index) * frames, frames)], sems[index])
+        for index, piece in enumerate(pieces)
+    ]
+    for copy in copies:
+        copy.start()
+    for copy in copies:
+        copy.wait()
 
 
 def time_span(frames, patches):
@@ -146,17 +182,70 @@
     ]
 
 
-def call(kernel, out_shape, scratch, scale, rows, gain, proj, out):
+def small_kernel(*refs):
+    count = len(refs) // 2
+    for source, target in zip(refs[:count], refs[count:]):
+        target[...] = jnp.broadcast_to(source[...], target.shape) * (LOG2_E if target.shape[0] == HEADS else 1.0)
+
+
+def small(time_scale, space_scale, time_gain, space_gain):
     whole = pl.BlockSpec(memory_space=pltpu.VMEM)
+    shapes = [(HEADS, LANES), (HEADS, LANES), (1, WIDTH), (1, WIDTH)]
+    return pl.pallas_call(
+        small_kernel,
+        out_shape=[jax.ShapeDtypeStruct(shape, jnp.float32) for shape in shapes],
+        in_specs=[whole] * 4,
+        out_specs=[whole] * 4,
+        compiler_params=pltpu.CompilerParams(vmem_limit_bytes=1024 * 1024),
+        cost_estimate=pl.CostEstimate(flops=10**10, bytes_accessed=10**5, transcendentals=0),
+    )(time_scale[:, None], space_scale[:, None], time_gain[None], space_gain[None])
+
+
+def call(kernel, out_shapes, scratch, scale, gain, proj, out, *rows):
+    whole = pl.BlockSpec(memory_space=pltpu.VMEM)
     return pl.pallas_call(
         kernel,
-        out_shape=jax.ShapeDtypeStruct(out_shape, jnp.bfloat16),
-        in_specs=[pl.BlockSpec(memory_space=pltpu.SMEM)] + [whole] * 4,
-        out_specs=whole,
+        out_shape=[jax.ShapeDtypeStruct(shape, jnp.bfloat16) for shape in out_shapes],
+        in_specs=[whole] * (4 + len(rows)),
+        out_specs=[whole] * len(out_shapes),
         scratch_shapes=scratch,
-        compiler_params=pltpu.CompilerParams(vmem_limit_bytes=40 * 1024 * 1024),
-        cost_estimate=pl.CostEstimate(flops=3 * 10**9, bytes_accessed=7 * 10**6, transcendentals=10**6),
-    )(scale, rows, gain.reshape(1, -1), proj, out)
+        compiler_params=pltpu.CompilerParams(vmem_limit_bytes=VMEM_BYTES),
+        cost_estimate=pl.CostEstimate(flops=10**10, bytes_accessed=7 * 10**6, transcendentals=10**6),
+    )(scale, gain, proj, out, *rows)
+
+
+def pack(tokens, peers):
+    frames, patches, width = tokens.shape
+    whole = pl.BlockSpec(memory_space=pltpu.VMEM)
+    return pl.pallas_call(
+        pack_kernel,
+        out_shape=[jax.ShapeDtypeStruct((frames * patches // peers, width), tokens.dtype)] * peers,
+        in_specs=[whole],
+        out_specs=[whole] * peers,
+        scratch_shapes=[pltpu.VMEM((width // LANES, frames, patches, LANES), jnp.float32)],
+        compiler_params=pltpu.CompilerParams(vmem_limit_bytes=8 * 1024 * 1024),
+    )(tokens)
+
+
+def place(pieces):
+    anywhere = pl.BlockSpec(memory_space=pl.ANY)
+    frames, patches, width = pieces[0].shape
+    return pl.pallas_call(
+        place_kernel,
+        out_shape=jax.ShapeDtypeStruct((frames * len(pieces), patches, width), pieces[0].dtype),
+        in_specs=[anywhere] * len(pieces),
+        out_specs=anywhere,
+        scratch_shapes=[pltpu.SemaphoreType.DMA] * len(pieces),
+        compiler_params=pltpu.CompilerParams(vmem_limit_bytes=1024 * 1024),
+    )(*pieces)
+
+
+def swap(pieces, axis):
+    size = len(pieces)
+    return [
+        lax.ppermute(piece, axis, [(i, i ^ index) for i in range(size)]) if index else piece
+        for index, piece in enumerate(pieces)
+    ]
 
 
 def per_device(
@@ -174,28 +263,32 @@
     peers, sides = lax.axis_size("tm"), lax.axis_size("patch")
     rows = frames * local_count
     all_frames = frames * peers
-    outgoing = tokens.reshape(frames, peers, local_count // peers, width)
-    outgoing = jnp.swapaxes(outgoing, 0, 1).reshape(peers, rows // peers, width)
-    arrived = lax.all_to_all(outgoing, "tm", split_axis=0, concat_axis=0, tiled=True).reshape(rows, width)
+    time_scale, space_scale, time_gain, space_gain = small(time_scale, space_scale, time_gain, space_gain)
+    if peers <= 8:
+        arrived = swap(pack(tokens, peers), "tm")
+    else:
+        outgoing = tokens.reshape(frames, peers, local_count // peers, width)
+        outgoing = jnp.swapaxes(outgoing, 0, 1).reshape(peers, rows // peers, width)
+        arrived = [lax.all_to_all(outgoing, "tm", split_axis=0, concat_axis=0, tiled=True).reshape(rows, width)]
     held = pltpu.VMEM((width // LANES, rows, LANES), jnp.float32)
     stream = call(
-        functools.partial(time_kernel, all_frames),
-        (rows, width),
+        functools.partial(time_kernel, all_frames, len(arrived)),
+        [(rows, width)],
         [held, held] + work_space(rows, time_span(all_frames, local_count // peers)[0]),
-        time_scale, arrived, time_gain, time_proj, time_out,
-    )
+        time_scale, time_gain, time_proj, time_out, *arrived,
+    )[0]
     senders = peers * sides
     stream = lax.all_to_all(
         stream.reshape(senders, rows // senders, width), ("tm", "patch"), split_axis=0, concat_axis=0, tiled=True
     ).reshape(rows, width)
-    block = call(
+    piece = (frames // sides, local_count, width)
+    blocks = call(
         functools.partial(space_kernel, senders, sides),
-        (sides, frames // sides, local_count, width),
-        [held] + work_space(rows, sides * local_count),
-        space_scale, stream, space_gain, space_proj, space_out,
+        [piece] * sides,
+        [pltpu.VMEM((sides,) + piece, jnp.bfloat16), held] + work_space(rows, sides * local_count),
+        space_scale, space_gain, space_proj, space_out, stream,
     )
-    block = lax.all_to_all(block, "patch", split_axis=0, concat_axis=0, tiled=True)
-    return block.reshape(frames, local_count, width)
+    return place(swap(blocks, "patch"))
 
 
 def solution(mesh):

time: 87.9 us -> 74.3 us (0.85)
  waiting for transfers between devices: 40.1 us -> 16.5 us
  blocking collectives: 14.2 us -> 26.9 us
  local copies, waits for them, and re-layouts: 9.58 us -> 4.02 us
  starting transfers between devices: 10.9 us -> 14.5 us
    all_to_all x2 -> x0, waiting for transfers between devices: 40.1 us -> none  [the longest x1 20.6 us: per_device(): lax.all_to_all(stream.reshape(senders, rows // senders, width), ('tm', 'p...]
    ppermute x0 -> x10, waiting for transfers between devices: none -> 16.5 us  [swap(): lax.ppermute(piece, axis, [(i, i ^ index) for i in range(size)])]
    ppermute x0 -> x10, starting transfers between devices: none -> 14.5 us  [swap(): lax.ppermute(piece, axis, [(i, i ^ index) for i in range(size)])]
    all_to_all x1, blocking collectives: 14.2 us -> 26.9 us  [per_device(): lax.all_to_all(stream.reshape(senders, rows // senders, width), ('tm', 'p...]
    all_to_all x2 -> x0, starting transfers between devices: 10.9 us -> none  [the longest x1 7.28 us: per_device(): lax.all_to_all(outgoing, 'tm', split_axis=0, concat_axis=0, tiled=True)]
    unnamed x17 -> x10, local copies, waits for them, and re-layouts: 7.95 us -> 1.15 us
    broadcast_in_dim x0 -> x4, local copies, waits for them, and re-layouts: none -> 2.86 us  [the longest x1 0.74 us: small(): time_scale[:, None]]
    reshape x3 -> x0, local copies, waits for them, and re-layouts: 1.63 us -> none  [the longest x1 0.94 us: per_device(): outgoing = jnp.swapaxes(outgoing, 0, 1).reshape(peers, rows // peers, width)]
  transfers between devices with their start and end apart: 2 -> 10, of which waited for: 2 -> 3; matrix products, arithmetic and copies ran while one was open for 1% -> 4% of each run, Pallas kernels for 0% -> 0%
where the time goes in v3:
time: 74.3 us; the launch traced here: 74 us
  blocking collectives  26.9 us (36%)
  waiting for transfers between devices  16.5 us (22%)
  starting transfers between devices  14.5 us (20%)
  Pallas kernels  12.1 us (16%)
  local copies, waits for them, and re-layouts  4.02 us (5%)
    all_to_all x1, blocking collectives, per_device(): lax.all_to_all(stream.reshape(senders, rows // senders, width), ('tm', 'p...  26.9 us
    ppermute x10, waiting for transfers between devices, swap(): lax.ppermute(piece, axis, [(i, i ^ index) for i in range(size)])  16.5 us
    ppermute x10, starting transfers between devices, swap(): lax.ppermute(piece, axis, [(i, i ^ index) for i in range(size)])  14.5 us
    pallas_call x2, Pallas kernels, call(): pl.pallas_call(kernel, out_shape=[jax.ShapeDtypeStruct(shape, jnp.bfloat1...  10.8 us
  transfers between devices with their start and end apart: 10, of which 3 were waited for; matrix products, arithmetic and copies ran while one was open for 4% of the time, Pallas kernels for 0%

profile of v3, /device:TPU:0, one launch (start us, length us, event | category | flops | bytes accessed | tf_op | source)
XLA Modules:
  0.0 74.0 jit_solution(15489710594091488463)
XLA Ops:
  0.0 1.1 %copy-done = bf16[8,64,768]{2,1,0:T(8,128)(2,1)S(1)} copy-done((bf16[8,64,768]{2,1,0:T(8,128)(2,1)S(1)}, bf16[8,64,768]{2,1,0:T(8,128)(2,1)}, u32[]{:S(2)}) %copy-start) | copy-done | bytes 786456
  1.1 0.3 shard_map.92
  1.4 3.0 %collective-permute-start = (bf16[64,768]{1,0:T(8,128)(2,1)S(1)}, bf16[64,768]{1,0:T(8,128)(2,1)S(1)}, u32[]{:S(2)}, u32[]{:S(2)}) collective-permute-start(bf16[64,768]{1,0:T(8,128)(2,1)S(1)} %get-tuple-element.26), channel_id=1, source_target_pairs={{0,4},{4,0},{8,12},{12,8},{16,20},{20,16},{24,28},{28,24},{1,5},{5... | collective-permute-start | bytes 294920 | tf_op jit(solution)/shard_map/ppermute | solution.py:246
  4.5 1.6 %collective-permute-start.1 = (bf16[64,768]{1,0:T(8,128)(2,1)S(1)}, bf16[64,768]{1,0:T(8,128)(2,1)S(1)}, u32[]{:S(2)}, u32[]{:S(2)}) collective-permute-start(bf16[64,768]{1,0:T(8,128)(2,1)S(1)} %get-tuple-element.27), channel_id=1, source_target_pairs={{0,8},{4,12},{8,0},{12,4},{16,24},{20,28},{24,16},{28,20},{1,9},{5... | collective-permute-start | bytes 294920 | tf_op jit(solution)/shard_map/ppermute | solution.py:246
  6.1 0.0 collective-permute-start.2
  6.1 3.0 %collective-permute-start.3 = (bf16[64,768]{1,0:T(8,128)(2,1)S(1)}, bf16[64,768]{1,0:T(8,128)(2,1)S(1)}, u32[]{:S(2)}, u32[]{:S(2)}) collective-permute-start(bf16[64,768]{1,0:T(8,128)(2,1)S(1)} %get-tuple-element.29), channel_id=1, source_target_pairs={{0,16},{4,20},{8,24},{12,28},{16,0},{20,4},{24,8},{28,12},{1,17},{... | collective-permute-start | bytes 294920 | tf_op jit(solution)/shard_map/ppermute | solution.py:246
  9.0 1.3 %collective-permute-start.4 = (bf16[64,768]{1,0:T(8,128)(2,1)S(1)}, bf16[64,768]{1,0:T(8,128)(2,1)S(1)}, u32[]{:S(2)}, u32[]{:S(2)}) collective-permute-start(bf16[64,768]{1,0:T(8,128)(2,1)S(1)} %get-tuple-element.30), channel_id=1, source_target_pairs={{0,20},{4,16},{8,28},{12,24},{16,4},{20,0},{24,12},{28,8},{1,21},{... | collective-permute-start | bytes 294920 | tf_op jit(solution)/shard_map/ppermute | solution.py:246
  10.3 0.7 broadcast_in_dim.14.refs_2_
  11.0 0.7 broadcast_in_dim.15.refs_3_
  11.7 0.7 %copy.10.refs_0_ = f32[12,1]{1,0:T(8,128)S(1)} copy(f32[12,1]{0,1:T(1,128)} %bitcast.6) | data formatting | bytes 96 | tf_op jit(solution)/shard_map/broadcast_in_dim | solution.py:201
  12.5 0.7 %copy.11.refs_1_ = f32[12,1]{1,0:T(8,128)S(1)} copy(f32[12,1]{0,1:T(1,128)} %bitcast.7) | data formatting | bytes 96 | tf_op jit(solution)/shard_map/broadcast_in_dim | solution.py:201
  13.2 0.0 collective-permute-done.refs_1_
  13.2 3.6 %collective-permute-start.5 = (bf16[64,768]{1,0:T(8,128)(2,1)S(1)}, bf16[64,768]{1,0:T(8,128)(2,1)S(1)}, u32[]{:S(2)}, u32[]{:S(2)}) collective-permute-start(bf16[64,768]{1,0:T(8,128)(2,1)S(1)} %get-tuple-element.31), channel_id=1, source_target_pairs={{0,24},{4,28},{8,16},{12,20},{16,8},{20,12},{24,0},{28,4},{1,25},{... | collective-permute-start | bytes 294920 | tf_op jit(solution)/shard_map/ppermute | solution.py:246
  16.8 0.0 collective-permute-done.1.refs_2_
  16.8 0.0 collective-permute-start.6
  16.9 0.1 shard_map.91
  16.9 0.0 collective-permute-done.2.refs_3_
  16.9 0.0 collective-permute-done.3.refs_4_
  16.9 7.3 %collective-permute-done.4.refs_5_ = bf16[64,768]{1,0:T(8,128)(2,1)S(1)} collective-permute-done((bf16[64,768]{1,0:T(8,128)(2,1)S(1)}, bf16[64,768]{1,0:T(8,128)(2,1)S(1)}, u32[]{:S(2)}, u32[]{:S(2)}) %collective-permute-start.4) | collective-permute-done | bytes 98336 | tf_op jit(solution)/shard_map/ppermute | solution.py:246
  24.2 0.0 collective-permute-done.5.refs_6_
  24.3 0.0 copy-start.2
  24.3 0.0 copy-start.4
  24.3 5.3 %shard_map.93 = bf16[512,768]{1,0:T(8,128)(2,1)S(1)} custom-call(f32[12,128]{1,0:T(8,128)S(1)} %get-tuple-element.23.scale_ref, f32[1,768]{1,0:T(1,128)S(1)} %get-tuple-element.24.gain_ref, bf16[768,2304]{1,0:T(8,128)(2,1)S(1)} %copy-done.1, bf16[768,768]{1,0:T(8,128)(2,1)S(1)} %copy-done.3, bf16[64,768]{1,0:T(8,128)(2,1)S(1)} %get-tuple-element.25.refs_0_, ...), custom_call_target="tpu_custom_call" | custom-call | flops 10000000000 | bytes 7000000 | tf_op jit(solution)/shard_map/pallas_call | solution.py:206
  29.6 26.9 %all_to_all.5 = bf16[32,16,768]{2,1,0:T(8,128)(2,1)S(1)} all-to-all(bf16[32,16,768]{2,1,0:T(8,128)(2,1)S(1)} %bitcast.4), channel_id=1, replica_groups=mesh['tm'=8,'patch'=4] {'tm','patch'}, dimensions={0} | all-to-all | bytes 1572864 | tf_op jit(solution)/shard_map/all_to_all | solution.py:281
  56.5 5.4 %shard_map.94 = (bf16[2,64,768]{2,1,0:T(8,128)(2,1)S(1)}, bf16[2,64,768]{2,1,0:T(8,128)(2,1)S(1)}, bf16[2,64,768]{2,1,0:T(8,128)(2,1)S(1)}, bf16[2,64,768]{2,1,0:T(8,128)(2,1)S(1)}) custom-call(f32[12,128]{1,0:T(8,128)S(1)} %get-tuple-element.21.scale_ref, f32[1,768]{1,0:T(1,128)S(1)} %get-tuple-element.22.gain_ref, bf16[768,2304]{1,0:T(8,128)(2,1)S(1)} %copy-done.2, ...), custom_call_target="tpu_custom_call" | custom-call | flops 10000000000 | bytes 7000000 | tf_op jit(solution)/shard_map/pallas_call | solution.py:206
  62.0 0.1 collective-permute-start.7
  62.0 1.6 %collective-permute-start.8 = (bf16[2,64,768]{2,1,0:T(8,128)(2,1)S(1)}, bf16[2,64,768]{2,1,0:T(8,128)(2,1)S(1)}, u32[]{:S(2)}, u32[]{:S(2)}) collective-permute-start(bf16[2,64,768]{2,1,0:T(8,128)(2,1)S(1)} %get-tuple-element.35), channel_id=1, source_target_pairs={{0,2},{1,3},{2,0},{3,1},{4,6},{5,7},{6,4},{7,5},{8,10},{9,11},{10,... | collective-permute-start | bytes 589832 | tf_op jit(solution)/shard_map/ppermute | solution.py:246
  63.7 0.2 collective-permute-start.9
  63.9 0.0 collective-permute-done.7.refs_1_
  63.9 5.9 %collective-permute-done.8.refs_2_ = bf16[2,64,768]{2,1,0:T(8,128)(2,1)S(1)} collective-permute-done((bf16[2,64,768]{2,1,0:T(8,128)(2,1)S(1)}, bf16[2,64,768]{2,1,0:T(8,128)(2,1)S(1)}, u32[]{:S(2)}, u32[]{:S(2)}) %collective-permute-start.8) | collective-permute-done | bytes 196640 | tf_op jit(solution)/shard_map/ppermute | solution.py:246
  69.8 3.3 %collective-permute-done.9.refs_3_ = bf16[2,64,768]{2,1,0:T(8,128)(2,1)S(1)} collective-permute-done((bf16[2,64,768]{2,1,0:T(8,128)(2,1)S(1)}, bf16[2,64,768]{2,1,0:T(8,128)(2,1)S(1)}, u32[]{:S(2)}, u32[]{:S(2)}) %collective-permute-start.9) | collective-permute-done | bytes 196640 | tf_op jit(solution)/shard_map/ppermute | solution.py:246
  73.1 0.9 %shard_map.95 = bf16[8,64,768]{2,1,0:T(8,128)(2,1)} custom-call(bf16[2,64,768]{2,1,0:T(8,128)(2,1)S(1)} %get-tuple-element.33.refs_0_, bf16[2,64,768]{2,1,0:T(8,128)(2,1)S(1)} %collective-permute-done.7.refs_1_, bf16[2,64,768]{2,1,0:T(8,128)(2,1)S(1)} %collective-permute-done.8.refs_2_, bf16[2,64,768]{2,1,0:T(8,128)(2,1)S(1)} %collective-permute-done.9.refs_3_), custom_call_target="tpu_custom_call" | custom-call | tf_op jit(solution)/shard_map/pallas_call | solution.py:233
  (8 shorter events, 0.0 us)
Async XLA Ops:
  0.0 1.1 %copy-start = (bf16[8,64,768]{2,1,0:T(8,128)(2,1)S(1)}, bf16[8,64,768]{2,1,0:T(8,128)(2,1)}, u32[]{:S(2)}) copy-start(bf16[8,64,768]{2,1,0:T(8,128)(2,1)} %tokens_ref.1) | copy-start | bytes 2359300
  1.4 11.8 %collective-permute-start = (bf16[64,768]{1,0:T(8,128)(2,1)S(1)}, bf16[64,768]{1,0:T(8,128)(2,1)S(1)}, u32[]{:S(2)}, u32[]{:S(2)}) collective-permute-start(bf16[64,768]{1,0:T(8,128)(2,1)S(1)} %get-tuple-element.26), channel_id=1, source_target_pairs={{0,4},{4,0},{8,12},{12,8},{16,20},{20,16},{24,28},{28,24},{1,5},{5... | collective-permute-start | bytes 294920 | tf_op jit(solution)/shard_map/ppermute | solution.py:246
  4.5 12.3 %collective-permute-start.1 = (bf16[64,768]{1,0:T(8,128)(2,1)S(1)}, bf16[64,768]{1,0:T(8,128)(2,1)S(1)}, u32[]{:S(2)}, u32[]{:S(2)}) collective-permute-start(bf16[64,768]{1,0:T(8,128)(2,1)S(1)} %get-tuple-element.27), channel_id=1, source_target_pairs={{0,8},{4,12},{8,0},{12,4},{16,24},{20,28},{24,16},{28,20},{1,9},{5... | collective-permute-start | bytes 294920 | tf_op jit(solution)/shard_map/ppermute | solution.py:246
  6.1 10.9 %collective-permute-start.2 = (bf16[64,768]{1,0:T(8,128)(2,1)S(1)}, bf16[64,768]{1,0:T(8,128)(2,1)S(1)}, u32[]{:S(2)}, u32[]{:S(2)}) collective-permute-start(bf16[64,768]{1,0:T(8,128)(2,1)S(1)} %get-tuple-element.28), channel_id=1, source_target_pairs={{0,12},{4,8},{8,4},{12,0},{16,28},{20,24},{24,20},{28,16},{1,13},{... | collective-permute-start | bytes 294920 | tf_op jit(solution)/shard_map/ppermute | solution.py:246
  6.1 10.9 %collective-permute-start.3 = (bf16[64,768]{1,0:T(8,128)(2,1)S(1)}, bf16[64,768]{1,0:T(8,128)(2,1)S(1)}, u32[]{:S(2)}, u32[]{:S(2)}) collective-permute-start(bf16[64,768]{1,0:T(8,128)(2,1)S(1)} %get-tuple-element.29), channel_id=1, source_target_pairs={{0,16},{4,20},{8,24},{12,28},{16,0},{20,4},{24,8},{28,12},{1,17},{... | collective-permute-start | bytes 294920 | tf_op jit(solution)/shard_map/ppermute | solution.py:246
  9.0 15.2 %collective-permute-start.4 = (bf16[64,768]{1,0:T(8,128)(2,1)S(1)}, bf16[64,768]{1,0:T(8,128)(2,1)S(1)}, u32[]{:S(2)}, u32[]{:S(2)}) collective-permute-start(bf16[64,768]{1,0:T(8,128)(2,1)S(1)} %get-tuple-element.30), channel_id=1, source_target_pairs={{0,20},{4,16},{8,28},{12,24},{16,4},{20,0},{24,12},{28,8},{1,21},{... | collective-permute-start | bytes 294920 | tf_op jit(solution)/shard_map/ppermute | solution.py:246
  13.2 11.0 %collective-permute-start.5 = (bf16[64,768]{1,0:T(8,128)(2,1)S(1)}, bf16[64,768]{1,0:T(8,128)(2,1)S(1)}, u32[]{:S(2)}, u32[]{:S(2)}) collective-permute-start(bf16[64,768]{1,0:T(8,128)(2,1)S(1)} %get-tuple-element.31), channel_id=1, source_target_pairs={{0,24},{4,28},{8,16},{12,20},{16,8},{20,12},{24,0},{28,4},{1,25},{... | collective-permute-start | bytes 294920 | tf_op jit(solution)/shard_map/ppermute | solution.py:246
  16.8 7.4 %copy-start.1 = (bf16[768,2304]{1,0:T(8,128)(2,1)S(1)}, bf16[768,2304]{1,0:T(8,128)(2,1)}, u32[]{:S(2)}) copy-start(bf16[768,2304]{1,0:T(8,128)(2,1)} %proj_ref.2) | copy-start | bytes 10616836
  16.8 7.4 %copy-start.3 = (bf16[768,768]{1,0:T(8,128)(2,1)S(1)}, bf16[768,768]{1,0:T(8,128)(2,1)}, u32[]{:S(2)}) copy-start(bf16[768,768]{1,0:T(8,128)(2,1)} %out_ref.2) | copy-start | bytes 3538948
  16.8 7.4 %collective-permute-start.6 = (bf16[64,768]{1,0:T(8,128)(2,1)S(1)}, bf16[64,768]{1,0:T(8,128)(2,1)S(1)}, u32[]{:S(2)}, u32[]{:S(2)}) collective-permute-start(bf16[64,768]{1,0:T(8,128)(2,1)S(1)} %get-tuple-element.32), channel_id=1, source_target_pairs={{0,28},{4,24},{8,20},{12,16},{16,12},{20,8},{24,4},{28,0},{1,29},{... | collective-permute-start | bytes 294920 | tf_op jit(solution)/shard_map/ppermute | solution.py:246
  24.3 32.2 %copy-start.2 = (bf16[768,2304]{1,0:T(8,128)(2,1)S(1)}, bf16[768,2304]{1,0:T(8,128)(2,1)}, u32[]{:S(2)}) copy-start(bf16[768,2304]{1,0:T(8,128)(2,1)} %proj_ref.3) | copy-start | bytes 10616836
  24.3 32.2 %copy-start.4 = (bf16[768,768]{1,0:T(8,128)(2,1)S(1)}, bf16[768,768]{1,0:T(8,128)(2,1)}, u32[]{:S(2)}) copy-start(bf16[768,768]{1,0:T(8,128)(2,1)} %out_ref.3) | copy-start | bytes 3538948
  62.0 1.9 %collective-permute-start.7 = (bf16[2,64,768]{2,1,0:T(8,128)(2,1)S(1)}, bf16[2,64,768]{2,1,0:T(8,128)(2,1)S(1)}, u32[]{:S(2)}, u32[]{:S(2)}) collective-permute-start(bf16[2,64,768]{2,1,0:T(8,128)(2,1)S(1)} %get-tuple-element.34), channel_id=1, source_target_pairs={{0,1},{1,0},{2,3},{3,2},{4,5},{5,4},{6,7},{7,6},{8,9},{9,8},{10,11... | collective-permute-start | bytes 589832 | tf_op jit(solution)/shard_map/ppermute | solution.py:246
  62.0 7.8 %collective-permute-start.8 = (bf16[2,64,768]{2,1,0:T(8,128)(2,1)S(1)}, bf16[2,64,768]{2,1,0:T(8,128)(2,1)S(1)}, u32[]{:S(2)}, u32[]{:S(2)}) collective-permute-start(bf16[2,64,768]{2,1,0:T(8,128)(2,1)S(1)} %get-tuple-element.35), channel_id=1, source_target_pairs={{0,2},{1,3},{2,0},{3,1},{4,6},{5,7},{6,4},{7,5},{8,10},{9,11},{10,... | collective-permute-start | bytes 589832 | tf_op jit(solution)/shard_map/ppermute | solution.py:246
  63.7 9.4 %collective-permute-start.9 = (bf16[2,64,768]{2,1,0:T(8,128)(2,1)S(1)}, bf16[2,64,768]{2,1,0:T(8,128)(2,1)S(1)}, u32[]{:S(2)}, u32[]{:S(2)}) collective-permute-start(bf16[2,64,768]{2,1,0:T(8,128)(2,1)S(1)} %get-tuple-element.36), channel_id=1, source_target_pairs={{0,3},{1,2},{2,1},{3,0},{4,7},{5,6},{6,5},{7,4},{8,11},{9,10},{10,... | collective-permute-start | bytes 589832 | tf_op jit(solution)/shard_map/ppermute | solution.py:246

commit v4 on v3

--- a/solution.py
+++ b/solution.py
@@ -86,6 +86,9 @@
             mixed_ref[head_rows(0, head), cut] = mixed.astype(jnp.bfloat16)
 
 
+ORDER = {2: [1], 4: [2, 3, 1], 8: [2, 4, 6, 5, 7, 3, 1]}
+
+
 def pack_kernel(tokens_ref, *refs):
     pieces, held = refs[:-1], refs[-1]
     frames, patches = tokens_ref.shape[0], tokens_ref.shape[1] // len(pieces)
@@ -102,10 +105,11 @@
 
 def time_kernel(frames, count, scale_ref, gain_ref, proj_ref, out_ref, *refs):
     pieces, (stream_ref, held, result, fields, mixed, *work) = refs[:count], refs[count:]
+    order = [0] + ORDER[count] if count > 1 else [0]
     patches = stream_ref.shape[0] // frames
     span, packed = time_span(frames, patches)
     me = lax.axis_index("tm")
-    for index, piece in enumerate(pieces):
+    for index, piece in zip(order, pieces):
         size = piece.shape[0]
         start = 0 if count == 1 else pl.multiple_of((me ^ index) * size, size)
         for part in range(held.shape[0]):
@@ -122,43 +126,40 @@
         stream_ref[:, part * LANES : (part + 1) * LANES] = result[part].astype(jnp.bfloat16)
 
 
-def space_kernel(senders, sides, scale_ref, gain_ref, proj_ref, out_ref, stream_ref, *refs):
+def space_kernel(
+    frame, senders, sides, frames, scale_ref, gain_ref, proj_ref, out_ref, stream_ref, *refs
+):
     pieces, (block, held, fields, mixed, *work) = refs[:sides], refs[sides:]
-    frames, side_patches = pieces[0].shape[:2]
+    side_patches = pieces[0].shape[0]
     piece = stream_ref.shape[0] // senders // frames
     hold(held, stream_ref)
 
     def ordered():
         parts = []
-        for frame in range(frames):
-            for side in range(sides):
-                if piece % 8:
-                    start = (side * frames + frame) * piece
-                    parts.append(pick(held, start, senders // sides, sides * frames))
-                else:
-                    for sender in range(side, senders, sides):
-                        parts.append(pick(held, (sender * frames + frame) * piece, piece, 1))
+        for side in range(sides):
+            if piece % 8:
+                start = (side * frames + frame) * piece
+                parts.append(pick(held, start, senders // sides, sides * frames))
+            else:
+                for sender in range(side, senders, sides):
+                    parts.append(pick(held, (sender * frames + frame) * piece, piece, 1))
         return jnp.concatenate(parts, axis=0)
 
     project(layer_norm(ordered(), gain_ref[...]), proj_ref, fields)
     attend(fields, scale_ref, mixed, *work, sides * side_patches, 1)
     stream = ordered() + dot(mixed[...], out_ref[...], TN)
-    for frame in range(frames):
-        for side in range(sides):
-            start = (frame * sides + side) * side_patches
-            block[side, frame] = stream[start : start + side_patches].astype(jnp.bfloat16)
+    for side in range(sides):
+        block[side] = stream[side * side_patches : (side + 1) * side_patches].astype(jnp.bfloat16)
     me = lax.axis_index("patch")
     for index in range(sides):
         pieces[index][...] = block[me ^ index]
 
 
-def place_kernel(*refs):
-    count = len(refs) // 2
-    pieces, whole, sems = refs[:count], refs[count], refs[count + 1 :]
-    frames = pieces[0].shape[0]
+def place_kernel(frame, frames, sides, *refs):
+    pieces, whole, sems = refs[:sides], refs[-sides - 1], refs[-sides:]
     me = lax.axis_index("patch")
     copies = [
-        pltpu.make_async_copy(piece, whole.at[pl.ds((me ^ index) * frames, frames)], sems[index])
+        pltpu.make_async_copy(piece, whole.at[(me ^ index) * frames + frame], sems[index])
         for index, piece in enumerate(pieces)
     ]
     for copy in copies:
@@ -227,25 +228,28 @@
     )(tokens)
 
 
-def place(pieces):
+def place(frame, frames, pieces, whole):
     anywhere = pl.BlockSpec(memory_space=pl.ANY)
-    frames, patches, width = pieces[0].shape
+    sides = len(pieces)
+    others = [] if whole is None else [whole]
     return pl.pallas_call(
-        place_kernel,
-        out_shape=jax.ShapeDtypeStruct((frames * len(pieces), patches, width), pieces[0].dtype),
-        in_specs=[anywhere] * len(pieces),
+        functools.partial(place_kernel, frame, frames, sides),
+        out_shape=jax.ShapeDtypeStruct((sides * frames,) + pieces[0].shape, pieces[0].dtype),
+        in_specs=[anywhere] * (sides + len(others)),
         out_specs=anywhere,
-        scratch_shapes=[pltpu.SemaphoreType.DMA] * len(pieces),
+        scratch_shapes=[pltpu.SemaphoreType.DMA] * sides,
+        input_output_aliases={sides: 0} if others else {},
         compiler_params=pltpu.CompilerParams(vmem_limit_bytes=1024 * 1024),
-    )(*pieces)
+        cost_estimate=pl.CostEstimate(flops=10**10, bytes_accessed=10**6, transcendentals=0),
+    )(*pieces, *others)
 
 
 def swap(pieces, axis):
     size = len(pieces)
-    return [
-        lax.ppermute(piece, axis, [(i, i ^ index) for i in range(size)]) if index else piece
-        for index, piece in enumerate(pieces)
-    ]
+    arrived = list(pieces)
+    for index in ORDER[size]:
+        arrived[index] = lax.ppermute(pieces[index], axis, [(i, i ^ index) for i in range(size)])
+    return arrived
 
 
 def per_device(
@@ -266,6 +270,7 @@
     time_scale, space_scale, time_gain, space_gain = small(time_scale, space_scale, time_gain, space_gain)
     if peers <= 8:
         arrived = swap(pack(tokens, peers), "tm")
+        arrived = [arrived[index] for index in [0] + ORDER[peers]]
     else:
         outgoing = tokens.reshape(frames, peers, local_count // peers, width)
         outgoing = jnp.swapaxes(outgoing, 0, 1).reshape(peers, rows // peers, width)
@@ -281,14 +286,18 @@
     stream = lax.all_to_all(
         stream.reshape(senders, rows // senders, width), ("tm", "patch"), split_axis=0, concat_axis=0, tiled=True
     ).reshape(rows, width)
-    piece = (frames // sides, local_count, width)
-    blocks = call(
-        functools.partial(space_kernel, senders, sides),
-        [piece] * sides,
-        [pltpu.VMEM((sides,) + piece, jnp.bfloat16), held] + work_space(rows, sides * local_count),
-        space_scale, space_gain, space_proj, space_out, stream,
-    )
-    return place(swap(blocks, "patch"))
+    own_frames = frames // sides
+    piece = (local_count, width)
+    block = None
+    for frame in range(own_frames):
+        blocks = call(
+            functools.partial(space_kernel, frame, senders, sides, own_frames),
+            [piece] * sides,
+            [pltpu.VMEM((sides,) + piece, jnp.bfloat16), held] + work_space(rows // own_frames, sides * local_count),
+            space_scale, space_gain, space_proj, space_out, stream,
+        )
+        block = place(frame, own_frames, swap(blocks, "patch"), block)
+    return block
 
 
 def solution(mesh):

time: 74.3 us -> 70.5 us (0.949)
  waiting for transfers between devices: 16.5 us -> 11.9 us
  blocking collectives: 26.9 us -> 24.6 us
  starting transfers between devices: 14.5 us -> 16.6 us
  Pallas kernels: 12.1 us -> 13 us
    ppermute x10 -> x13, waiting for transfers between devices: 16.5 us -> 11.9 us  [swap(): lax.ppermute(pieces[index], axis, [(i, i ^ index) for i in range(size)])]
    all_to_all x1, blocking collectives: 26.9 us -> 24.6 us  [per_device(): lax.all_to_all(stream.reshape(senders, rows // senders, width), ('tm', 'p...]
    ppermute x10 -> x13, starting transfers between devices: 14.5 us -> 16.6 us  [swap(): lax.ppermute(pieces[index], axis, [(i, i ^ index) for i in range(size)])]
    pallas_call x1 -> x2, Pallas kernels: 0.9 us -> 1.54 us  [place(): pl.pallas_call(functools.partial(place_kernel, frame, frames, sides), out...]
    pallas_call x2 -> x3, Pallas kernels: 10.8 us -> 11.1 us  [call(): pl.pallas_call(kernel, out_shape=[jax.ShapeDtypeStruct(shape, jnp.bfloat1...]
  transfers between devices with their start and end apart: 10 -> 13, of which waited for: 3 -> 6; matrix products, arithmetic and copies ran while one was open for 4% -> 4% of each run, Pallas kernels for 0% -> 5%
where the time goes in v4:
time: 70.5 us; the launch traced here: 70.3 us
  blocking collectives  24.6 us (35%)
  starting transfers between devices  16.6 us (24%)
  Pallas kernels  13 us (18%)
  waiting for transfers between devices  11.9 us (17%)
  local copies, waits for them, and re-layouts  4.01 us (6%)
    all_to_all x1, blocking collectives, per_device(): lax.all_to_all(stream.reshape(senders, rows // senders, width), ('tm', 'p...  24.6 us
    ppermute x13, starting transfers between devices, swap(): lax.ppermute(pieces[index], axis, [(i, i ^ index) for i in range(size)])  16.6 us
    ppermute x13, waiting for transfers between devices, swap(): lax.ppermute(pieces[index], axis, [(i, i ^ index) for i in range(size)])  11.9 us
    pallas_call x3, Pallas kernels, call(): pl.pallas_call(kernel, out_shape=[jax.ShapeDtypeStruct(shape, jnp.bfloat1...  11.1 us
    pallas_call x2, Pallas kernels, place(): pl.pallas_call(functools.partial(place_kernel, frame, frames, sides), out...  1.54 us
  transfers between devices with their start and end apart: 13, of which 6 were waited for; matrix products, arithmetic and copies ran while one was open for 4% of the time, Pallas kernels for 5%

profile of v4, /device:TPU:0, one launch (start us, length us, event | category | flops | bytes accessed | tf_op | source)
XLA Modules:
  0.0 70.3 jit_solution(9878907740454401486)
XLA Ops:
  0.0 1.1 %copy-done = bf16[8,64,768]{2,1,0:T(8,128)(2,1)S(1)} copy-done((bf16[8,64,768]{2,1,0:T(8,128)(2,1)S(1)}, bf16[8,64,768]{2,1,0:T(8,128)(2,1)}, u32[]{:S(2)}) %copy-start) | copy-done | bytes 786456
  1.1 0.3 shard_map.92
  1.4 3.1 %collective-permute-start = (bf16[64,768]{1,0:T(8,128)(2,1)S(1)}, bf16[64,768]{1,0:T(8,128)(2,1)S(1)}, u32[]{:S(2)}, u32[]{:S(2)}) collective-permute-start(bf16[64,768]{1,0:T(8,128)(2,1)S(1)} %get-tuple-element.30), channel_id=1, source_target_pairs={{0,8},{4,12},{8,0},{12,4},{16,24},{20,28},{24,16},{28,20},{1,9},{5... | collective-permute-start | bytes 294920 | tf_op jit(solution)/shard_map/ppermute | solution.py:251
  4.5 2.6 %collective-permute-start.1 = (bf16[64,768]{1,0:T(8,128)(2,1)S(1)}, bf16[64,768]{1,0:T(8,128)(2,1)S(1)}, u32[]{:S(2)}, u32[]{:S(2)}) collective-permute-start(bf16[64,768]{1,0:T(8,128)(2,1)S(1)} %get-tuple-element.31), channel_id=1, source_target_pairs={{0,16},{4,20},{8,24},{12,28},{16,0},{20,4},{24,8},{28,12},{1,17},{... | collective-permute-start | bytes 294920 | tf_op jit(solution)/shard_map/ppermute | solution.py:251
  7.1 0.0 collective-permute-start.2
  7.1 2.9 %collective-permute-start.3 = (bf16[64,768]{1,0:T(8,128)(2,1)S(1)}, bf16[64,768]{1,0:T(8,128)(2,1)S(1)}, u32[]{:S(2)}, u32[]{:S(2)}) collective-permute-start(bf16[64,768]{1,0:T(8,128)(2,1)S(1)} %get-tuple-element.33), channel_id=1, source_target_pairs={{0,20},{4,16},{8,28},{12,24},{16,4},{20,0},{24,12},{28,8},{1,21},{... | collective-permute-start | bytes 294920 | tf_op jit(solution)/shard_map/ppermute | solution.py:251
  10.0 1.9 %collective-permute-start.4 = (bf16[64,768]{1,0:T(8,128)(2,1)S(1)}, bf16[64,768]{1,0:T(8,128)(2,1)S(1)}, u32[]{:S(2)}, u32[]{:S(2)}) collective-permute-start(bf16[64,768]{1,0:T(8,128)(2,1)S(1)} %get-tuple-element.34), channel_id=1, source_target_pairs={{0,28},{4,24},{8,20},{12,16},{16,12},{20,8},{24,4},{28,0},{1,29},{... | collective-permute-start | bytes 294920 | tf_op jit(solution)/shard_map/ppermute | solution.py:251
  11.9 0.7 broadcast_in_dim.14.refs_2_
  12.6 0.7 broadcast_in_dim.15.refs_3_
  13.3 0.7 %copy.11.refs_0_ = f32[12,1]{1,0:T(8,128)S(1)} copy(f32[12,1]{0,1:T(1,128)} %bitcast.7) | data formatting | bytes 96 | tf_op jit(solution)/shard_map/broadcast_in_dim | solution.py:202
  14.0 0.7 %copy.12.refs_1_ = f32[12,1]{1,0:T(8,128)S(1)} copy(f32[12,1]{0,1:T(1,128)} %bitcast.8) | data formatting | bytes 96 | tf_op jit(solution)/shard_map/broadcast_in_dim | solution.py:202
  14.8 0.8 %collective-permute-start.5 = (bf16[64,768]{1,0:T(8,128)(2,1)S(1)}, bf16[64,768]{1,0:T(8,128)(2,1)S(1)}, u32[]{:S(2)}, u32[]{:S(2)}) collective-permute-start(bf16[64,768]{1,0:T(8,128)(2,1)S(1)} %get-tuple-element.35), channel_id=1, source_target_pairs={{0,12},{4,8},{8,4},{12,0},{16,28},{20,24},{24,20},{28,16},{1,13},{... | collective-permute-start | bytes 294920 | tf_op jit(solution)/shard_map/ppermute | solution.py:251
  15.6 3.7 %collective-permute-done.1.refs_2_ = bf16[64,768]{1,0:T(8,128)(2,1)S(1)} collective-permute-done((bf16[64,768]{1,0:T(8,128)(2,1)S(1)}, bf16[64,768]{1,0:T(8,128)(2,1)S(1)}, u32[]{:S(2)}, u32[]{:S(2)}) %collective-permute-start.1) | collective-permute-done | bytes 98336 | tf_op jit(solution)/shard_map/ppermute | solution.py:251
  19.3 1.5 %collective-permute-start.6 = (bf16[64,768]{1,0:T(8,128)(2,1)S(1)}, bf16[64,768]{1,0:T(8,128)(2,1)S(1)}, u32[]{:S(2)}, u32[]{:S(2)}) collective-permute-start(bf16[64,768]{1,0:T(8,128)(2,1)S(1)} %get-tuple-element.36), channel_id=1, source_target_pairs={{0,4},{4,0},{8,12},{12,8},{16,20},{20,16},{24,28},{28,24},{1,5},{5... | collective-permute-start | bytes 294920 | tf_op jit(solution)/shard_map/ppermute | solution.py:251
  20.8 0.1 shard_map.91
  20.9 3.5 %collective-permute-done.3.refs_4_ = bf16[64,768]{1,0:T(8,128)(2,1)S(1)} collective-permute-done((bf16[64,768]{1,0:T(8,128)(2,1)S(1)}, bf16[64,768]{1,0:T(8,128)(2,1)S(1)}, u32[]{:S(2)}, u32[]{:S(2)}) %collective-permute-start.3) | collective-permute-done | bytes 98336 | tf_op jit(solution)/shard_map/ppermute | solution.py:251
  24.4 0.0 collective-permute-done.5.refs_6_
  24.4 0.4 collective-permute-done.6.refs_7_
  24.7 5.3 %shard_map.93 = bf16[512,768]{1,0:T(8,128)(2,1)S(1)} custom-call(f32[12,128]{1,0:T(8,128)S(1)} %get-tuple-element.27.scale_ref, f32[1,768]{1,0:T(1,128)S(1)} %get-tuple-element.28.gain_ref, bf16[768,2304]{1,0:T(8,128)(2,1)S(1)} %copy-done.1, bf16[768,768]{1,0:T(8,128)(2,1)S(1)} %copy-done.3, bf16[64,768]{1,0:T(8,128)(2,1)S(1)} %get-tuple-element.29.refs_0_, ...), custom_call_target="tpu_custom_call" | custom-call | flops 10000000000 | bytes 7000000 | tf_op jit(solution)/shard_map/pallas_call | solution.py:207
  30.1 24.6 %all_to_all.5 = bf16[32,16,768]{2,1,0:T(8,128)(2,1)S(1)} all-to-all(bf16[32,16,768]{2,1,0:T(8,128)(2,1)S(1)} %bitcast.6), channel_id=1, replica_groups=mesh['tm'=8,'patch'=4] {'tm','patch'}, dimensions={0} | all-to-all | bytes 1572864 | tf_op jit(solution)/shard_map/all_to_all | solution.py:286
  54.7 2.9 %shard_map.95 = (bf16[64,768]{1,0:T(8,128)(2,1)S(1)}, bf16[64,768]{1,0:T(8,128)(2,1)S(1)}, bf16[64,768]{1,0:T(8,128)(2,1)S(1)}, bf16[64,768]{1,0:T(8,128)(2,1)S(1)}) custom-call(f32[12,128]{1,0:T(8,128)S(1)} %get-tuple-element.25.scale_ref, f32[1,768]{1,0:T(1,128)S(1)} %get-tuple-element.26.gain_ref, bf16[768,2304]{1,0:T(8,128)(2,1)S(1)} %copy-done.2, ...), custom_call_target="tpu_custom_call" | custom-call | flops 10000000000 | bytes 7000000 | tf_op jit(solution)/shard_map/pallas_call | solution.py:207
  57.6 0.1 collective-permute-start.10
  57.7 1.6 %collective-permute-start.11 = (bf16[64,768]{1,0:T(8,128)(2,1)S(1)}, bf16[64,768]{1,0:T(8,128)(2,1)S(1)}, u32[]{:S(2)}, u32[]{:S(2)}) collective-permute-start(bf16[64,768]{1,0:T(8,128)(2,1)S(1)} %get-tuple-element.43), channel_id=1, source_target_pairs={{0,2},{1,3},{2,0},{3,1},{4,6},{5,7},{6,4},{7,5},{8,10},{9,11},{10,... | collective-permute-start | bytes 294920 | tf_op jit(solution)/shard_map/ppermute | solution.py:251
  59.3 0.2 collective-permute-start.12
  59.5 2.9 %shard_map.94 = (bf16[64,768]{1,0:T(8,128)(2,1)S(1)}, bf16[64,768]{1,0:T(8,128)(2,1)S(1)}, bf16[64,768]{1,0:T(8,128)(2,1)S(1)}, bf16[64,768]{1,0:T(8,128)(2,1)S(1)}) custom-call(f32[12,128]{1,0:T(8,128)S(1)} %get-tuple-element.25.scale_ref, f32[1,768]{1,0:T(1,128)S(1)} %get-tuple-element.26.gain_ref, bf16[768,2304]{1,0:T(8,128)(2,1)S(1)} %copy-done.2, ...), custom_call_target="tpu_custom_call" | custom-call | flops 10000000000 | bytes 7000000 | tf_op jit(solution)/shard_map/pallas_call | solution.py:207
  62.4 0.4 collective-permute-start.7
  62.8 1.6 %collective-permute-start.8 = (bf16[64,768]{1,0:T(8,128)(2,1)S(1)}, bf16[64,768]{1,0:T(8,128)(2,1)S(1)}, u32[]{:S(2)}, u32[]{:S(2)}) collective-permute-start(bf16[64,768]{1,0:T(8,128)(2,1)S(1)} %get-tuple-element.39), channel_id=1, source_target_pairs={{0,2},{1,3},{2,0},{3,1},{4,6},{5,7},{6,4},{7,5},{8,10},{9,11},{10,... | collective-permute-start | bytes 294920 | tf_op jit(solution)/shard_map/ppermute | solution.py:251
  64.4 0.1 collective-permute-done.12.refs_3_
  64.5 0.8 %shard_map.96.refs_4_ = bf16[8,64,768]{2,1,0:T(8,128)(2,1)} custom-call(bf16[64,768]{1,0:T(8,128)(2,1)S(1)} %get-tuple-element.41.refs_0_, bf16[64,768]{1,0:T(8,128)(2,1)S(1)} %collective-permute-done.10.refs_1_, bf16[64,768]{1,0:T(8,128)(2,1)S(1)} %collective-permute-done.11.refs_2_, bf16[64,768]{1,0:T(8,128)(2,1)S(1)} %collective-permute-done.12.refs_3_), custom_call_target="tpu_custom_call" | custom-call | flops 10000000000 | bytes 1000000 | tf_op jit(solution)/shard_map/pallas_call | solution.py:235
  65.3 2.7 %collective-permute-done.8.refs_2_ = bf16[64,768]{1,0:T(8,128)(2,1)S(1)} collective-permute-done((bf16[64,768]{1,0:T(8,128)(2,1)S(1)}, bf16[64,768]{1,0:T(8,128)(2,1)S(1)}, u32[]{:S(2)}, u32[]{:S(2)}) %collective-permute-start.8) | collective-permute-done | bytes 98336 | tf_op jit(solution)/shard_map/ppermute | solution.py:251
  68.0 1.5 %collective-permute-done.9.refs_3_ = bf16[64,768]{1,0:T(8,128)(2,1)S(1)} collective-permute-done((bf16[64,768]{1,0:T(8,128)(2,1)S(1)}, bf16[64,768]{1,0:T(8,128)(2,1)S(1)}, u32[]{:S(2)}, u32[]{:S(2)}) %collective-permute-start.9) | collective-permute-done | bytes 98336 | tf_op jit(solution)/shard_map/ppermute | solution.py:251
  69.5 0.8 %shard_map.97 = bf16[8,64,768]{2,1,0:T(8,128)(2,1)} custom-call(bf16[64,768]{1,0:T(8,128)(2,1)S(1)} %get-tuple-element.37.refs_0_, bf16[64,768]{1,0:T(8,128)(2,1)S(1)} %collective-permute-done.7.refs_1_, bf16[64,768]{1,0:T(8,128)(2,1)S(1)} %collective-permute-done.8.refs_2_, ...), custom_call_target="tpu_custom_call", output_to_operand_aliasing={{}: (4, {})} | custom-call | flops 10000000000 | bytes 1000000 | tf_op jit(solution)/shard_map/pallas_call | solution.py:235
  (16 shorter events, 0.0 us)
Async XLA Ops:
  0.0 1.1 %copy-start = (bf16[8,64,768]{2,1,0:T(8,128)(2,1)S(1)}, bf16[8,64,768]{2,1,0:T(8,128)(2,1)}, u32[]{:S(2)}) copy-start(bf16[8,64,768]{2,1,0:T(8,128)(2,1)} %tokens_ref.1) | copy-start | bytes 2359300
  1.4 13.3 %collective-permute-start = (bf16[64,768]{1,0:T(8,128)(2,1)S(1)}, bf16[64,768]{1,0:T(8,128)(2,1)S(1)}, u32[]{:S(2)}, u32[]{:S(2)}) collective-permute-start(bf16[64,768]{1,0:T(8,128)(2,1)S(1)} %get-tuple-element.30), channel_id=1, source_target_pairs={{0,8},{4,12},{8,0},{12,4},{16,24},{20,28},{24,16},{28,20},{1,9},{5... | collective-permute-start | bytes 294920 | tf_op jit(solution)/shard_map/ppermute | solution.py:251
  4.5 14.8 %collective-permute-start.1 = (bf16[64,768]{1,0:T(8,128)(2,1)S(1)}, bf16[64,768]{1,0:T(8,128)(2,1)S(1)}, u32[]{:S(2)}, u32[]{:S(2)}) collective-permute-start(bf16[64,768]{1,0:T(8,128)(2,1)S(1)} %get-tuple-element.31), channel_id=1, source_target_pairs={{0,16},{4,20},{8,24},{12,28},{16,0},{20,4},{24,8},{28,12},{1,17},{... | collective-permute-start | bytes 294920 | tf_op jit(solution)/shard_map/ppermute | solution.py:251
  7.1 13.7 %collective-permute-start.2 = (bf16[64,768]{1,0:T(8,128)(2,1)S(1)}, bf16[64,768]{1,0:T(8,128)(2,1)S(1)}, u32[]{:S(2)}, u32[]{:S(2)}) collective-permute-start(bf16[64,768]{1,0:T(8,128)(2,1)S(1)} %get-tuple-element.32), channel_id=1, source_target_pairs={{0,24},{4,28},{8,16},{12,20},{16,8},{20,12},{24,0},{28,4},{1,25},{... | collective-permute-start | bytes 294920 | tf_op jit(solution)/shard_map/ppermute | solution.py:251
  7.1 17.2 %collective-permute-start.3 = (bf16[64,768]{1,0:T(8,128)(2,1)S(1)}, bf16[64,768]{1,0:T(8,128)(2,1)S(1)}, u32[]{:S(2)}, u32[]{:S(2)}) collective-permute-start(bf16[64,768]{1,0:T(8,128)(2,1)S(1)} %get-tuple-element.33), channel_id=1, source_target_pairs={{0,20},{4,16},{8,28},{12,24},{16,4},{20,0},{24,12},{28,8},{1,21},{... | collective-permute-start | bytes 294920 | tf_op jit(solution)/shard_map/ppermute | solution.py:251
  10.0 14.4 %collective-permute-start.4 = (bf16[64,768]{1,0:T(8,128)(2,1)S(1)}, bf16[64,768]{1,0:T(8,128)(2,1)S(1)}, u32[]{:S(2)}, u32[]{:S(2)}) collective-permute-start(bf16[64,768]{1,0:T(8,128)(2,1)S(1)} %get-tuple-element.34), channel_id=1, source_target_pairs={{0,28},{4,24},{8,20},{12,16},{16,12},{20,8},{24,4},{28,0},{1,29},{... | collective-permute-start | bytes 294920 | tf_op jit(solution)/shard_map/ppermute | solution.py:251
  14.8 9.6 %collective-permute-start.5 = (bf16[64,768]{1,0:T(8,128)(2,1)S(1)}, bf16[64,768]{1,0:T(8,128)(2,1)S(1)}, u32[]{:S(2)}, u32[]{:S(2)}) collective-permute-start(bf16[64,768]{1,0:T(8,128)(2,1)S(1)} %get-tuple-element.35), channel_id=1, source_target_pairs={{0,12},{4,8},{8,4},{12,0},{16,28},{20,24},{24,20},{28,16},{1,13},{... | collective-permute-start | bytes 294920 | tf_op jit(solution)/shard_map/ppermute | solution.py:251
  19.3 5.4 %copy-start.1 = (bf16[768,2304]{1,0:T(8,128)(2,1)S(1)}, bf16[768,2304]{1,0:T(8,128)(2,1)}, u32[]{:S(2)}) copy-start(bf16[768,2304]{1,0:T(8,128)(2,1)} %proj_ref.3) | copy-start | bytes 10616836
  19.3 5.4 %copy-start.3 = (bf16[768,768]{1,0:T(8,128)(2,1)S(1)}, bf16[768,768]{1,0:T(8,128)(2,1)}, u32[]{:S(2)}) copy-start(bf16[768,768]{1,0:T(8,128)(2,1)} %out_ref.3) | copy-start | bytes 3538948
  19.3 5.4 %collective-permute-start.6 = (bf16[64,768]{1,0:T(8,128)(2,1)S(1)}, bf16[64,768]{1,0:T(8,128)(2,1)S(1)}, u32[]{:S(2)}, u32[]{:S(2)}) collective-permute-start(bf16[64,768]{1,0:T(8,128)(2,1)S(1)} %get-tuple-element.36), channel_id=1, source_target_pairs={{0,4},{4,0},{8,12},{12,8},{16,20},{20,16},{24,28},{28,24},{1,5},{5... | collective-permute-start | bytes 294920 | tf_op jit(solution)/shard_map/ppermute | solution.py:251
  24.7 30.0 %copy-start.2 = (bf16[768,2304]{1,0:T(8,128)(2,1)S(1)}, bf16[768,2304]{1,0:T(8,128)(2,1)}, u32[]{:S(2)}) copy-start(bf16[768,2304]{1,0:T(8,128)(2,1)} %proj_ref.5) | copy-start | bytes 10616836
  24.7 30.0 %copy-start.4 = (bf16[768,768]{1,0:T(8,128)(2,1)S(1)}, bf16[768,768]{1,0:T(8,128)(2,1)}, u32[]{:S(2)}) copy-start(bf16[768,768]{1,0:T(8,128)(2,1)} %out_ref.5) | copy-start | bytes 3538948
  57.6 6.8 %collective-permute-start.10 = (bf16[64,768]{1,0:T(8,128)(2,1)S(1)}, bf16[64,768]{1,0:T(8,128)(2,1)S(1)}, u32[]{:S(2)}, u32[]{:S(2)}) collective-permute-start(bf16[64,768]{1,0:T(8,128)(2,1)S(1)} %get-tuple-element.42), channel_id=1, source_target_pairs={{0,1},{1,0},{2,3},{3,2},{4,5},{5,4},{6,7},{7,6},{8,9},{9,8},{10,11... | collective-permute-start | bytes 294920 | tf_op jit(solution)/shard_map/ppermute | solution.py:251
  57.7 6.7 %collective-permute-start.11 = (bf16[64,768]{1,0:T(8,128)(2,1)S(1)}, bf16[64,768]{1,0:T(8,128)(2,1)S(1)}, u32[]{:S(2)}, u32[]{:S(2)}) collective-permute-start(bf16[64,768]{1,0:T(8,128)(2,1)S(1)} %get-tuple-element.43), channel_id=1, source_target_pairs={{0,2},{1,3},{2,0},{3,1},{4,6},{5,7},{6,4},{7,5},{8,10},{9,11},{10,... | collective-permute-start | bytes 294920 | tf_op jit(solution)/shard_map/ppermute | solution.py:251
  59.3 5.2 %collective-permute-start.12 = (bf16[64,768]{1,0:T(8,128)(2,1)S(1)}, bf16[64,768]{1,0:T(8,128)(2,1)S(1)}, u32[]{:S(2)}, u32[]{:S(2)}) collective-permute-start(bf16[64,768]{1,0:T(8,128)(2,1)S(1)} %get-tuple-element.44), channel_id=1, source_target_pairs={{0,3},{1,2},{2,1},{3,0},{4,7},{5,6},{6,5},{7,4},{8,11},{9,10},{10,... | collective-permute-start | bytes 294920 | tf_op jit(solution)/shard_map/ppermute | solution.py:251
  62.4 2.9 %collective-permute-start.7 = (bf16[64,768]{1,0:T(8,128)(2,1)S(1)}, bf16[64,768]{1,0:T(8,128)(2,1)S(1)}, u32[]{:S(2)}, u32[]{:S(2)}) collective-permute-start(bf16[64,768]{1,0:T(8,128)(2,1)S(1)} %get-tuple-element.38), channel_id=1, source_target_pairs={{0,1},{1,0},{2,3},{3,2},{4,5},{5,4},{6,7},{7,6},{8,9},{9,8},{10,11... | collective-permute-start | bytes 294920 | tf_op jit(solution)/shard_map/ppermute | solution.py:251
  62.8 5.2 %collective-permute-start.8 = (bf16[64,768]{1,0:T(8,128)(2,1)S(1)}, bf16[64,768]{1,0:T(8,128)(2,1)S(1)}, u32[]{:S(2)}, u32[]{:S(2)}) collective-permute-start(bf16[64,768]{1,0:T(8,128)(2,1)S(1)} %get-tuple-element.39), channel_id=1, source_target_pairs={{0,2},{1,3},{2,0},{3,1},{4,6},{5,7},{6,4},{7,5},{8,10},{9,11},{10,... | collective-permute-start | bytes 294920 | tf_op jit(solution)/shard_map/ppermute | solution.py:251
  64.4 5.1 %collective-permute-start.9 = (bf16[64,768]{1,0:T(8,128)(2,1)S(1)}, bf16[64,768]{1,0:T(8,128)(2,1)S(1)}, u32[]{:S(2)}, u32[]{:S(2)}) collective-permute-start(bf16[64,768]{1,0:T(8,128)(2,1)S(1)} %get-tuple-element.40), channel_id=1, source_target_pairs={{0,3},{1,2},{2,1},{3,0},{4,7},{5,6},{6,5},{7,4},{8,11},{9,10},{10,... | collective-permute-start | bytes 294920 | tf_op jit(solution)/shard_map/ppermute | solution.py:251

commit v5 on v4

v5 whole, which is shorter than its diff:
```python
import functools
import math

import jax
import jax.numpy as jnp
from jax import lax
from jax.experimental import pallas as pl
from jax.experimental.pallas import tpu as pltpu
from jax.sharding import PartitionSpec as P

HEADS = 12
HEAD_DIM = 64
WIDTH = HEADS * HEAD_DIM
EPSILON = 1e-06
LOG2_E = math.log2(math.e)
LANES = 128
AHEAD = 12
VMEM_BYTES = 24 * 1024 * 1024

TN = (((0,), (0,)), ((), ()))
TT = (((0,), (1,)), ((), ()))


def dot(left, right, dims=(((1,), (0,)), ((), ()))):
    return lax.dot_general(left, right, dims, preferred_element_type=jnp.float32)


def layer_norm(values, gain):
    centred = values - jnp.mean(values, axis=-1, keepdims=True)
    spread = jnp.mean(centred * centred, axis=-1, keepdims=True)
    return (centred * lax.rsqrt(spread + EPSILON) * gain).astype(jnp.bfloat16)


def unit_columns(fields):
    heads = fields.reshape(HEADS, HEAD_DIM, fields.shape[1])
    squares = jnp.sum(heads * heads, axis=1, keepdims=True)
    return (heads * lax.rsqrt(squares + EPSILON)).reshape(fields.shape)


def project(normed, proj_ref, fields_ref):
    for part in range(3):
        cut = slice(part * WIDTH, (part + 1) * WIDTH)
        fields = dot(proj_ref[:, cut], normed, TT)
        if part < 2:
            fields = unit_columns(fields)
        fields_ref[cut] = fields.astype(jnp.bfloat16)


def hold(held, values):
    for part in range(held.shape[0]):
        held[part] = values[:, part * LANES : (part + 1) * LANES].astype(jnp.float32)


def pick(held, start, count, step):
    return jnp.concatenate(
        [held[part, pl.ds(start, count, stride=step), :] for part in range(held.shape[0])], axis=1
    )


def head_rows(part, head):
    return slice(part * WIDTH + head * HEAD_DIM, part * WIDTH + (head + 1) * HEAD_DIM)


def attend(fields_ref, scale_ref, mixed_ref, scores_ref, weights_ref, totals_ref, groups, packed, length):
    span = groups * packed * length
    runs = fields_ref.shape[1] // span
    item_of = (lax.broadcasted_iota(jnp.int32, (1, span), 1) // length) % packed

    def rows(group, item):
        first = (group * packed + item) * length
        return slice(first, first + length)

    def score(at, head):
        cut = slice(at // HEADS * span, (at // HEADS + 1) * span)
        scores_ref[at] = dot(fields_ref[head_rows(1, head), cut], fields_ref[head_rows(0, head), cut], TN)

    def soften(at, head):
        factor = scale_ref[head : head + 1]
        for low in range(0, span, LANES):
            lanes = slice(low, low + LANES)
            mine = jnp.broadcast_to(item_of[:, lanes], (length, LANES))
            scores = []
            for group in range(groups):
                own = scores_ref[at, rows(group, 0), lanes]
                for item in range(1, packed):
                    own = jnp.where(mine == item, scores_ref[at, rows(group, item), lanes], own)
                scores.append(own)
            largest = functools.reduce(jnp.maximum, [jnp.max(own, axis=0, keepdims=True) for own in scores])
            powers = [jnp.exp2((own - largest) * factor) for own in scores]
            totals_ref[at, :, lanes] = 1.0 / sum(jnp.sum(part, axis=0, keepdims=True) for part in powers)
            for group in range(groups):
                for item in range(packed):
                    part = powers[group] if packed == 1 else jnp.where(mine == item, powers[group], 0.0)
                    weights_ref[at, rows(group, item), lanes] = part.astype(jnp.bfloat16)

    def mix(at, head):
        cut = slice(at // HEADS * span, (at // HEADS + 1) * span)
        mixed = dot(fields_ref[head_rows(2, head), cut], weights_ref[at]) * totals_ref[at]
        mixed_ref[head_rows(0, head), cut] = mixed.astype(jnp.bfloat16)

    count = runs * HEADS
    apart = max(1, AHEAD * 256 // span)
    for step in range(count + 2 * apart):
        for stage, late in ((score, 0), (soften, apart), (mix, 2 * apart)):
            at = step - late
            if 0 <= at < count:
                stage(at, at % HEADS)


GROUPS = [[0, 2, 4, 6], [5, 7, 3, 1]]
ORDER = {2: [1], 4: [2, 3, 1], 8: [2, 4, 6, 5, 7, 3, 1]}


def pack_kernel(tokens_ref, *refs):
    pieces, held = refs[:-1], refs[-1]
    frames, patches = tokens_ref.shape[0], tokens_ref.shape[1] // len(pieces)
    me = lax.axis_index("tm")
    for frame in range(frames):
        for part in range(held.shape[0]):
            held[part, frame] = tokens_ref[frame, :, part * LANES : (part + 1) * LANES].astype(jnp.float32)
    for index, piece in enumerate(pieces):
        start = pl.multiple_of((me ^ index) * patches, patches)
        for part in range(held.shape[0]):
            rows = [held[part, frame, pl.ds(start, patches)] for frame in range(frames)]
            piece[:, part * LANES : (part + 1) * LANES] = jnp.concatenate(rows, axis=0).astype(jnp.bfloat16)


def hold_pieces(held, pieces):
    start = 0
    for piece in pieces:
        for part in range(held.shape[0]):
            held[part, start : start + piece.shape[0]] = piece[:, part * LANES : (part + 1) * LANES].astype(jnp.float32)
        start += piece.shape[0]


def fields_kernel(patches, gain_ref, proj_ref, *refs):
    pieces, (fields_ref, held) = refs[:-2], refs[-2:]
    hold_pieces(held, pieces)
    tokens = [pick(held, patch, held.shape[1] // patches, patches) for patch in range(patches)]
    project(layer_norm(jnp.concatenate(tokens, axis=0), gain_ref[...]), proj_ref, fields_ref)


def time_kernel(groups, patches, scale_ref, gain_ref, proj_ref, out_ref, *refs):
    count, ready = sum(map(len, groups)), len(groups) - 1
    fields, pieces = refs[:ready], refs[ready : ready + count]
    stream_ref, held, result, merged, mixed, own_fields, *work = refs[ready + count :]
    fields = fields + (own_fields,)
    rows = held.shape[1] // len(groups)
    length = rows // patches
    packed = time_packed(len(groups) * length, patches)
    hold_pieces(held, pieces)
    turn = len(groups) == 2
    order = [patch ^ packed if turn else patch for patch in range(patches)]
    tokens = [pick(held, ready * rows + patch, length, patches) for patch in order]
    project(layer_norm(jnp.concatenate(tokens, axis=0), gain_ref[...]), proj_ref, own_fields)
    if turn:
        near = lax.broadcasted_iota(jnp.int32, (HEAD_DIM, LANES), 1) < packed * length
        for low in range(0, 3 * WIDTH, HEAD_DIM):
            cut = slice(low, low + HEAD_DIM)
            for tile in range(0, rows, LANES):
                first, second = (group[cut, tile : tile + LANES] for group in fields)
                merged[cut, 2 * tile : 2 * tile + LANES] = jnp.where(near, first, second)
                merged[cut, 2 * tile + LANES : 2 * tile + 2 * LANES] = jnp.where(near, second, first)
    else:
        merged = own_fields
    attend(merged, scale_ref, mixed, *work, len(groups), packed, length)
    half = max(patches // 2, packed)
    for patch in range(patches):
        if patch % half == 0:
            cut = slice(patch * len(groups) * length, (patch + half) * len(groups) * length)
            update = dot(mixed[:, cut], out_ref[...], TN)
        for group in range(len(groups)):
            unit = patch % half // packed
            slot = group ^ (unit % 2) if turn else group
            first = ((unit * len(groups) + slot) * packed + patch % packed) * length
            place = pl.ds(group * rows + patch, length, stride=patches)
            for part in range(result.shape[0]):
                lanes = slice(part * LANES, (part + 1) * LANES)
                result[part, place, :] = held[part, place, :] + update[first : first + length, lanes]
    me = lax.axis_index("tm")
    size = pieces[0].shape[0]
    for index, piece in enumerate(place for group in groups for place in group):
        start = 0 if count == 1 else pl.multiple_of((me ^ piece) * size, size)
        for part in range(result.shape[0]):
            values = result[part, index * size : (index + 1) * size]
            stream_ref[pl.ds(start, size), part * LANES : (part + 1) * LANES] = values.astype(jnp.bfloat16)


def space_kernel(
    frame, senders, sides, frames, scale_ref, gain_ref, proj_ref, out_ref, stream_ref, *refs
):
    pieces, (block, held, tokens, fields, mixed, *work) = refs[:sides], refs[sides:]
    side_patches = pieces[0].shape[0]
    piece = stream_ref.shape[0] // senders // frames
    if piece % 8:
        hold(held, stream_ref)
        for side in range(sides):
            rows = pick(held, (side * frames + frame) * piece, senders // sides, sides * frames)
            tokens[side * side_patches : (side + 1) * side_patches] = rows
    else:
        for sender in range(senders):
            block_rows = stream_ref[sender * frames * piece : (sender + 1) * frames * piece].astype(jnp.float32)
            place = sender % sides * side_patches + sender // sides * piece
            tokens[place : place + piece] = block_rows[frame * piece : (frame + 1) * piece]
    project(layer_norm(tokens[...], gain_ref[...]), proj_ref, fields)
    attend(fields, scale_ref, mixed, *work, 1, 1, sides * side_patches)
    stream = tokens[...] + dot(mixed[...], out_ref[...], TN)
    for side in range(sides):
        block[side] = stream[side * side_patches : (side + 1) * side_patches].astype(jnp.bfloat16)
    me = lax.axis_index("patch")
    for index in range(sides):
        pieces[index][...] = block[me ^ index]


def place_kernel(frame, frames, sides, *refs):
    pieces, whole, sems = refs[:sides], refs[-sides - 1], refs[-sides:]
    me = lax.axis_index("patch")
    copies = [
        pltpu.make_async_copy(piece, whole.at[(me ^ index) * frames + frame], sems[index])
        for index, piece in enumerate(pieces)
    ]
    for copy in copies:
        copy.start()
    for copy in copies:
        copy.wait()


def time_packed(frames, patches):
    return max(1, min(patches, LANES // frames))


def work_space(rows, span):
    return [
        pltpu.VMEM((3 * WIDTH, rows), jnp.bfloat16),
        pltpu.VMEM((WIDTH, rows), jnp.bfloat16),
    ], [
        pltpu.VMEM((rows // span * HEADS, span, span), jnp.float32),
        pltpu.VMEM((rows // span * HEADS, span, span), jnp.bfloat16),
        pltpu.VMEM((rows // span * HEADS, 1, span), jnp.float32),
    ]


def small_kernel(packed_ref, time_scale_ref, space_scale_ref, time_gain_ref, space_gain_ref):
    time_gain_ref[...] = packed_ref[:, :WIDTH]
    space_gain_ref[...] = packed_ref[:, WIDTH : 2 * WIDTH]
    for index, target in enumerate((time_scale_ref, space_scale_ref)):
        for head in range(HEADS):
            place = 2 * WIDTH + index * HEADS + head
            target[head : head + 1] = jnp.broadcast_to(packed_ref[:, place : place + 1] * LOG2_E, (1, LANES))


def small(time_scale, space_scale, time_gain, space_gain):
    whole = pl.BlockSpec(memory_space=pltpu.VMEM)
    shapes = [(HEADS, LANES), (HEADS, LANES), (1, WIDTH), (1, WIDTH)]
    return pl.pallas_call(
        small_kernel,
        out_shape=[jax.ShapeDtypeStruct(shape, jnp.float32) for shape in shapes],
        in_specs=[whole],
        out_specs=[whole] * 4,
        compiler_params=pltpu.CompilerParams(vmem_limit_bytes=1024 * 1024),
        cost_estimate=pl.CostEstimate(flops=10**10, bytes_accessed=10**5, transcendentals=0),
    )(jnp.concatenate([time_gain, space_gain, time_scale, space_scale])[None])


def call(kernel, out_shapes, scratch, scale, gain, proj, out, *rows):
    whole = pl.BlockSpec(memory_space=pltpu.VMEM)
    return pl.pallas_call(
        kernel,
        out_shape=[jax.ShapeDtypeStruct(shape, jnp.bfloat16) for shape in out_shapes],
        in_specs=[whole] * (4 + len(rows)),
        out_specs=[whole] * len(out_shapes),
        scratch_shapes=scratch,
        compiler_params=pltpu.CompilerParams(vmem_limit_bytes=VMEM_BYTES),
        cost_estimate=pl.CostEstimate(flops=10**10, bytes_accessed=7 * 10**6, transcendentals=10**6),
    )(scale, gain, proj, out, *rows)


def project_early(patches, gain, proj, pieces):
    whole = pl.BlockSpec(memory_space=pltpu.VMEM)
    rows = sum(piece.shape[0] for piece in pieces)
    return pl.pallas_call(
        functools.partial(fields_kernel, patches),
        out_shape=jax.ShapeDtypeStruct((3 * WIDTH, rows), jnp.bfloat16),
        in_specs=[whole] * (2 + len(pieces)),
        out_specs=whole,
        scratch_shapes=[pltpu.VMEM((WIDTH // LANES, rows, LANES), jnp.float32)],
        compiler_params=pltpu.CompilerParams(vmem_limit_bytes=VMEM_BYTES),
        cost_estimate=pl.CostEstimate(flops=5 * 10**9, bytes_accessed=7 * 10**6, transcendentals=10**6),
    )(gain, proj, *pieces)


def pack(tokens, peers):
    frames, patches, width = tokens.shape
    whole = pl.BlockSpec(memory_space=pltpu.VMEM)
    return pl.pallas_call(
        pack_kernel,
        out_shape=[jax.ShapeDtypeStruct((frames * patches // peers, width), tokens.dtype)] * peers,
        in_specs=[whole],
        out_specs=[whole] * peers,
        scratch_shapes=[pltpu.VMEM((width // LANES, frames, patches, LANES), jnp.float32)],
        compiler_params=pltpu.CompilerParams(vmem_limit_bytes=8 * 1024 * 1024),
    )(tokens)


def place(frame, frames, pieces, whole):
    anywhere = pl.BlockSpec(memory_space=pl.ANY)
    sides = len(pieces)
    others = [] if whole is None else [whole]
    return pl.pallas_call(
        functools.partial(place_kernel, frame, frames, sides),
        out_shape=jax.ShapeDtypeStruct((sides * frames,) + pieces[0].shape, pieces[0].dtype),
        in_specs=[anywhere] * (sides + len(others)),
        out_specs=anywhere,
        scratch_shapes=[pltpu.SemaphoreType.DMA] * sides,
        input_output_aliases={sides: 0} if others else {},
        compiler_params=pltpu.CompilerParams(vmem_limit_bytes=1024 * 1024),
        cost_estimate=pl.CostEstimate(flops=10**10, bytes_accessed=10**6, transcendentals=0),
    )(*pieces, *others)


def swap(pieces, axis):
    size = len(pieces)
    arrived = list(pieces)
    for index in ORDER[size]:
        arrived[index] = lax.ppermute(pieces[index], axis, [(i, i ^ index) for i in range(size)])
    return arrived


def per_device(
    tokens,
    time_gain,
    time_proj,
    time_out,
    time_scale,
    space_gain,
    space_proj,
    space_out,
    space_scale,
):
    frames, local_count, width = tokens.shape
    peers, sides = lax.axis_size("tm"), lax.axis_size("patch")
    rows = frames * local_count
    all_frames = frames * peers
    time_scale, space_scale, time_gain, space_gain = small(time_scale, space_scale, time_gain, space_gain)
    patches = local_count // peers
    fields = []
    if peers == 8:
        groups = GROUPS
        arrived = swap(pack(tokens, peers), "tm")
        arrived = [[arrived[index] for index in group] for group in groups]
        fields = [project_early(patches, time_gain, time_proj, pieces) for pieces in arrived[:-1]]
        arrived = sum(arrived, [])
    else:
        groups = [[0]]
        outgoing = jnp.swapaxes(tokens.reshape(frames, peers, patches, width), 0, 1).reshape(peers, rows // peers, width)
        arrived = [lax.all_to_all(outgoing, "tm", split_axis=0, concat_axis=0, tiled=True).reshape(rows, width)]
    held = pltpu.VMEM((width // LANES, rows, LANES), jnp.float32)
    space, work = work_space(rows, time_packed(all_frames, patches) * all_frames)
    stream = call(
        functools.partial(time_kernel, groups, patches),
        [(rows, width)],
        [held, held] + space + [pltpu.VMEM((3 * width, rows // len(groups)), jnp.bfloat16)] + work,
        time_scale, time_gain, time_proj, time_out, *fields, *arrived,
    )[0]
    senders = peers * sides
    stream = lax.all_to_all(
        stream.reshape(senders, rows // senders, width), ("tm", "patch"), split_axis=0, concat_axis=0, tiled=True
    ).reshape(rows, width)
    own_frames = frames // sides
    piece = (local_count, width)
    space, work = work_space(rows // own_frames, sides * local_count)
    tokens_held = pltpu.VMEM((sides * local_count, width), jnp.float32)
    block = None
    for frame in range(own_frames):
        blocks = call(
            functools.partial(space_kernel, frame, senders, sides, own_frames),
            [piece] * sides,
            [pltpu.VMEM((sides,) + piece, jnp.bfloat16), held, tokens_held] + space + work,
            space_scale, space_gain, space_proj, space_out, stream,
        )
        block = place(frame, own_frames, swap(blocks, "patch"), block)
    return block


def solution(mesh):
    in_specs = (P("tm", "patch", None), P(), P(), P(), P(), P(), P(), P(), P())
    out_specs = P("tm", "patch", None)
    return jax.shard_map(
        per_device, mesh=mesh, in_specs=in_specs, out_specs=out_specs, check_vma=False
    )
```

time: 70.5 us -> 69.2 us (0.982)
  local copies, waits for them, and re-layouts: 4.01 us -> 1.93 us
    broadcast_in_dim x4 -> x1, local copies, waits for them, and re-layouts: 2.86 us -> 0.01 us  [small(): jnp.concatenate([time_gain, space_gain, time_scale, space_scale])[None]]
    pallas_call x0 -> x1, Pallas kernels: none -> 1.51 us  [project_early(): pl.pallas_call(functools.partial(fields_kernel, patches), out_shape=jax.S...]
    pallas_call x3, Pallas kernels: 11.1 us -> 9.77 us  [call(): pl.pallas_call(kernel, out_shape=[jax.ShapeDtypeStruct(shape, jnp.bfloat1...]
    concatenate x0 -> x1, local copies, waits for them, and re-layouts: none -> 0.78 us  [small(): jnp.concatenate([time_gain, space_gain, time_scale, space_scale])[None]]
  transfers between devices with their start and end apart: 13 -> 13, of which waited for: 6 -> 6; matrix products, arithmetic and copies ran while one was open for 4% -> 1% of each run, Pallas kernels for 5% -> 8%
where the time goes in v5:
time: 69.2 us; the launch traced here: 69 us
  blocking collectives  24.7 us (36%)
  starting transfers between devices  16.7 us (24%)
  Pallas kernels  13.2 us (19%)
  waiting for transfers between devices  12.3 us (18%)
  local copies, waits for them, and re-layouts  1.93 us (3%)
    all_to_all x1, blocking collectives, per_device(): lax.all_to_all(stream.reshape(senders, rows // senders, width), ('tm', 'p...  24.7 us
    ppermute x13, starting transfers between devices, swap(): lax.ppermute(pieces[index], axis, [(i, i ^ index) for i in range(size)])  16.7 us
    ppermute x13, waiting for transfers between devices, swap(): lax.ppermute(pieces[index], axis, [(i, i ^ index) for i in range(size)])  12.3 us
    pallas_call x3, Pallas kernels, call(): pl.pallas_call(kernel, out_shape=[jax.ShapeDtypeStruct(shape, jnp.bfloat1...  9.77 us
    pallas_call x2, Pallas kernels, place(): pl.pallas_call(functools.partial(place_kernel, frame, frames, sides), out...  1.54 us
    pallas_call x1, Pallas kernels, project_early(): pl.pallas_call(functools.partial(fields_kernel, patches), out_shape=jax.S...  1.51 us
  transfers between devices with their start and end apart: 13, of which 6 were waited for; matrix products, arithmetic and copies ran while one was open for 1% of the time, Pallas kernels for 8%

profile of v5, /device:TPU:0, one launch (start us, length us, event | category | flops | bytes accessed | tf_op | source)
XLA Modules:
  0.0 69.0 jit_solution(18127863141368154623)
XLA Ops:
  0.0 1.1 %copy-done = bf16[8,64,768]{2,1,0:T(8,128)(2,1)S(1)} copy-done((bf16[8,64,768]{2,1,0:T(8,128)(2,1)S(1)}, bf16[8,64,768]{2,1,0:T(8,128)(2,1)}, u32[]{:S(2)}) %copy-start) | copy-done | bytes 786456
  1.1 0.3 shard_map.92
  1.4 3.1 %collective-permute-start = (bf16[64,768]{1,0:T(8,128)(2,1)S(1)}, bf16[64,768]{1,0:T(8,128)(2,1)S(1)}, u32[]{:S(2)}, u32[]{:S(2)}) collective-permute-start(bf16[64,768]{1,0:T(8,128)(2,1)S(1)} %get-tuple-element.30), channel_id=1, source_target_pairs={{0,8},{4,12},{8,0},{12,4},{16,24},{20,28},{24,16},{28,20},{1,9},{5... | collective-permute-start | bytes 294920 | tf_op jit(solution)/shard_map/ppermute | solution.py:325
  4.5 2.6 %collective-permute-start.1 = (bf16[64,768]{1,0:T(8,128)(2,1)S(1)}, bf16[64,768]{1,0:T(8,128)(2,1)S(1)}, u32[]{:S(2)}, u32[]{:S(2)}) collective-permute-start(bf16[64,768]{1,0:T(8,128)(2,1)S(1)} %get-tuple-element.31), channel_id=1, source_target_pairs={{0,16},{4,20},{8,24},{12,28},{16,0},{20,4},{24,8},{28,12},{1,17},{... | collective-permute-start | bytes 294920 | tf_op jit(solution)/shard_map/ppermute | solution.py:325
  7.1 0.0 collective-permute-start.2
  7.1 2.9 %collective-permute-start.3 = (bf16[64,768]{1,0:T(8,128)(2,1)S(1)}, bf16[64,768]{1,0:T(8,128)(2,1)S(1)}, u32[]{:S(2)}, u32[]{:S(2)}) collective-permute-start(bf16[64,768]{1,0:T(8,128)(2,1)S(1)} %get-tuple-element.33), channel_id=1, source_target_pairs={{0,20},{4,16},{8,28},{12,24},{16,4},{20,0},{24,12},{28,8},{1,21},{... | collective-permute-start | bytes 294920 | tf_op jit(solution)/shard_map/ppermute | solution.py:325
  10.0 1.9 %collective-permute-start.4 = (bf16[64,768]{1,0:T(8,128)(2,1)S(1)}, bf16[64,768]{1,0:T(8,128)(2,1)S(1)}, u32[]{:S(2)}, u32[]{:S(2)}) collective-permute-start(bf16[64,768]{1,0:T(8,128)(2,1)S(1)} %get-tuple-element.34), channel_id=1, source_target_pairs={{0,28},{4,24},{8,20},{12,16},{16,12},{20,8},{24,4},{28,0},{1,29},{... | collective-permute-start | bytes 294920 | tf_op jit(solution)/shard_map/ppermute | solution.py:325
  11.9 0.8 %concatenate.3 = f32[1560]{0:T(1024)S(1)} concatenate(f32[768]{0:T(1024)} %param.10, f32[768]{0:T(1024)} %param.14, f32[12]{0:T(128)} %param.13, f32[12]{0:T(128)} %param.17), dimensions={0} | concatenate | bytes 12480 | tf_op jit(solution)/shard_map/concatenate | solution.py:262
  12.7 0.1 shard_map.91
  12.8 0.8 %collective-permute-start.5 = (bf16[64,768]{1,0:T(8,128)(2,1)S(1)}, bf16[64,768]{1,0:T(8,128)(2,1)S(1)}, u32[]{:S(2)}, u32[]{:S(2)}) collective-permute-start(bf16[64,768]{1,0:T(8,128)(2,1)S(1)} %get-tuple-element.35), channel_id=1, source_target_pairs={{0,12},{4,8},{8,4},{12,0},{16,28},{20,24},{24,20},{28,16},{1,13},{... | collective-permute-start | bytes 294920 | tf_op jit(solution)/shard_map/ppermute | solution.py:325
  13.7 5.6 %collective-permute-done.1.refs_2_.refs_3_ = bf16[64,768]{1,0:T(8,128)(2,1)S(1)} collective-permute-done((bf16[64,768]{1,0:T(8,128)(2,1)S(1)}, bf16[64,768]{1,0:T(8,128)(2,1)S(1)}, u32[]{:S(2)}, u32[]{:S(2)}) %collective-permute-start.1) | collective-permute-done | bytes 98336 | tf_op jit(solution)/shard_map/ppermute | solution.py:325
  19.3 1.5 %collective-permute-start.6 = (bf16[64,768]{1,0:T(8,128)(2,1)S(1)}, bf16[64,768]{1,0:T(8,128)(2,1)S(1)}, u32[]{:S(2)}, u32[]{:S(2)}) collective-permute-start(bf16[64,768]{1,0:T(8,128)(2,1)S(1)} %get-tuple-element.36), channel_id=1, source_target_pairs={{0,4},{4,0},{8,12},{12,8},{16,20},{20,16},{24,28},{28,24},{1,5},{5... | collective-permute-start | bytes 294920 | tf_op jit(solution)/shard_map/ppermute | solution.py:325
  20.8 1.5 %shard_map.93.refs_0_ = bf16[2304,256]{1,0:T(8,128)(2,1)S(1)} custom-call(f32[1,768]{1,0:T(1,128)S(1)} %get-tuple-element.28.gain_ref, bf16[768,2304]{1,0:T(8,128)(2,1)S(1)} %copy-done.1, bf16[64,768]{1,0:T(8,128)(2,1)S(1)} %get-tuple-element.29.refs_0_.refs_1_, bf16[64,768]{1,0:T(8,128)(2,1)S(1)} %collective-permute-done.refs_1_.refs_2_, ...), custom_call_target="tpu_custom_call" | custom-call | flops 5000000000 | bytes 7000000 | tf_op jit(solution)/shard_map/pallas_call | solution.py:281
  22.3 2.0 %collective-permute-done.3.refs_5_ = bf16[64,768]{1,0:T(8,128)(2,1)S(1)} collective-permute-done((bf16[64,768]{1,0:T(8,128)(2,1)S(1)}, bf16[64,768]{1,0:T(8,128)(2,1)S(1)}, u32[]{:S(2)}, u32[]{:S(2)}) %collective-permute-start.3) | collective-permute-done | bytes 98336 | tf_op jit(solution)/shard_map/ppermute | solution.py:325
  24.4 0.0 collective-permute-done.4.refs_6_
  24.4 0.0 collective-permute-done.5.refs_7_
  24.4 0.3 collective-permute-done.6.refs_8_
  24.7 4.0 %shard_map.94 = bf16[512,768]{1,0:T(8,128)(2,1)S(1)} custom-call(f32[12,128]{1,0:T(8,128)S(1)} %get-tuple-element.27.scale_ref, f32[1,768]{1,0:T(1,128)S(1)} %get-tuple-element.28.gain_ref, bf16[768,2304]{1,0:T(8,128)(2,1)S(1)} %copy-done.1, bf16[768,768]{1,0:T(8,128)(2,1)S(1)} %copy-done.3, bf16[2304,256]{1,0:T(8,128)(2,1)S(1)} %shard_map.93.refs_0_, ...), custom_call_target="tpu_custom_call" | custom-call | flops 10000000000 | bytes 7000000 | tf_op jit(solution)/shard_map/pallas_call | solution.py:267
  28.7 0.0 copy-start.4
  28.7 24.7 %all_to_all.5 = bf16[32,16,768]{2,1,0:T(8,128)(2,1)S(1)} all-to-all(bf16[32,16,768]{2,1,0:T(8,128)(2,1)S(1)} %bitcast.4), channel_id=1, replica_groups=mesh['tm'=8,'patch'=4] {'tm','patch'}, dimensions={0} | all-to-all | bytes 1572864 | tf_op jit(solution)/shard_map/all_to_all | solution.py:366
  53.4 2.9 %shard_map.96 = (bf16[64,768]{1,0:T(8,128)(2,1)S(1)}, bf16[64,768]{1,0:T(8,128)(2,1)S(1)}, bf16[64,768]{1,0:T(8,128)(2,1)S(1)}, bf16[64,768]{1,0:T(8,128)(2,1)S(1)}) custom-call(f32[12,128]{1,0:T(8,128)S(1)} %get-tuple-element.25.scale_ref, f32[1,768]{1,0:T(1,128)S(1)} %get-tuple-element.26.gain_ref, bf16[768,2304]{1,0:T(8,128)(2,1)S(1)} %copy-done.2, ...), custom_call_target="tpu_custom_call" | custom-call | flops 10000000000 | bytes 7000000 | tf_op jit(solution)/shard_map/pallas_call | solution.py:267
  56.3 0.1 collective-permute-start.10
  56.3 1.6 %collective-permute-start.11 = (bf16[64,768]{1,0:T(8,128)(2,1)S(1)}, bf16[64,768]{1,0:T(8,128)(2,1)S(1)}, u32[]{:S(2)}, u32[]{:S(2)}) collective-permute-start(bf16[64,768]{1,0:T(8,128)(2,1)S(1)} %get-tuple-element.43), channel_id=1, source_target_pairs={{0,2},{1,3},{2,0},{3,1},{4,6},{5,7},{6,4},{7,5},{8,10},{9,11},{10,... | collective-permute-start | bytes 294920 | tf_op jit(solution)/shard_map/ppermute | solution.py:325
  58.0 0.2 collective-permute-start.12
  58.2 2.9 %shard_map.95 = (bf16[64,768]{1,0:T(8,128)(2,1)S(1)}, bf16[64,768]{1,0:T(8,128)(2,1)S(1)}, bf16[64,768]{1,0:T(8,128)(2,1)S(1)}, bf16[64,768]{1,0:T(8,128)(2,1)S(1)}) custom-call(f32[12,128]{1,0:T(8,128)S(1)} %get-tuple-element.25.scale_ref, f32[1,768]{1,0:T(1,128)S(1)} %get-tuple-element.26.gain_ref, bf16[768,2304]{1,0:T(8,128)(2,1)S(1)} %copy-done.2, ...), custom_call_target="tpu_custom_call" | custom-call | flops 10000000000 | bytes 7000000 | tf_op jit(solution)/shard_map/pallas_call | solution.py:267
  61.1 0.4 collective-permute-start.7
  61.5 1.6 %collective-permute-start.8 = (bf16[64,768]{1,0:T(8,128)(2,1)S(1)}, bf16[64,768]{1,0:T(8,128)(2,1)S(1)}, u32[]{:S(2)}, u32[]{:S(2)}) collective-permute-start(bf16[64,768]{1,0:T(8,128)(2,1)S(1)} %get-tuple-element.39), channel_id=1, source_target_pairs={{0,2},{1,3},{2,0},{3,1},{4,6},{5,7},{6,4},{7,5},{8,10},{9,11},{10,... | collective-permute-start | bytes 294920 | tf_op jit(solution)/shard_map/ppermute | solution.py:325
  63.1 0.1 collective-permute-done.12.refs_3_
  63.2 0.8 %shard_map.97.refs_4_ = bf16[8,64,768]{2,1,0:T(8,128)(2,1)} custom-call(bf16[64,768]{1,0:T(8,128)(2,1)S(1)} %get-tuple-element.41.refs_0_, bf16[64,768]{1,0:T(8,128)(2,1)S(1)} %collective-permute-done.10.refs_1_, bf16[64,768]{1,0:T(8,128)(2,1)S(1)} %collective-permute-done.11.refs_2_, bf16[64,768]{1,0:T(8,128)(2,1)S(1)} %collective-permute-done.12.refs_3_), custom_call_target="tpu_custom_call" | custom-call | flops 10000000000 | bytes 1000000 | tf_op jit(solution)/shard_map/pallas_call | solution.py:309
  64.0 2.7 %collective-permute-done.8.refs_2_ = bf16[64,768]{1,0:T(8,128)(2,1)S(1)} collective-permute-done((bf16[64,768]{1,0:T(8,128)(2,1)S(1)}, bf16[64,768]{1,0:T(8,128)(2,1)S(1)}, u32[]{:S(2)}, u32[]{:S(2)}) %collective-permute-start.8) | collective-permute-done | bytes 98336 | tf_op jit(solution)/shard_map/ppermute | solution.py:325
  66.7 1.5 %collective-permute-done.9.refs_3_ = bf16[64,768]{1,0:T(8,128)(2,1)S(1)} collective-permute-done((bf16[64,768]{1,0:T(8,128)(2,1)S(1)}, bf16[64,768]{1,0:T(8,128)(2,1)S(1)}, u32[]{:S(2)}, u32[]{:S(2)}) %collective-permute-start.9) | collective-permute-done | bytes 98336 | tf_op jit(solution)/shard_map/ppermute | solution.py:325
  68.2 0.8 %shard_map.98 = bf16[8,64,768]{2,1,0:T(8,128)(2,1)} custom-call(bf16[64,768]{1,0:T(8,128)(2,1)S(1)} %get-tuple-element.37.refs_0_, bf16[64,768]{1,0:T(8,128)(2,1)S(1)} %collective-permute-done.7.refs_1_, bf16[64,768]{1,0:T(8,128)(2,1)S(1)} %collective-permute-done.8.refs_2_, ...), custom_call_target="tpu_custom_call", output_to_operand_aliasing={{}: (4, {})} | custom-call | flops 10000000000 | bytes 1000000 | tf_op jit(solution)/shard_map/pallas_call | solution.py:309
  (15 shorter events, 0.0 us)
Async XLA Ops:
  0.0 1.1 %copy-start = (bf16[8,64,768]{2,1,0:T(8,128)(2,1)S(1)}, bf16[8,64,768]{2,1,0:T(8,128)(2,1)}, u32[]{:S(2)}) copy-start(bf16[8,64,768]{2,1,0:T(8,128)(2,1)} %tokens_ref.1) | copy-start | bytes 2359300
  1.4 11.4 %collective-permute-start = (bf16[64,768]{1,0:T(8,128)(2,1)S(1)}, bf16[64,768]{1,0:T(8,128)(2,1)S(1)}, u32[]{:S(2)}, u32[]{:S(2)}) collective-permute-start(bf16[64,768]{1,0:T(8,128)(2,1)S(1)} %get-tuple-element.30), channel_id=1, source_target_pairs={{0,8},{4,12},{8,0},{12,4},{16,24},{20,28},{24,16},{28,20},{1,9},{5... | collective-permute-start | bytes 294920 | tf_op jit(solution)/shard_map/ppermute | solution.py:325
  4.5 14.7 %collective-permute-start.1 = (bf16[64,768]{1,0:T(8,128)(2,1)S(1)}, bf16[64,768]{1,0:T(8,128)(2,1)S(1)}, u32[]{:S(2)}, u32[]{:S(2)}) collective-permute-start(bf16[64,768]{1,0:T(8,128)(2,1)S(1)} %get-tuple-element.31), channel_id=1, source_target_pairs={{0,16},{4,20},{8,24},{12,28},{16,0},{20,4},{24,8},{28,12},{1,17},{... | collective-permute-start | bytes 294920 | tf_op jit(solution)/shard_map/ppermute | solution.py:325
  7.1 13.7 %collective-permute-start.2 = (bf16[64,768]{1,0:T(8,128)(2,1)S(1)}, bf16[64,768]{1,0:T(8,128)(2,1)S(1)}, u32[]{:S(2)}, u32[]{:S(2)}) collective-permute-start(bf16[64,768]{1,0:T(8,128)(2,1)S(1)} %get-tuple-element.32), channel_id=1, source_target_pairs={{0,24},{4,28},{8,16},{12,20},{16,8},{20,12},{24,0},{28,4},{1,25},{... | collective-permute-start | bytes 294920 | tf_op jit(solution)/shard_map/ppermute | solution.py:325
  7.1 17.2 %collective-permute-start.3 = (bf16[64,768]{1,0:T(8,128)(2,1)S(1)}, bf16[64,768]{1,0:T(8,128)(2,1)S(1)}, u32[]{:S(2)}, u32[]{:S(2)}) collective-permute-start(bf16[64,768]{1,0:T(8,128)(2,1)S(1)} %get-tuple-element.33), channel_id=1, source_target_pairs={{0,20},{4,16},{8,28},{12,24},{16,4},{20,0},{24,12},{28,8},{1,21},{... | collective-permute-start | bytes 294920 | tf_op jit(solution)/shard_map/ppermute | solution.py:325
  10.0 14.4 %collective-permute-start.4 = (bf16[64,768]{1,0:T(8,128)(2,1)S(1)}, bf16[64,768]{1,0:T(8,128)(2,1)S(1)}, u32[]{:S(2)}, u32[]{:S(2)}) collective-permute-start(bf16[64,768]{1,0:T(8,128)(2,1)S(1)} %get-tuple-element.34), channel_id=1, source_target_pairs={{0,28},{4,24},{8,20},{12,16},{16,12},{20,8},{24,4},{28,0},{1,29},{... | collective-permute-start | bytes 294920 | tf_op jit(solution)/shard_map/ppermute | solution.py:325
  12.7 8.1 %copy-start.1 = (bf16[768,2304]{1,0:T(8,128)(2,1)S(1)}, bf16[768,2304]{1,0:T(8,128)(2,1)}, u32[]{:S(2)}) copy-start(bf16[768,2304]{1,0:T(8,128)(2,1)} %proj_ref.5) | copy-start | bytes 10616836
  12.8 11.5 %collective-permute-start.5 = (bf16[64,768]{1,0:T(8,128)(2,1)S(1)}, bf16[64,768]{1,0:T(8,128)(2,1)S(1)}, u32[]{:S(2)}, u32[]{:S(2)}) collective-permute-start(bf16[64,768]{1,0:T(8,128)(2,1)S(1)} %get-tuple-element.35), channel_id=1, source_target_pairs={{0,12},{4,8},{8,4},{12,0},{16,28},{20,24},{24,20},{28,16},{1,13},{... | collective-permute-start | bytes 294920 | tf_op jit(solution)/shard_map/ppermute | solution.py:325
  19.3 5.4 %collective-permute-start.6 = (bf16[64,768]{1,0:T(8,128)(2,1)S(1)}, bf16[64,768]{1,0:T(8,128)(2,1)S(1)}, u32[]{:S(2)}, u32[]{:S(2)}) collective-permute-start(bf16[64,768]{1,0:T(8,128)(2,1)S(1)} %get-tuple-element.36), channel_id=1, source_target_pairs={{0,4},{4,0},{8,12},{12,8},{16,20},{20,16},{24,28},{28,24},{1,5},{5... | collective-permute-start | bytes 294920 | tf_op jit(solution)/shard_map/ppermute | solution.py:325
  20.8 3.9 %copy-start.3 = (bf16[768,768]{1,0:T(8,128)(2,1)S(1)}, bf16[768,768]{1,0:T(8,128)(2,1)}, u32[]{:S(2)}) copy-start(bf16[768,768]{1,0:T(8,128)(2,1)} %out_ref.3) | copy-start | bytes 3538948
  24.7 28.7 %copy-start.2 = (bf16[768,2304]{1,0:T(8,128)(2,1)S(1)}, bf16[768,2304]{1,0:T(8,128)(2,1)}, u32[]{:S(2)}) copy-start(bf16[768,2304]{1,0:T(8,128)(2,1)} %proj_ref.7) | copy-start | bytes 10616836
  28.7 24.7 %copy-start.4 = (bf16[768,768]{1,0:T(8,128)(2,1)S(1)}, bf16[768,768]{1,0:T(8,128)(2,1)}, u32[]{:S(2)}) copy-start(bf16[768,768]{1,0:T(8,128)(2,1)} %out_ref.5) | copy-start | bytes 3538948
  56.3 6.8 %collective-permute-start.10 = (bf16[64,768]{1,0:T(8,128)(2,1)S(1)}, bf16[64,768]{1,0:T(8,128)(2,1)S(1)}, u32[]{:S(2)}, u32[]{:S(2)}) collective-permute-start(bf16[64,768]{1,0:T(8,128)(2,1)S(1)} %get-tuple-element.42), channel_id=1, source_target_pairs={{0,1},{1,0},{2,3},{3,2},{4,5},{5,4},{6,7},{7,6},{8,9},{9,8},{10,11... | collective-permute-start | bytes 294920 | tf_op jit(solution)/shard_map/ppermute | solution.py:325
  56.3 6.7 %collective-permute-start.11 = (bf16[64,768]{1,0:T(8,128)(2,1)S(1)}, bf16[64,768]{1,0:T(8,128)(2,1)S(1)}, u32[]{:S(2)}, u32[]{:S(2)}) collective-permute-start(bf16[64,768]{1,0:T(8,128)(2,1)S(1)} %get-tuple-element.43), channel_id=1, source_target_pairs={{0,2},{1,3},{2,0},{3,1},{4,6},{5,7},{6,4},{7,5},{8,10},{9,11},{10,... | collective-permute-start | bytes 294920 | tf_op jit(solution)/shard_map/ppermute | solution.py:325
  58.0 5.2 %collective-permute-start.12 = (bf16[64,768]{1,0:T(8,128)(2,1)S(1)}, bf16[64,768]{1,0:T(8,128)(2,1)S(1)}, u32[]{:S(2)}, u32[]{:S(2)}) collective-permute-start(bf16[64,768]{1,0:T(8,128)(2,1)S(1)} %get-tuple-element.44), channel_id=1, source_target_pairs={{0,3},{1,2},{2,1},{3,0},{4,7},{5,6},{6,5},{7,4},{8,11},{9,10},{10,... | collective-permute-start | bytes 294920 | tf_op jit(solution)/shard_map/ppermute | solution.py:325
  61.1 2.9 %collective-permute-start.7 = (bf16[64,768]{1,0:T(8,128)(2,1)S(1)}, bf16[64,768]{1,0:T(8,128)(2,1)S(1)}, u32[]{:S(2)}, u32[]{:S(2)}) collective-permute-start(bf16[64,768]{1,0:T(8,128)(2,1)S(1)} %get-tuple-element.38), channel_id=1, source_target_pairs={{0,1},{1,0},{2,3},{3,2},{4,5},{5,4},{6,7},{7,6},{8,9},{9,8},{10,11... | collective-permute-start | bytes 294920 | tf_op jit(solution)/shard_map/ppermute | solution.py:325
  61.5 5.2 %collective-permute-start.8 = (bf16[64,768]{1,0:T(8,128)(2,1)S(1)}, bf16[64,768]{1,0:T(8,128)(2,1)S(1)}, u32[]{:S(2)}, u32[]{:S(2)}) collective-permute-start(bf16[64,768]{1,0:T(8,128)(2,1)S(1)} %get-tuple-element.39), channel_id=1, source_target_pairs={{0,2},{1,3},{2,0},{3,1},{4,6},{5,7},{6,4},{7,5},{8,10},{9,11},{10,... | collective-permute-start | bytes 294920 | tf_op jit(solution)/shard_map/ppermute | solution.py:325
  63.1 5.1 %collective-permute-start.9 = (bf16[64,768]{1,0:T(8,128)(2,1)S(1)}, bf16[64,768]{1,0:T(8,128)(2,1)S(1)}, u32[]{:S(2)}, u32[]{:S(2)}) collective-permute-start(bf16[64,768]{1,0:T(8,128)(2,1)S(1)} %get-tuple-element.40), channel_id=1, source_target_pairs={{0,3},{1,2},{2,1},{3,0},{4,7},{5,6},{6,5},{7,4},{8,11},{9,10},{10,... | collective-permute-start | bytes 294920 | tf_op jit(solution)/shard_map/ppermute | solution.py:325

commit v6 on v5

--- a/solution.py
+++ b/solution.py
@@ -107,8 +107,22 @@
                 stage(at, at % HEADS)
 
 
-GROUPS = [[0, 2, 4, 6], [5, 7, 3, 1]]
-ORDER = {2: [1], 4: [2, 3, 1], 8: [2, 4, 6, 5, 7, 3, 1]}
+def attend_lanes(fields_ref, scale_ref, mixed_ref, scores_ref, weights_ref, totals_ref, lanes):
+    for head in range(HEADS):
+        scores_ref[head] = dot(fields_ref[head_rows(1, head)], fields_ref[head_rows(0, head), lanes], TN)
+    for head in range(HEADS):
+        scores = scores_ref[head]
+        factor = jnp.broadcast_to(scale_ref[head : head + 1, :1], (1, scores.shape[1]))
+        powers = jnp.exp2((scores - jnp.max(scores, axis=0, keepdims=True)) * factor)
+        totals_ref[head] = 1.0 / jnp.sum(powers, axis=0, keepdims=True)
+        weights_ref[head] = powers.astype(jnp.bfloat16)
+    for head in range(HEADS):
+        mixed = dot(fields_ref[head_rows(2, head)], weights_ref[head]) * totals_ref[head]
+        mixed_ref[head_rows(0, head)] = mixed.astype(jnp.bfloat16)
+
+
+GROUPS = [[0, 2, 4, 5], [6, 7, 3, 1]]
+ORDER = [2, 4, 5, 6, 7, 3, 1]
 
 
 def pack_kernel(tokens_ref, *refs):
@@ -189,35 +203,50 @@
 def space_kernel(
     frame, senders, sides, frames, scale_ref, gain_ref, proj_ref, out_ref, stream_ref, *refs
 ):
-    pieces, (block, held, tokens, fields, mixed, *work) = refs[:sides], refs[sides:]
+    pieces, (fields, kept, held, tokens, mixed, *work) = refs[: sides // 2], refs[sides // 2 :]
     side_patches = pieces[0].shape[0]
     piece = stream_ref.shape[0] // senders // frames
+    me = lax.axis_index("patch")
     if piece % 8:
         hold(held, stream_ref)
-        for side in range(sides):
-            rows = pick(held, (side * frames + frame) * piece, senders // sides, sides * frames)
-            tokens[side * side_patches : (side + 1) * side_patches] = rows
-    else:
-        for sender in range(senders):
-            block_rows = stream_ref[sender * frames * piece : (sender + 1) * frames * piece].astype(jnp.float32)
-            place = sender % sides * side_patches + sender // sides * piece
-            tokens[place : place + piece] = block_rows[frame * piece : (frame + 1) * piece]
+    for index in range(sides):
+        first = index * side_patches
+        if piece % 8:
+            rows = pick(held, ((me ^ index) * frames + frame) * piece, senders // sides, sides * frames)
+            tokens[first : first + side_patches] = rows
+        else:
+            for sender in range(senders // sides):
+                start = pl.multiple_of((sender * sides + (me ^ index)) * frames * piece, frames * piece)
+                rows = stream_ref[pl.ds(start, frames * piece), :].astype(jnp.float32)
+                place = first + sender * piece
+                tokens[place : place + piece] = rows[frame * piece : (frame + 1) * piece]
+    half = sides // 2 * side_patches
     project(layer_norm(tokens[...], gain_ref[...]), proj_ref, fields)
-    attend(fields, scale_ref, mixed, *work, 1, 1, sides * side_patches)
-    stream = tokens[...] + dot(mixed[...], out_ref[...], TN)
-    for side in range(sides):
-        block[side] = stream[side * side_patches : (side + 1) * side_patches].astype(jnp.bfloat16)
-    me = lax.axis_index("patch")
-    for index in range(sides):
-        pieces[index][...] = block[me ^ index]
-
-
-def place_kernel(frame, frames, sides, *refs):
-    pieces, whole, sems = refs[:sides], refs[-sides - 1], refs[-sides:]
+    attend_lanes(fields, scale_ref, mixed, *work, slice(half, 2 * half))
+    stream = tokens[half:] + dot(mixed[...], out_ref[...], TN)
+    for index, target in enumerate(pieces):
+        target[...] = stream[index * side_patches : (index + 1) * side_patches].astype(jnp.bfloat16)
+    kept[...] = tokens[:half]
+
+
+def near_kernel(frames, scale_ref, out_ref, *refs):
+    pieces, (mixed, *work) = refs[2 * frames : -4], refs[-4:]
+    side_patches = pieces[0].shape[1]
+    for frame in range(frames):
+        fields, kept = refs[2 * frame : 2 * frame + 2]
+        attend_lanes(fields, scale_ref, mixed, *work, slice(0, kept.shape[0]))
+        stream = kept[...] + dot(mixed[...], out_ref[...], TN)
+        for index, target in enumerate(pieces):
+            target[frame] = stream[index * side_patches : (index + 1) * side_patches].astype(jnp.bfloat16)
+
+
+def place_kernel(places, *refs):
+    count = len(places)
+    pieces, whole, sems = refs[:count], refs[-count - 1], refs[-count:]
     me = lax.axis_index("patch")
     copies = [
-        pltpu.make_async_copy(piece, whole.at[(me ^ index) * frames + frame], sems[index])
-        for index, piece in enumerate(pieces)
+        pltpu.make_async_copy(piece, whole.at[pl.ds((me ^ index) * frames + first, piece.shape[0])], sem)
+        for piece, (index, first, frames), sem in zip(pieces, places, sems)
     ]
     for copy in copies:
         copy.start()
@@ -262,17 +291,17 @@
     )(jnp.concatenate([time_gain, space_gain, time_scale, space_scale])[None])
 
 
-def call(kernel, out_shapes, scratch, scale, gain, proj, out, *rows):
+def call(kernel, out_shapes, scratch, flops, *rows):
     whole = pl.BlockSpec(memory_space=pltpu.VMEM)
     return pl.pallas_call(
         kernel,
-        out_shape=[jax.ShapeDtypeStruct(shape, jnp.bfloat16) for shape in out_shapes],
-        in_specs=[whole] * (4 + len(rows)),
+        out_shape=[jax.ShapeDtypeStruct(*shape) for shape in out_shapes],
+        in_specs=[whole] * len(rows),
         out_specs=[whole] * len(out_shapes),
         scratch_shapes=scratch,
         compiler_params=pltpu.CompilerParams(vmem_limit_bytes=VMEM_BYTES),
-        cost_estimate=pl.CostEstimate(flops=10**10, bytes_accessed=7 * 10**6, transcendentals=10**6),
-    )(scale, gain, proj, out, *rows)
+        cost_estimate=pl.CostEstimate(flops=flops, bytes_accessed=flops // 1000, transcendentals=0),
+    )(*rows)
 
 
 def project_early(patches, gain, proj, pieces):
@@ -302,27 +331,31 @@
     )(tokens)
 
 
-def place(frame, frames, pieces, whole):
+def place(places, pieces, whole, shape):
     anywhere = pl.BlockSpec(memory_space=pl.ANY)
-    sides = len(pieces)
+    count = len(pieces)
     others = [] if whole is None else [whole]
     return pl.pallas_call(
-        functools.partial(place_kernel, frame, frames, sides),
-        out_shape=jax.ShapeDtypeStruct((sides * frames,) + pieces[0].shape, pieces[0].dtype),
-        in_specs=[anywhere] * (sides + len(others)),
+        functools.partial(place_kernel, places),
+        out_shape=jax.ShapeDtypeStruct(shape, jnp.bfloat16),
+        in_specs=[anywhere] * (count + len(others)),
         out_specs=anywhere,
-        scratch_shapes=[pltpu.SemaphoreType.DMA] * sides,
-        input_output_aliases={sides: 0} if others else {},
+        scratch_shapes=[pltpu.SemaphoreType.DMA] * count,
+        input_output_aliases={count: 0} if others else {},
         compiler_params=pltpu.CompilerParams(vmem_limit_bytes=1024 * 1024),
         cost_estimate=pl.CostEstimate(flops=10**10, bytes_accessed=10**6, transcendentals=0),
     )(*pieces, *others)
 
 
+def exchange(piece, axis, index):
+    size = lax.axis_size(axis)
+    return lax.ppermute(piece, axis, [(i, i ^ index) for i in range(size)])
+
+
 def swap(pieces, axis):
-    size = len(pieces)
     arrived = list(pieces)
-    for index in ORDER[size]:
-        arrived[index] = lax.ppermute(pieces[index], axis, [(i, i ^ index) for i in range(size)])
+    for index in ORDER:
+        arrived[index] = exchange(pieces[index], axis, index)
     return arrived
 
 
@@ -358,27 +391,50 @@
     space, work = work_space(rows, time_packed(all_frames, patches) * all_frames)
     stream = call(
         functools.partial(time_kernel, groups, patches),
-        [(rows, width)],
+        [((rows, width), jnp.bfloat16)],
         [held, held] + space + [pltpu.VMEM((3 * width, rows // len(groups)), jnp.bfloat16)] + work,
+        10**10,
         time_scale, time_gain, time_proj, time_out, *fields, *arrived,
     )[0]
     senders = peers * sides
     stream = lax.all_to_all(
         stream.reshape(senders, rows // senders, width), ("tm", "patch"), split_axis=0, concat_axis=0, tiled=True
     ).reshape(rows, width)
-    own_frames = frames // sides
+    own_frames, columns, half = frames // sides, sides * local_count, sides // 2
     piece = (local_count, width)
-    space, work = work_space(rows // own_frames, sides * local_count)
-    tokens_held = pltpu.VMEM((sides * local_count, width), jnp.float32)
+    near_rows = half * local_count
+    work = [
+        pltpu.VMEM((width, near_rows), jnp.bfloat16),
+        pltpu.VMEM((HEADS, columns, near_rows), jnp.float32),
+        pltpu.VMEM((HEADS, columns, near_rows), jnp.bfloat16),
+        pltpu.VMEM((HEADS, 1, near_rows), jnp.float32),
+    ]
+    far, kept = [], []
+    for frame in range(own_frames):
+        *pieces, fields, tokens_near = call(
+            functools.partial(space_kernel, frame, senders, sides, own_frames),
+            [(piece, jnp.bfloat16)] * half
+            + [((3 * width, columns), jnp.bfloat16), ((near_rows, width), jnp.float32)],
+            [held, pltpu.VMEM((columns, width), jnp.float32)] + work,
+            10**10,
+            space_scale, space_gain, space_proj, space_out, stream,
+        )
+        far.append([exchange(piece[None], "patch", half + index) for index, piece in enumerate(pieces)])
+        kept += [fields, tokens_near]
+    near = call(
+        functools.partial(near_kernel, own_frames),
+        [((own_frames,) + piece, jnp.bfloat16)] * half,
+        work,
+        10**6,
+        space_scale, space_out, *kept,
+    )
+    near = [exchange(piece, "patch", index) if index else piece for index, piece in enumerate(near)]
     block = None
     for frame in range(own_frames):
-        blocks = call(
-            functools.partial(space_kernel, frame, senders, sides, own_frames),
-            [piece] * sides,
-            [pltpu.VMEM((sides,) + piece, jnp.bfloat16), held, tokens_held] + space + work,
-            space_scale, space_gain, space_proj, space_out, stream,
-        )
-        block = place(frame, own_frames, swap(blocks, "patch"), block)
+        places, pieces = [(half + index, frame, own_frames) for index in range(half)], far[frame]
+        if frame == own_frames - 1:
+            places, pieces = places + [(index, 0, own_frames) for index in range(half)], pieces + near
+        block = place(places, pieces, block, tokens.shape)
     return block
 
 

time: 69.2 us -> 67.8 us (0.980)
  waiting for transfers between devices: 12.3 us -> 8.9 us
  Pallas kernels: 13.2 us -> 14.2 us
    ppermute x13 -> x12, waiting for transfers between devices: 12.3 us -> 8.9 us  [exchange(): return lax.ppermute(piece, axis, [(i, i ^ index) for i in range(size)])]
    pallas_call x5 -> x6, Pallas kernels: 11.3 us -> 12.3 us  [the longest x4 10.8 us: call(): pl.pallas_call(kernel, out_shape=[jax.ShapeDtypeStruct(*shape) for shape...]
    ppermute x13 -> x12, starting transfers between devices: 16.7 us -> 17.2 us  [exchange(): return lax.ppermute(piece, axis, [(i, i ^ index) for i in range(size)])]
  transfers between devices with their start and end apart: 13 -> 12, of which waited for: 6 -> 5; matrix products, arithmetic and copies ran while one was open for 1% -> 1% of each run, Pallas kernels for 8% -> 10%
where the time goes in v6:
time: 67.8 us; the launch traced here: 67.6 us
  blocking collectives  25.1 us (37%)
  starting transfers between devices  17.2 us (25%)
  Pallas kernels  14.2 us (21%)
  waiting for transfers between devices  8.9 us (13%)
  local copies, waits for them, and re-layouts  1.93 us (3%)
    all_to_all x1, blocking collectives, per_device(): lax.all_to_all(stream.reshape(senders, rows // senders, width), ('tm', 'p...  25.1 us
    ppermute x12, starting transfers between devices, exchange(): return lax.ppermute(piece, axis, [(i, i ^ index) for i in range(size)])  17.2 us
    pallas_call x4, Pallas kernels, call(): pl.pallas_call(kernel, out_shape=[jax.ShapeDtypeStruct(*shape) for shape...  10.8 us
    ppermute x12, waiting for transfers between devices, exchange(): return lax.ppermute(piece, axis, [(i, i ^ index) for i in range(size)])  8.9 us
    pallas_call x2, Pallas kernels, place(): pl.pallas_call(functools.partial(place_kernel, places), out_shape=jax.Sha...  1.53 us
    pallas_call x1, Pallas kernels, project_early(): pl.pallas_call(functools.partial(fields_kernel, patches), out_shape=jax.S...  1.5 us
  transfers between devices with their start and end apart: 12, of which 5 were waited for; matrix products, arithmetic and copies ran while one was open for 1% of the time, Pallas kernels for 10%

profile of v6, /device:TPU:0, one launch (start us, length us, event | category | flops | bytes accessed | tf_op | source)
XLA Modules:
  0.0 67.6 jit_solution(2971073583738363866)
XLA Ops:
  0.0 1.1 %copy-done.1 = bf16[8,64,768]{2,1,0:T(8,128)(2,1)S(1)} copy-done((bf16[8,64,768]{2,1,0:T(8,128)(2,1)S(1)}, bf16[8,64,768]{2,1,0:T(8,128)(2,1)}, u32[]{:S(2)}) %copy-start.1) | copy-done | bytes 786456
  1.1 0.3 shard_map.92
  1.4 3.1 %collective-permute-start = (bf16[64,768]{1,0:T(8,128)(2,1)S(1)}, bf16[64,768]{1,0:T(8,128)(2,1)S(1)}, u32[]{:S(2)}, u32[]{:S(2)}) collective-permute-start(bf16[64,768]{1,0:T(8,128)(2,1)S(1)} %get-tuple-element.32), channel_id=1, source_target_pairs={{0,8},{4,12},{8,0},{12,4},{16,24},{20,28},{24,16},{28,20},{1,9},{5... | collective-permute-start | bytes 294920 | tf_op jit(solution)/shard_map/ppermute | solution.py:352
  4.5 2.6 %collective-permute-start.1 = (bf16[64,768]{1,0:T(8,128)(2,1)S(1)}, bf16[64,768]{1,0:T(8,128)(2,1)S(1)}, u32[]{:S(2)}, u32[]{:S(2)}) collective-permute-start(bf16[64,768]{1,0:T(8,128)(2,1)S(1)} %get-tuple-element.33), channel_id=1, source_target_pairs={{0,16},{4,20},{8,24},{12,28},{16,0},{20,4},{24,8},{28,12},{1,17},{... | collective-permute-start | bytes 294920 | tf_op jit(solution)/shard_map/ppermute | solution.py:352
  7.1 1.3 %collective-permute-start.2 = (bf16[64,768]{1,0:T(8,128)(2,1)S(1)}, bf16[64,768]{1,0:T(8,128)(2,1)S(1)}, u32[]{:S(2)}, u32[]{:S(2)}) collective-permute-start(bf16[64,768]{1,0:T(8,128)(2,1)S(1)} %get-tuple-element.34), channel_id=1, source_target_pairs={{0,20},{4,16},{8,28},{12,24},{16,4},{20,0},{24,12},{28,8},{1,21},{... | collective-permute-start | bytes 294920 | tf_op jit(solution)/shard_map/ppermute | solution.py:352
  8.4 2.5 %collective-permute-start.3 = (bf16[64,768]{1,0:T(8,128)(2,1)S(1)}, bf16[64,768]{1,0:T(8,128)(2,1)S(1)}, u32[]{:S(2)}, u32[]{:S(2)}) collective-permute-start(bf16[64,768]{1,0:T(8,128)(2,1)S(1)} %get-tuple-element.35), channel_id=1, source_target_pairs={{0,24},{4,28},{8,16},{12,20},{16,8},{20,12},{24,0},{28,4},{1,25},{... | collective-permute-start | bytes 294920 | tf_op jit(solution)/shard_map/ppermute | solution.py:352
  10.9 1.3 %collective-permute-start.4 = (bf16[64,768]{1,0:T(8,128)(2,1)S(1)}, bf16[64,768]{1,0:T(8,128)(2,1)S(1)}, u32[]{:S(2)}, u32[]{:S(2)}) collective-permute-start(bf16[64,768]{1,0:T(8,128)(2,1)S(1)} %get-tuple-element.36), channel_id=1, source_target_pairs={{0,28},{4,24},{8,20},{12,16},{16,12},{20,8},{24,4},{28,0},{1,29},{... | collective-permute-start | bytes 294920 | tf_op jit(solution)/shard_map/ppermute | solution.py:352
  12.2 0.8 %concatenate.3 = f32[1560]{0:T(1024)S(1)} concatenate(f32[768]{0:T(1024)} %param.10, f32[768]{0:T(1024)} %param.14, f32[12]{0:T(128)} %param.13, f32[12]{0:T(128)} %param.17), dimensions={0} | concatenate | bytes 12480 | tf_op jit(solution)/shard_map/concatenate | solution.py:291
  13.0 0.1 shard_map.91
  13.1 0.0 collective-permute-done.refs_1_.refs_2_
  13.1 0.4 collective-permute-start.5
  13.4 4.5 %collective-permute-done.1.refs_2_.refs_3_ = bf16[64,768]{1,0:T(8,128)(2,1)S(1)} collective-permute-done((bf16[64,768]{1,0:T(8,128)(2,1)S(1)}, bf16[64,768]{1,0:T(8,128)(2,1)S(1)}, u32[]{:S(2)}, u32[]{:S(2)}) %collective-permute-start.1) | collective-permute-done | bytes 98336 | tf_op jit(solution)/shard_map/ppermute | solution.py:352
  18.0 2.2 %collective-permute-start.6 = (bf16[64,768]{1,0:T(8,128)(2,1)S(1)}, bf16[64,768]{1,0:T(8,128)(2,1)S(1)}, u32[]{:S(2)}, u32[]{:S(2)}) collective-permute-start(bf16[64,768]{1,0:T(8,128)(2,1)S(1)} %get-tuple-element.38), channel_id=1, source_target_pairs={{0,4},{4,0},{8,12},{12,8},{16,20},{20,16},{24,28},{28,24},{1,5},{5... | collective-permute-start | bytes 294920 | tf_op jit(solution)/shard_map/ppermute | solution.py:352
  20.2 1.7 %collective-permute-done.2.refs_3_.refs_4_ = bf16[64,768]{1,0:T(8,128)(2,1)S(1)} collective-permute-done((bf16[64,768]{1,0:T(8,128)(2,1)S(1)}, bf16[64,768]{1,0:T(8,128)(2,1)S(1)}, u32[]{:S(2)}, u32[]{:S(2)}) %collective-permute-start.2) | collective-permute-done | bytes 98336 | tf_op jit(solution)/shard_map/ppermute | solution.py:352
  22.0 1.5 %shard_map.93.refs_0_ = bf16[2304,256]{1,0:T(8,128)(2,1)S(1)} custom-call(f32[1,768]{1,0:T(1,128)S(1)} %get-tuple-element.30.gain_ref, bf16[768,2304]{1,0:T(8,128)(2,1)S(1)} %copy-done.2, bf16[64,768]{1,0:T(8,128)(2,1)S(1)} %get-tuple-element.31.refs_0_.refs_1_, bf16[64,768]{1,0:T(8,128)(2,1)S(1)} %collective-permute-done.refs_1_.refs_2_, ...), custom_call_target="tpu_custom_call" | custom-call | flops 5000000000 | bytes 7000000 | tf_op jit(solution)/shard_map/pallas_call | solution.py:310
  23.5 0.0 collective-permute-done.5.refs_7_
  23.5 0.5 collective-permute-done.6.refs_8_
  24.0 4.0 %shard_map.94 = bf16[512,768]{1,0:T(8,128)(2,1)S(1)} custom-call(f32[12,128]{1,0:T(8,128)S(1)} %get-tuple-element.29.scale_ref, f32[1,768]{1,0:T(1,128)S(1)} %get-tuple-element.30.gain_ref, bf16[768,2304]{1,0:T(8,128)(2,1)S(1)} %copy-done.2, bf16[768,768]{1,0:T(8,128)(2,1)S(1)} %copy-done.4, bf16[2304,256]{1,0:T(8,128)(2,1)S(1)} %shard_map.93.refs_0_, ...), custom_call_target="tpu_custom_call" | custom-call | flops 10000000000 | bytes 10000000 | tf_op jit(solution)/shard_map/pallas_call | solution.py:296
  28.0 0.0 copy-start
  28.0 25.1 %all_to_all.5 = bf16[32,16,768]{2,1,0:T(8,128)(2,1)S(1)} all-to-all(bf16[32,16,768]{2,1,0:T(8,128)(2,1)S(1)} %bitcast.8), channel_id=1, replica_groups=mesh['tm'=8,'patch'=4] {'tm','patch'}, dimensions={0} | all-to-all | bytes 1572864 | tf_op jit(solution)/shard_map/all_to_all | solution.py:400
  53.1 2.3 %shard_map.96 = (bf16[64,768]{1,0:T(8,128)(2,1)S(1)}, bf16[64,768]{1,0:T(8,128)(2,1)S(1)}, bf16[2304,256]{1,0:T(8,128)(2,1)S(1)}, f32[128,768]{1,0:T(8,128)S(1)}) custom-call(f32[12,128]{1,0:T(8,128)S(1)} %get-tuple-element.27.scale_ref, f32[1,768]{1,0:T(1,128)S(1)} %get-tuple-element.28.gain_ref, bf16[768,2304]{1,0:T(8,128)(2,1)S(1)} %copy-done.3, ...), custom_call_target="tpu_custom_call" | custom-call | flops 10000000000 | bytes 10000000 | tf_op jit(solution)/shard_map/pallas_call | solution.py:296
  55.4 1.5 %collective-permute-start.10 = (bf16[1,64,768]{2,1,0:T(8,128)(2,1)S(1)}, bf16[1,64,768]{2,1,0:T(8,128)(2,1)S(1)}, u32[]{:S(2)}, u32[]{:S(2)}) collective-permute-start(bf16[1,64,768]{2,1,0:T(8,128)(2,1)S(1)} %bitcast.11), channel_id=1, source_target_pairs={{0,2},{1,3},{2,0},{3,1},{4,6},{5,7},{6,4},{7,5},{8,10},{9,11},{10,... | collective-permute-start | bytes 294920 | tf_op jit(solution)/shard_map/ppermute | solution.py:352
  57.0 0.0 collective-permute-start.11
  57.0 2.3 %shard_map.95 = (bf16[64,768]{1,0:T(8,128)(2,1)S(1)}, bf16[64,768]{1,0:T(8,128)(2,1)S(1)}, bf16[2304,256]{1,0:T(8,128)(2,1)S(1)}, f32[128,768]{1,0:T(8,128)S(1)}) custom-call(f32[12,128]{1,0:T(8,128)S(1)} %get-tuple-element.27.scale_ref, f32[1,768]{1,0:T(1,128)S(1)} %get-tuple-element.28.gain_ref, bf16[768,2304]{1,0:T(8,128)(2,1)S(1)} %copy-done.3, ...), custom_call_target="tpu_custom_call" | custom-call | flops 10000000000 | bytes 10000000 | tf_op jit(solution)/shard_map/pallas_call | solution.py:296
  59.3 1.6 %collective-permute-start.7 = (bf16[1,64,768]{2,1,0:T(8,128)(2,1)S(1)}, bf16[1,64,768]{2,1,0:T(8,128)(2,1)S(1)}, u32[]{:S(2)}, u32[]{:S(2)}) collective-permute-start(bf16[1,64,768]{2,1,0:T(8,128)(2,1)S(1)} %bitcast.12), channel_id=1, source_target_pairs={{0,2},{1,3},{2,0},{3,1},{4,6},{5,7},{6,4},{7,5},{8,10},{9,11},{10,... | collective-permute-start | bytes 294920 | tf_op jit(solution)/shard_map/ppermute | solution.py:352
  60.9 0.5 collective-permute-start.8
  61.4 2.1 %shard_map.97 = (bf16[2,64,768]{2,1,0:T(8,128)(2,1)S(1)}, bf16[2,64,768]{2,1,0:T(8,128)(2,1)S(1)}) custom-call(f32[12,128]{1,0:T(8,128)S(1)} %get-tuple-element.27.scale_ref, bf16[768,768]{1,0:T(8,128)(2,1)S(1)} %copy-done, bf16[2304,256]{1,0:T(8,128)(2,1)S(1)} %get-tuple-element.41.refs_0_, f32[128,768]{1,0:T(8,128)S(1)} %get-tuple-element.42.refs_1_, ...), custom_call_target="tpu_custom_call" | custom-call | flops 1000000 | bytes 1000 | tf_op jit(solution)/shard_map/pallas_call | solution.py:296
  63.5 0.2 collective-permute-start.9
  63.8 0.7 %shard_map.98.refs_4_ = bf16[8,64,768]{2,1,0:T(8,128)(2,1)} custom-call(bf16[1,64,768]{2,1,0:T(8,128)(2,1)S(1)} %collective-permute-done.10.refs_0_, bf16[1,64,768]{2,1,0:T(8,128)(2,1)S(1)} %collective-permute-done.11.refs_1_), custom_call_target="tpu_custom_call" | custom-call | flops 10000000000 | bytes 1000000 | tf_op jit(solution)/shard_map/pallas_call | solution.py:338
  64.5 0.6 collective-permute-done.7.refs_0_
  65.0 1.5 %collective-permute-done.8.refs_1_ = bf16[1,64,768]{2,1,0:T(8,128)(2,1)S(1)} collective-permute-done((bf16[1,64,768]{2,1,0:T(8,128)(2,1)S(1)}, bf16[1,64,768]{2,1,0:T(8,128)(2,1)S(1)}, u32[]{:S(2)}, u32[]{:S(2)}) %collective-permute-start.8) | collective-permute-done | bytes 98336 | tf_op jit(solution)/shard_map/ppermute | solution.py:352
  66.6 0.8 %shard_map.99 = bf16[8,64,768]{2,1,0:T(8,128)(2,1)} custom-call(bf16[1,64,768]{2,1,0:T(8,128)(2,1)S(1)} %collective-permute-done.7.refs_0_, bf16[1,64,768]{2,1,0:T(8,128)(2,1)S(1)} %collective-permute-done.8.refs_1_, bf16[2,64,768]{2,1,0:T(8,128)(2,1)S(1)} %get-tuple-element.45.refs_2_, ...), custom_call_target="tpu_custom_call", output_to_operand_aliasing={{}: (4, {})} | custom-call | flops 10000000000 | bytes 1000000 | tf_op jit(solution)/shard_map/pallas_call | solution.py:338
  (14 shorter events, 0.0 us)
Async XLA Ops:
  0.0 1.1 %copy-start.1 = (bf16[8,64,768]{2,1,0:T(8,128)(2,1)S(1)}, bf16[8,64,768]{2,1,0:T(8,128)(2,1)}, u32[]{:S(2)}) copy-start(bf16[8,64,768]{2,1,0:T(8,128)(2,1)} %tokens_ref.1) | copy-start | bytes 2359300
  1.4 11.6 %collective-permute-start = (bf16[64,768]{1,0:T(8,128)(2,1)S(1)}, bf16[64,768]{1,0:T(8,128)(2,1)S(1)}, u32[]{:S(2)}, u32[]{:S(2)}) collective-permute-start(bf16[64,768]{1,0:T(8,128)(2,1)S(1)} %get-tuple-element.32), channel_id=1, source_target_pairs={{0,8},{4,12},{8,0},{12,4},{16,24},{20,28},{24,16},{28,20},{1,9},{5... | collective-permute-start | bytes 294920 | tf_op jit(solution)/shard_map/ppermute | solution.py:352
  4.5 13.5 %collective-permute-start.1 = (bf16[64,768]{1,0:T(8,128)(2,1)S(1)}, bf16[64,768]{1,0:T(8,128)(2,1)S(1)}, u32[]{:S(2)}, u32[]{:S(2)}) collective-permute-start(bf16[64,768]{1,0:T(8,128)(2,1)S(1)} %get-tuple-element.33), channel_id=1, source_target_pairs={{0,16},{4,20},{8,24},{12,28},{16,0},{20,4},{24,8},{28,12},{1,17},{... | collective-permute-start | bytes 294920 | tf_op jit(solution)/shard_map/ppermute | solution.py:352
  7.1 14.8 %collective-permute-start.2 = (bf16[64,768]{1,0:T(8,128)(2,1)S(1)}, bf16[64,768]{1,0:T(8,128)(2,1)S(1)}, u32[]{:S(2)}, u32[]{:S(2)}) collective-permute-start(bf16[64,768]{1,0:T(8,128)(2,1)S(1)} %get-tuple-element.34), channel_id=1, source_target_pairs={{0,20},{4,16},{8,28},{12,24},{16,4},{20,0},{24,12},{28,8},{1,21},{... | collective-permute-start | bytes 294920 | tf_op jit(solution)/shard_map/ppermute | solution.py:352
  8.4 15.0 %collective-permute-start.3 = (bf16[64,768]{1,0:T(8,128)(2,1)S(1)}, bf16[64,768]{1,0:T(8,128)(2,1)S(1)}, u32[]{:S(2)}, u32[]{:S(2)}) collective-permute-start(bf16[64,768]{1,0:T(8,128)(2,1)S(1)} %get-tuple-element.35), channel_id=1, source_target_pairs={{0,24},{4,28},{8,16},{12,20},{16,8},{20,12},{24,0},{28,4},{1,25},{... | collective-permute-start | bytes 294920 | tf_op jit(solution)/shard_map/ppermute | solution.py:352
  10.9 12.6 %collective-permute-start.4 = (bf16[64,768]{1,0:T(8,128)(2,1)S(1)}, bf16[64,768]{1,0:T(8,128)(2,1)S(1)}, u32[]{:S(2)}, u32[]{:S(2)}) collective-permute-start(bf16[64,768]{1,0:T(8,128)(2,1)S(1)} %get-tuple-element.36), channel_id=1, source_target_pairs={{0,28},{4,24},{8,20},{12,16},{16,12},{20,8},{24,4},{28,0},{1,29},{... | collective-permute-start | bytes 294920 | tf_op jit(solution)/shard_map/ppermute | solution.py:352
  13.0 9.0 %copy-start.2 = (bf16[768,2304]{1,0:T(8,128)(2,1)S(1)}, bf16[768,2304]{1,0:T(8,128)(2,1)}, u32[]{:S(2)}) copy-start(bf16[768,2304]{1,0:T(8,128)(2,1)} %proj_ref.5) | copy-start | bytes 10616836
  13.1 10.4 %collective-permute-start.5 = (bf16[64,768]{1,0:T(8,128)(2,1)S(1)}, bf16[64,768]{1,0:T(8,128)(2,1)S(1)}, u32[]{:S(2)}, u32[]{:S(2)}) collective-permute-start(bf16[64,768]{1,0:T(8,128)(2,1)S(1)} %get-tuple-element.37), channel_id=1, source_target_pairs={{0,12},{4,8},{8,4},{12,0},{16,28},{20,24},{24,20},{28,16},{1,13},{... | collective-permute-start | bytes 294920 | tf_op jit(solution)/shard_map/ppermute | solution.py:352
  18.0 6.0 %collective-permute-start.6 = (bf16[64,768]{1,0:T(8,128)(2,1)S(1)}, bf16[64,768]{1,0:T(8,128)(2,1)S(1)}, u32[]{:S(2)}, u32[]{:S(2)}) collective-permute-start(bf16[64,768]{1,0:T(8,128)(2,1)S(1)} %get-tuple-element.38), channel_id=1, source_target_pairs={{0,4},{4,0},{8,12},{12,8},{16,20},{20,16},{24,28},{28,24},{1,5},{5... | collective-permute-start | bytes 294920 | tf_op jit(solution)/shard_map/ppermute | solution.py:352
  22.0 2.1 %copy-start.4 = (bf16[768,768]{1,0:T(8,128)(2,1)S(1)}, bf16[768,768]{1,0:T(8,128)(2,1)}, u32[]{:S(2)}) copy-start(bf16[768,768]{1,0:T(8,128)(2,1)} %out_ref.4) | copy-start | bytes 3538948
  24.0 29.1 %copy-start.3 = (bf16[768,2304]{1,0:T(8,128)(2,1)S(1)}, bf16[768,2304]{1,0:T(8,128)(2,1)}, u32[]{:S(2)}) copy-start(bf16[768,2304]{1,0:T(8,128)(2,1)} %proj_ref.7) | copy-start | bytes 10616836
  28.0 25.1 %copy-start = (bf16[768,768]{1,0:T(8,128)(2,1)S(1)}, bf16[768,768]{1,0:T(8,128)(2,1)}, u32[]{:S(2)}) copy-start(bf16[768,768]{1,0:T(8,128)(2,1)} %out_ref.7) | copy-start | bytes 3538948
  55.4 8.3 %collective-permute-start.10 = (bf16[1,64,768]{2,1,0:T(8,128)(2,1)S(1)}, bf16[1,64,768]{2,1,0:T(8,128)(2,1)S(1)}, u32[]{:S(2)}, u32[]{:S(2)}) collective-permute-start(bf16[1,64,768]{2,1,0:T(8,128)(2,1)S(1)} %bitcast.11), channel_id=1, source_target_pairs={{0,2},{1,3},{2,0},{3,1},{4,6},{5,7},{6,4},{7,5},{8,10},{9,11},{10,... | collective-permute-start | bytes 294920 | tf_op jit(solution)/shard_map/ppermute | solution.py:352
  57.0 6.8 %collective-permute-start.11 = (bf16[1,64,768]{2,1,0:T(8,128)(2,1)S(1)}, bf16[1,64,768]{2,1,0:T(8,128)(2,1)S(1)}, u32[]{:S(2)}, u32[]{:S(2)}) collective-permute-start(bf16[1,64,768]{2,1,0:T(8,128)(2,1)S(1)} %bitcast.9), channel_id=1, source_target_pairs={{0,3},{1,2},{2,1},{3,0},{4,7},{5,6},{6,5},{7,4},{8,11},{9,10},{10,... | collective-permute-start | bytes 294920 | tf_op jit(solution)/shard_map/ppermute | solution.py:352
  59.3 5.7 %collective-permute-start.7 = (bf16[1,64,768]{2,1,0:T(8,128)(2,1)S(1)}, bf16[1,64,768]{2,1,0:T(8,128)(2,1)S(1)}, u32[]{:S(2)}, u32[]{:S(2)}) collective-permute-start(bf16[1,64,768]{2,1,0:T(8,128)(2,1)S(1)} %bitcast.12), channel_id=1, source_target_pairs={{0,2},{1,3},{2,0},{3,1},{4,6},{5,7},{6,4},{7,5},{8,10},{9,11},{10,... | collective-permute-start | bytes 294920 | tf_op jit(solution)/shard_map/ppermute | solution.py:352
  60.9 5.7 %collective-permute-start.8 = (bf16[1,64,768]{2,1,0:T(8,128)(2,1)S(1)}, bf16[1,64,768]{2,1,0:T(8,128)(2,1)S(1)}, u32[]{:S(2)}, u32[]{:S(2)}) collective-permute-start(bf16[1,64,768]{2,1,0:T(8,128)(2,1)S(1)} %bitcast.10), channel_id=1, source_target_pairs={{0,3},{1,2},{2,1},{3,0},{4,7},{5,6},{6,5},{7,4},{8,11},{9,10},{10,... | collective-permute-start | bytes 294920 | tf_op jit(solution)/shard_map/ppermute | solution.py:352
  63.5 3.0 %collective-permute-start.9 = (bf16[2,64,768]{2,1,0:T(8,128)(2,1)S(1)}, bf16[2,64,768]{2,1,0:T(8,128)(2,1)S(1)}, u32[]{:S(2)}, u32[]{:S(2)}) collective-permute-start(bf16[2,64,768]{2,1,0:T(8,128)(2,1)S(1)} %get-tuple-element.46), channel_id=1, source_target_pairs={{0,1},{1,0},{2,3},{3,2},{4,5},{5,4},{6,7},{7,6},{8,9},{9,8},{10,11... | collective-permute-start | bytes 589832 | tf_op jit(solution)/shard_map/ppermute | solution.py:352

commit v7 on v6

--- a/solution.py
+++ b/solution.py
@@ -38,12 +38,17 @@
 
 
 def project(normed, proj_ref, fields_ref):
+    for cut, fields in projected(normed, proj_ref):
+        fields_ref[cut] = fields
+
+
+def projected(normed, proj_ref):
     for part in range(3):
         cut = slice(part * WIDTH, (part + 1) * WIDTH)
         fields = dot(proj_ref[:, cut], normed, TT)
         if part < 2:
             fields = unit_columns(fields)
-        fields_ref[cut] = fields.astype(jnp.bfloat16)
+        yield cut, fields.astype(jnp.bfloat16)
 
 
 def hold(held, values):
@@ -157,8 +162,7 @@
 def time_kernel(groups, patches, scale_ref, gain_ref, proj_ref, out_ref, *refs):
     count, ready = sum(map(len, groups)), len(groups) - 1
     fields, pieces = refs[:ready], refs[ready : ready + count]
-    stream_ref, held, result, merged, mixed, own_fields, *work = refs[ready + count :]
-    fields = fields + (own_fields,)
+    stream_ref, held, result, merged, mixed, *work = refs[ready + count :]
     rows = held.shape[1] // len(groups)
     length = rows // patches
     packed = time_packed(len(groups) * length, patches)
@@ -166,17 +170,16 @@
     turn = len(groups) == 2
     order = [patch ^ packed if turn else patch for patch in range(patches)]
     tokens = [pick(held, ready * rows + patch, length, patches) for patch in order]
-    project(layer_norm(jnp.concatenate(tokens, axis=0), gain_ref[...]), proj_ref, own_fields)
+    normed = layer_norm(jnp.concatenate(tokens, axis=0), gain_ref[...])
     if turn:
-        near = lax.broadcasted_iota(jnp.int32, (HEAD_DIM, LANES), 1) < packed * length
-        for low in range(0, 3 * WIDTH, HEAD_DIM):
-            cut = slice(low, low + HEAD_DIM)
+        near = lax.broadcasted_iota(jnp.int32, (WIDTH, LANES), 1) < packed * length
+        for cut, own in projected(normed, proj_ref):
             for tile in range(0, rows, LANES):
-                first, second = (group[cut, tile : tile + LANES] for group in fields)
+                first, second = fields[0][cut, tile : tile + LANES], own[:, tile : tile + LANES]
                 merged[cut, 2 * tile : 2 * tile + LANES] = jnp.where(near, first, second)
                 merged[cut, 2 * tile + LANES : 2 * tile + 2 * LANES] = jnp.where(near, second, first)
     else:
-        merged = own_fields
+        project(normed, proj_ref, merged)
     attend(merged, scale_ref, mixed, *work, len(groups), packed, length)
     half = max(patches // 2, packed)
     for patch in range(patches):
@@ -331,7 +334,7 @@
     )(tokens)
 
 
-def place(places, pieces, whole, shape):
+def place(places, pieces, whole, shape, flops):
     anywhere = pl.BlockSpec(memory_space=pl.ANY)
     count = len(pieces)
     others = [] if whole is None else [whole]
@@ -343,7 +346,7 @@
         scratch_shapes=[pltpu.SemaphoreType.DMA] * count,
         input_output_aliases={count: 0} if others else {},
         compiler_params=pltpu.CompilerParams(vmem_limit_bytes=1024 * 1024),
-        cost_estimate=pl.CostEstimate(flops=10**10, bytes_accessed=10**6, transcendentals=0),
+        cost_estimate=pl.CostEstimate(flops=flops, bytes_accessed=flops // 10**4, transcendentals=0),
     )(*pieces, *others)
 
 
@@ -392,7 +395,7 @@
     stream = call(
         functools.partial(time_kernel, groups, patches),
         [((rows, width), jnp.bfloat16)],
-        [held, held] + space + [pltpu.VMEM((3 * width, rows // len(groups)), jnp.bfloat16)] + work,
+        [held, held] + space + work,
         10**10,
         time_scale, time_gain, time_proj, time_out, *fields, *arrived,
     )[0]
@@ -431,10 +434,10 @@
     near = [exchange(piece, "patch", index) if index else piece for index, piece in enumerate(near)]
     block = None
     for frame in range(own_frames):
-        places, pieces = [(half + index, frame, own_frames) for index in range(half)], far[frame]
         if frame == own_frames - 1:
-            places, pieces = places + [(index, 0, own_frames) for index in range(half)], pieces + near
-        block = place(places, pieces, block, tokens.shape)
+            block = place([(index, 0, own_frames) for index in range(half)], near, block, tokens.shape, 10**6)
+        places = [(half + index, frame, own_frames) for index in range(half)]
+        block = place(places, far[frame], block, tokens.shape, 10**10)
     return block
 
 

time: 67.8 us -> 67.6 us (level)
  waiting for transfers between devices: 8.9 us -> 8.12 us
    ppermute x12, waiting for transfers between devices: 8.9 us -> 8.12 us  [exchange(): return lax.ppermute(piece, axis, [(i, i ^ index) for i in range(size)])]
    pallas_call x2 -> x3, Pallas kernels: 1.53 us -> 2.14 us  [place(): pl.pallas_call(functools.partial(place_kernel, places), out_shape=jax.Sha...]
  transfers between devices with their start and end apart: 12 -> 12, of which waited for: 5 -> 5; matrix products, arithmetic and copies ran while one was open for 1% -> 1% of each run, Pallas kernels for 10% -> 11%
where the time goes in v7:
time: 67.6 us; the launch traced here: 67.4 us
  blocking collectives  25.1 us (37%)
  starting transfers between devices  17.2 us (25%)
  Pallas kernels  14.8 us (22%)
  waiting for transfers between devices  8.12 us (12%)
  local copies, waits for them, and re-layouts  1.93 us (3%)
    all_to_all x1, blocking collectives, per_device(): lax.all_to_all(stream.reshape(senders, rows // senders, width), ('tm', 'p...  25.1 us
    ppermute x12, starting transfers between devices, exchange(): return lax.ppermute(piece, axis, [(i, i ^ index) for i in range(size)])  17.2 us
    pallas_call x4, Pallas kernels, call(): pl.pallas_call(kernel, out_shape=[jax.ShapeDtypeStruct(*shape) for shape...  10.8 us
    ppermute x12, waiting for transfers between devices, exchange(): return lax.ppermute(piece, axis, [(i, i ^ index) for i in range(size)])  8.12 us
    pallas_call x3, Pallas kernels, place(): pl.pallas_call(functools.partial(place_kernel, places), out_shape=jax.Sha...  2.14 us
    pallas_call x1, Pallas kernels, project_early(): pl.pallas_call(functools.partial(fields_kernel, patches), out_shape=jax.S...  1.5 us
  transfers between devices with their start and end apart: 12, of which 5 were waited for; matrix products, arithmetic and copies ran while one was open for 1% of the time, Pallas kernels for 11%

profile of v7, /device:TPU:0, one launch (start us, length us, event | category | flops | bytes accessed | tf_op | source)
XLA Modules:
  0.0 67.4 jit_solution(12688036822053452425)
XLA Ops:
  0.0 1.1 %copy-done.1 = bf16[8,64,768]{2,1,0:T(8,128)(2,1)S(1)} copy-done((bf16[8,64,768]{2,1,0:T(8,128)(2,1)S(1)}, bf16[8,64,768]{2,1,0:T(8,128)(2,1)}, u32[]{:S(2)}) %copy-start.1) | copy-done | bytes 786456
  1.1 0.3 shard_map.92
  1.4 3.1 %collective-permute-start = (bf16[64,768]{1,0:T(8,128)(2,1)S(1)}, bf16[64,768]{1,0:T(8,128)(2,1)S(1)}, u32[]{:S(2)}, u32[]{:S(2)}) collective-permute-start(bf16[64,768]{1,0:T(8,128)(2,1)S(1)} %get-tuple-element.32), channel_id=1, source_target_pairs={{0,8},{4,12},{8,0},{12,4},{16,24},{20,28},{24,16},{28,20},{1,9},{5... | collective-permute-start | bytes 294920 | tf_op jit(solution)/shard_map/ppermute | solution.py:355
  4.5 2.6 %collective-permute-start.1 = (bf16[64,768]{1,0:T(8,128)(2,1)S(1)}, bf16[64,768]{1,0:T(8,128)(2,1)S(1)}, u32[]{:S(2)}, u32[]{:S(2)}) collective-permute-start(bf16[64,768]{1,0:T(8,128)(2,1)S(1)} %get-tuple-element.33), channel_id=1, source_target_pairs={{0,16},{4,20},{8,24},{12,28},{16,0},{20,4},{24,8},{28,12},{1,17},{... | collective-permute-start | bytes 294920 | tf_op jit(solution)/shard_map/ppermute | solution.py:355
  7.1 1.3 %collective-permute-start.2 = (bf16[64,768]{1,0:T(8,128)(2,1)S(1)}, bf16[64,768]{1,0:T(8,128)(2,1)S(1)}, u32[]{:S(2)}, u32[]{:S(2)}) collective-permute-start(bf16[64,768]{1,0:T(8,128)(2,1)S(1)} %get-tuple-element.34), channel_id=1, source_target_pairs={{0,20},{4,16},{8,28},{12,24},{16,4},{20,0},{24,12},{28,8},{1,21},{... | collective-permute-start | bytes 294920 | tf_op jit(solution)/shard_map/ppermute | solution.py:355
  8.4 2.5 %collective-permute-start.3 = (bf16[64,768]{1,0:T(8,128)(2,1)S(1)}, bf16[64,768]{1,0:T(8,128)(2,1)S(1)}, u32[]{:S(2)}, u32[]{:S(2)}) collective-permute-start(bf16[64,768]{1,0:T(8,128)(2,1)S(1)} %get-tuple-element.35), channel_id=1, source_target_pairs={{0,24},{4,28},{8,16},{12,20},{16,8},{20,12},{24,0},{28,4},{1,25},{... | collective-permute-start | bytes 294920 | tf_op jit(solution)/shard_map/ppermute | solution.py:355
  10.9 1.3 %collective-permute-start.4 = (bf16[64,768]{1,0:T(8,128)(2,1)S(1)}, bf16[64,768]{1,0:T(8,128)(2,1)S(1)}, u32[]{:S(2)}, u32[]{:S(2)}) collective-permute-start(bf16[64,768]{1,0:T(8,128)(2,1)S(1)} %get-tuple-element.36), channel_id=1, source_target_pairs={{0,28},{4,24},{8,20},{12,16},{16,12},{20,8},{24,4},{28,0},{1,29},{... | collective-permute-start | bytes 294920 | tf_op jit(solution)/shard_map/ppermute | solution.py:355
  12.2 0.8 %concatenate.3 = f32[1560]{0:T(1024)S(1)} concatenate(f32[768]{0:T(1024)} %param.10, f32[768]{0:T(1024)} %param.14, f32[12]{0:T(128)} %param.13, f32[12]{0:T(128)} %param.17), dimensions={0} | concatenate | bytes 12480 | tf_op jit(solution)/shard_map/concatenate | solution.py:294
  13.0 0.1 shard_map.91
  13.1 0.0 collective-permute-done.refs_1_.refs_2_
  13.1 0.4 collective-permute-start.5
  13.4 4.5 %collective-permute-done.1.refs_2_.refs_3_ = bf16[64,768]{1,0:T(8,128)(2,1)S(1)} collective-permute-done((bf16[64,768]{1,0:T(8,128)(2,1)S(1)}, bf16[64,768]{1,0:T(8,128)(2,1)S(1)}, u32[]{:S(2)}, u32[]{:S(2)}) %collective-permute-start.1) | collective-permute-done | bytes 98336 | tf_op jit(solution)/shard_map/ppermute | solution.py:355
  18.0 2.2 %collective-permute-start.6 = (bf16[64,768]{1,0:T(8,128)(2,1)S(1)}, bf16[64,768]{1,0:T(8,128)(2,1)S(1)}, u32[]{:S(2)}, u32[]{:S(2)}) collective-permute-start(bf16[64,768]{1,0:T(8,128)(2,1)S(1)} %get-tuple-element.38), channel_id=1, source_target_pairs={{0,4},{4,0},{8,12},{12,8},{16,20},{20,16},{24,28},{28,24},{1,5},{5... | collective-permute-start | bytes 294920 | tf_op jit(solution)/shard_map/ppermute | solution.py:355
  20.2 1.7 %collective-permute-done.2.refs_3_.refs_4_ = bf16[64,768]{1,0:T(8,128)(2,1)S(1)} collective-permute-done((bf16[64,768]{1,0:T(8,128)(2,1)S(1)}, bf16[64,768]{1,0:T(8,128)(2,1)S(1)}, u32[]{:S(2)}, u32[]{:S(2)}) %collective-permute-start.2) | collective-permute-done | bytes 98336 | tf_op jit(solution)/shard_map/ppermute | solution.py:355
  22.0 1.5 %shard_map.93.refs_0_ = bf16[2304,256]{1,0:T(8,128)(2,1)S(1)} custom-call(f32[1,768]{1,0:T(1,128)S(1)} %get-tuple-element.30.gain_ref, bf16[768,2304]{1,0:T(8,128)(2,1)S(1)} %copy-done.2, bf16[64,768]{1,0:T(8,128)(2,1)S(1)} %get-tuple-element.31.refs_0_.refs_1_, bf16[64,768]{1,0:T(8,128)(2,1)S(1)} %collective-permute-done.refs_1_.refs_2_, ...), custom_call_target="tpu_custom_call" | custom-call | flops 5000000000 | bytes 7000000 | tf_op jit(solution)/shard_map/pallas_call | solution.py:313
  23.5 0.0 collective-permute-done.5.refs_7_
  23.5 0.5 collective-permute-done.6.refs_8_
  24.0 4.0 %shard_map.94 = bf16[512,768]{1,0:T(8,128)(2,1)S(1)} custom-call(f32[12,128]{1,0:T(8,128)S(1)} %get-tuple-element.29.scale_ref, f32[1,768]{1,0:T(1,128)S(1)} %get-tuple-element.30.gain_ref, bf16[768,2304]{1,0:T(8,128)(2,1)S(1)} %copy-done.2, bf16[768,768]{1,0:T(8,128)(2,1)S(1)} %copy-done.4, bf16[2304,256]{1,0:T(8,128)(2,1)S(1)} %shard_map.93.refs_0_, ...), custom_call_target="tpu_custom_call" | custom-call | flops 10000000000 | bytes 10000000 | tf_op jit(solution)/shard_map/pallas_call | solution.py:299
  28.0 0.0 copy-start
  28.0 25.1 %all_to_all.5 = bf16[32,16,768]{2,1,0:T(8,128)(2,1)S(1)} all-to-all(bf16[32,16,768]{2,1,0:T(8,128)(2,1)S(1)} %bitcast.8), channel_id=1, replica_groups=mesh['tm'=8,'patch'=4] {'tm','patch'}, dimensions={0} | all-to-all | bytes 1572864 | tf_op jit(solution)/shard_map/all_to_all | solution.py:403
  53.1 2.3 %shard_map.96 = (bf16[64,768]{1,0:T(8,128)(2,1)S(1)}, bf16[64,768]{1,0:T(8,128)(2,1)S(1)}, bf16[2304,256]{1,0:T(8,128)(2,1)S(1)}, f32[128,768]{1,0:T(8,128)S(1)}) custom-call(f32[12,128]{1,0:T(8,128)S(1)} %get-tuple-element.27.scale_ref, f32[1,768]{1,0:T(1,128)S(1)} %get-tuple-element.28.gain_ref, bf16[768,2304]{1,0:T(8,128)(2,1)S(1)} %copy-done.3, ...), custom_call_target="tpu_custom_call" | custom-call | flops 10000000000 | bytes 10000000 | tf_op jit(solution)/shard_map/pallas_call | solution.py:299
  55.4 1.5 %collective-permute-start.10 = (bf16[1,64,768]{2,1,0:T(8,128)(2,1)S(1)}, bf16[1,64,768]{2,1,0:T(8,128)(2,1)S(1)}, u32[]{:S(2)}, u32[]{:S(2)}) collective-permute-start(bf16[1,64,768]{2,1,0:T(8,128)(2,1)S(1)} %bitcast.12), channel_id=1, source_target_pairs={{0,2},{1,3},{2,0},{3,1},{4,6},{5,7},{6,4},{7,5},{8,10},{9,11},{10,... | collective-permute-start | bytes 294920 | tf_op jit(solution)/shard_map/ppermute | solution.py:355
  57.0 2.3 %shard_map.95 = (bf16[64,768]{1,0:T(8,128)(2,1)S(1)}, bf16[64,768]{1,0:T(8,128)(2,1)S(1)}, bf16[2304,256]{1,0:T(8,128)(2,1)S(1)}, f32[128,768]{1,0:T(8,128)S(1)}) custom-call(f32[12,128]{1,0:T(8,128)S(1)} %get-tuple-element.27.scale_ref, f32[1,768]{1,0:T(1,128)S(1)} %get-tuple-element.28.gain_ref, bf16[768,2304]{1,0:T(8,128)(2,1)S(1)} %copy-done.3, ...), custom_call_target="tpu_custom_call" | custom-call | flops 10000000000 | bytes 10000000 | tf_op jit(solution)/shard_map/pallas_call | solution.py:299
  59.3 1.6 %collective-permute-start.7 = (bf16[1,64,768]{2,1,0:T(8,128)(2,1)S(1)}, bf16[1,64,768]{2,1,0:T(8,128)(2,1)S(1)}, u32[]{:S(2)}, u32[]{:S(2)}) collective-permute-start(bf16[1,64,768]{2,1,0:T(8,128)(2,1)S(1)} %bitcast.10), channel_id=1, source_target_pairs={{0,2},{1,3},{2,0},{3,1},{4,6},{5,7},{6,4},{7,5},{8,10},{9,11},{10,... | collective-permute-start | bytes 294920 | tf_op jit(solution)/shard_map/ppermute | solution.py:355
  60.9 0.5 collective-permute-start.8
  61.4 2.1 %shard_map.97 = (bf16[2,64,768]{2,1,0:T(8,128)(2,1)S(1)}, bf16[2,64,768]{2,1,0:T(8,128)(2,1)S(1)}) custom-call(f32[12,128]{1,0:T(8,128)S(1)} %get-tuple-element.27.scale_ref, bf16[768,768]{1,0:T(8,128)(2,1)S(1)} %copy-done, bf16[2304,256]{1,0:T(8,128)(2,1)S(1)} %get-tuple-element.41.refs_0_, f32[128,768]{1,0:T(8,128)S(1)} %get-tuple-element.42.refs_1_, ...), custom_call_target="tpu_custom_call" | custom-call | flops 1000000 | bytes 1000 | tf_op jit(solution)/shard_map/pallas_call | solution.py:299
  63.5 0.2 collective-permute-start.9
  63.8 0.7 %shard_map.98.refs_2_ = bf16[8,64,768]{2,1,0:T(8,128)(2,1)} custom-call(bf16[1,64,768]{2,1,0:T(8,128)(2,1)S(1)} %collective-permute-done.10.refs_0_, bf16[1,64,768]{2,1,0:T(8,128)(2,1)S(1)} %collective-permute-done.11.refs_1_), custom_call_target="tpu_custom_call" | custom-call | flops 10000000000 | bytes 1000000 | tf_op jit(solution)/shard_map/pallas_call | solution.py:341
  64.5 0.6 collective-permute-done.9.refs_1_
  65.0 0.8 %shard_map.99.refs_2_ = bf16[8,64,768]{2,1,0:T(8,128)(2,1)} custom-call(bf16[2,64,768]{2,1,0:T(8,128)(2,1)S(1)} %get-tuple-element.45.refs_0_, bf16[2,64,768]{2,1,0:T(8,128)(2,1)S(1)} %collective-permute-done.9.refs_1_, bf16[8,64,768]{2,1,0:T(8,128)(2,1)} %shard_map.98.refs_2_), custom_call_target="tpu_custom_call", output_to_operand_aliasing={{}: (2, {})} | custom-call | flops 1000000 | bytes 100 | tf_op jit(solution)/shard_map/pallas_call | solution.py:341
  65.8 0.7 %collective-permute-done.8.refs_1_ = bf16[1,64,768]{2,1,0:T(8,128)(2,1)S(1)} collective-permute-done((bf16[1,64,768]{2,1,0:T(8,128)(2,1)S(1)}, bf16[1,64,768]{2,1,0:T(8,128)(2,1)S(1)}, u32[]{:S(2)}, u32[]{:S(2)}) %collective-permute-start.8) | collective-permute-done | bytes 98336 | tf_op jit(solution)/shard_map/ppermute | solution.py:355
  66.5 0.7 %shard_map.100 = bf16[8,64,768]{2,1,0:T(8,128)(2,1)} custom-call(bf16[1,64,768]{2,1,0:T(8,128)(2,1)S(1)} %collective-permute-done.7.refs_0_, bf16[1,64,768]{2,1,0:T(8,128)(2,1)S(1)} %collective-permute-done.8.refs_1_, bf16[8,64,768]{2,1,0:T(8,128)(2,1)} %shard_map.99.refs_2_), custom_call_target="tpu_custom_call", output_to_operand_aliasing={{}: (2, {})} | custom-call | flops 10000000000 | bytes 1000000 | tf_op jit(solution)/shard_map/pallas_call | solution.py:341
  (15 shorter events, 0.0 us)
Async XLA Ops:
  0.0 1.1 %copy-start.1 = (bf16[8,64,768]{2,1,0:T(8,128)(2,1)S(1)}, bf16[8,64,768]{2,1,0:T(8,128)(2,1)}, u32[]{:S(2)}) copy-start(bf16[8,64,768]{2,1,0:T(8,128)(2,1)} %tokens_ref.1) | copy-start | bytes 2359300
  1.4 11.6 %collective-permute-start = (bf16[64,768]{1,0:T(8,128)(2,1)S(1)}, bf16[64,768]{1,0:T(8,128)(2,1)S(1)}, u32[]{:S(2)}, u32[]{:S(2)}) collective-permute-start(bf16[64,768]{1,0:T(8,128)(2,1)S(1)} %get-tuple-element.32), channel_id=1, source_target_pairs={{0,8},{4,12},{8,0},{12,4},{16,24},{20,28},{24,16},{28,20},{1,9},{5... | collective-permute-start | bytes 294920 | tf_op jit(solution)/shard_map/ppermute | solution.py:355
  4.5 13.5 %collective-permute-start.1 = (bf16[64,768]{1,0:T(8,128)(2,1)S(1)}, bf16[64,768]{1,0:T(8,128)(2,1)S(1)}, u32[]{:S(2)}, u32[]{:S(2)}) collective-permute-start(bf16[64,768]{1,0:T(8,128)(2,1)S(1)} %get-tuple-element.33), channel_id=1, source_target_pairs={{0,16},{4,20},{8,24},{12,28},{16,0},{20,4},{24,8},{28,12},{1,17},{... | collective-permute-start | bytes 294920 | tf_op jit(solution)/shard_map/ppermute | solution.py:355
  7.1 14.8 %collective-permute-start.2 = (bf16[64,768]{1,0:T(8,128)(2,1)S(1)}, bf16[64,768]{1,0:T(8,128)(2,1)S(1)}, u32[]{:S(2)}, u32[]{:S(2)}) collective-permute-start(bf16[64,768]{1,0:T(8,128)(2,1)S(1)} %get-tuple-element.34), channel_id=1, source_target_pairs={{0,20},{4,16},{8,28},{12,24},{16,4},{20,0},{24,12},{28,8},{1,21},{... | collective-permute-start | bytes 294920 | tf_op jit(solution)/shard_map/ppermute | solution.py:355
  8.4 15.0 %collective-permute-start.3 = (bf16[64,768]{1,0:T(8,128)(2,1)S(1)}, bf16[64,768]{1,0:T(8,128)(2,1)S(1)}, u32[]{:S(2)}, u32[]{:S(2)}) collective-permute-start(bf16[64,768]{1,0:T(8,128)(2,1)S(1)} %get-tuple-element.35), channel_id=1, source_target_pairs={{0,24},{4,28},{8,16},{12,20},{16,8},{20,12},{24,0},{28,4},{1,25},{... | collective-permute-start | bytes 294920 | tf_op jit(solution)/shard_map/ppermute | solution.py:355
  10.9 12.6 %collective-permute-start.4 = (bf16[64,768]{1,0:T(8,128)(2,1)S(1)}, bf16[64,768]{1,0:T(8,128)(2,1)S(1)}, u32[]{:S(2)}, u32[]{:S(2)}) collective-permute-start(bf16[64,768]{1,0:T(8,128)(2,1)S(1)} %get-tuple-element.36), channel_id=1, source_target_pairs={{0,28},{4,24},{8,20},{12,16},{16,12},{20,8},{24,4},{28,0},{1,29},{... | collective-permute-start | bytes 294920 | tf_op jit(solution)/shard_map/ppermute | solution.py:355
  13.0 9.0 %copy-start.2 = (bf16[768,2304]{1,0:T(8,128)(2,1)S(1)}, bf16[768,2304]{1,0:T(8,128)(2,1)}, u32[]{:S(2)}) copy-start(bf16[768,2304]{1,0:T(8,128)(2,1)} %proj_ref.5) | copy-start | bytes 10616836
  13.1 10.4 %collective-permute-start.5 = (bf16[64,768]{1,0:T(8,128)(2,1)S(1)}, bf16[64,768]{1,0:T(8,128)(2,1)S(1)}, u32[]{:S(2)}, u32[]{:S(2)}) collective-permute-start(bf16[64,768]{1,0:T(8,128)(2,1)S(1)} %get-tuple-element.37), channel_id=1, source_target_pairs={{0,12},{4,8},{8,4},{12,0},{16,28},{20,24},{24,20},{28,16},{1,13},{... | collective-permute-start | bytes 294920 | tf_op jit(solution)/shard_map/ppermute | solution.py:355
  18.0 6.0 %collective-permute-start.6 = (bf16[64,768]{1,0:T(8,128)(2,1)S(1)}, bf16[64,768]{1,0:T(8,128)(2,1)S(1)}, u32[]{:S(2)}, u32[]{:S(2)}) collective-permute-start(bf16[64,768]{1,0:T(8,128)(2,1)S(1)} %get-tuple-element.38), channel_id=1, source_target_pairs={{0,4},{4,0},{8,12},{12,8},{16,20},{20,16},{24,28},{28,24},{1,5},{5... | collective-permute-start | bytes 294920 | tf_op jit(solution)/shard_map/ppermute | solution.py:355
  22.0 2.1 %copy-start.4 = (bf16[768,768]{1,0:T(8,128)(2,1)S(1)}, bf16[768,768]{1,0:T(8,128)(2,1)}, u32[]{:S(2)}) copy-start(bf16[768,768]{1,0:T(8,128)(2,1)} %out_ref.4) | copy-start | bytes 3538948
  24.0 29.1 %copy-start.3 = (bf16[768,2304]{1,0:T(8,128)(2,1)S(1)}, bf16[768,2304]{1,0:T(8,128)(2,1)}, u32[]{:S(2)}) copy-start(bf16[768,2304]{1,0:T(8,128)(2,1)} %proj_ref.7) | copy-start | bytes 10616836
  28.0 25.1 %copy-start = (bf16[768,768]{1,0:T(8,128)(2,1)S(1)}, bf16[768,768]{1,0:T(8,128)(2,1)}, u32[]{:S(2)}) copy-start(bf16[768,768]{1,0:T(8,128)(2,1)} %out_ref.7) | copy-start | bytes 3538948
  55.4 8.3 %collective-permute-start.10 = (bf16[1,64,768]{2,1,0:T(8,128)(2,1)S(1)}, bf16[1,64,768]{2,1,0:T(8,128)(2,1)S(1)}, u32[]{:S(2)}, u32[]{:S(2)}) collective-permute-start(bf16[1,64,768]{2,1,0:T(8,128)(2,1)S(1)} %bitcast.12), channel_id=1, source_target_pairs={{0,2},{1,3},{2,0},{3,1},{4,6},{5,7},{6,4},{7,5},{8,10},{9,11},{10,... | collective-permute-start | bytes 294920 | tf_op jit(solution)/shard_map/ppermute | solution.py:355
  57.0 6.8 %collective-permute-start.11 = (bf16[1,64,768]{2,1,0:T(8,128)(2,1)S(1)}, bf16[1,64,768]{2,1,0:T(8,128)(2,1)S(1)}, u32[]{:S(2)}, u32[]{:S(2)}) collective-permute-start(bf16[1,64,768]{2,1,0:T(8,128)(2,1)S(1)} %bitcast.11), channel_id=1, source_target_pairs={{0,3},{1,2},{2,1},{3,0},{4,7},{5,6},{6,5},{7,4},{8,11},{9,10},{10,... | collective-permute-start | bytes 294920 | tf_op jit(solution)/shard_map/ppermute | solution.py:355
  59.3 6.5 %collective-permute-start.7 = (bf16[1,64,768]{2,1,0:T(8,128)(2,1)S(1)}, bf16[1,64,768]{2,1,0:T(8,128)(2,1)S(1)}, u32[]{:S(2)}, u32[]{:S(2)}) collective-permute-start(bf16[1,64,768]{2,1,0:T(8,128)(2,1)S(1)} %bitcast.10), channel_id=1, source_target_pairs={{0,2},{1,3},{2,0},{3,1},{4,6},{5,7},{6,4},{7,5},{8,10},{9,11},{10,... | collective-permute-start | bytes 294920 | tf_op jit(solution)/shard_map/ppermute | solution.py:355
  60.9 5.7 %collective-permute-start.8 = (bf16[1,64,768]{2,1,0:T(8,128)(2,1)S(1)}, bf16[1,64,768]{2,1,0:T(8,128)(2,1)S(1)}, u32[]{:S(2)}, u32[]{:S(2)}) collective-permute-start(bf16[1,64,768]{2,1,0:T(8,128)(2,1)S(1)} %bitcast.9), channel_id=1, source_target_pairs={{0,3},{1,2},{2,1},{3,0},{4,7},{5,6},{6,5},{7,4},{8,11},{9,10},{10,... | collective-permute-start | bytes 294920 | tf_op jit(solution)/shard_map/ppermute | solution.py:355
  63.5 1.5 %collective-permute-start.9 = (bf16[2,64,768]{2,1,0:T(8,128)(2,1)S(1)}, bf16[2,64,768]{2,1,0:T(8,128)(2,1)S(1)}, u32[]{:S(2)}, u32[]{:S(2)}) collective-permute-start(bf16[2,64,768]{2,1,0:T(8,128)(2,1)S(1)} %get-tuple-element.46), channel_id=1, source_target_pairs={{0,1},{1,0},{2,3},{3,2},{4,5},{5,4},{6,7},{7,6},{8,9},{9,8},{10,11... | collective-permute-start | bytes 589832 | tf_op jit(solution)/shard_map/ppermute | solution.py:355

commit v8 on v7

--- a/solution.py
+++ b/solution.py
@@ -37,16 +37,19 @@
     return (heads * lax.rsqrt(squares + EPSILON)).reshape(fields.shape)
 
 
-def project(normed, proj_ref, fields_ref):
-    for cut, fields in projected(normed, proj_ref):
+QUERIES_KEYS = [slice(0, WIDTH), slice(WIDTH, 2 * WIDTH)]
+VALUES = [slice(2 * WIDTH, 3 * WIDTH)]
+
+
+def project(normed, proj_ref, fields_ref, cuts):
+    for cut, fields in projected(normed, proj_ref, cuts):
         fields_ref[cut] = fields
 
 
-def projected(normed, proj_ref):
-    for part in range(3):
-        cut = slice(part * WIDTH, (part + 1) * WIDTH)
+def projected(normed, proj_ref, cuts):
+    for cut in cuts:
         fields = dot(proj_ref[:, cut], normed, TT)
-        if part < 2:
+        if cut.start < 2 * WIDTH:
             fields = unit_columns(fields)
         yield cut, fields.astype(jnp.bfloat16)
 
@@ -66,7 +69,7 @@
     return slice(part * WIDTH + head * HEAD_DIM, part * WIDTH + (head + 1) * HEAD_DIM)
 
 
-def attend(fields_ref, scale_ref, mixed_ref, scores_ref, weights_ref, totals_ref, groups, packed, length):
+def attend(fields_ref, scale_ref, mixed_ref, scores_ref, weights_ref, totals_ref, groups, packed, length, project_part):
     span = groups * packed * length
     runs = fields_ref.shape[1] // span
     item_of = (lax.broadcasted_iota(jnp.int32, (1, span), 1) // length) % packed
@@ -106,6 +109,8 @@
     count = runs * HEADS
     apart = max(1, AHEAD * 256 // span)
     for step in range(count + 2 * apart):
+        if step == apart // 2:
+            project_part(VALUES)
         for stage, late in ((score, 0), (soften, apart), (mix, 2 * apart)):
             at = step - late
             if 0 <= at < count:
@@ -156,7 +161,7 @@
     pieces, (fields_ref, held) = refs[:-2], refs[-2:]
     hold_pieces(held, pieces)
     tokens = [pick(held, patch, held.shape[1] // patches, patches) for patch in range(patches)]
-    project(layer_norm(jnp.concatenate(tokens, axis=0), gain_ref[...]), proj_ref, fields_ref)
+    project(layer_norm(jnp.concatenate(tokens, axis=0), gain_ref[...]), proj_ref, fields_ref, QUERIES_KEYS + VALUES)
 
 
 def time_kernel(groups, patches, scale_ref, gain_ref, proj_ref, out_ref, *refs):
@@ -171,16 +176,19 @@
     order = [patch ^ packed if turn else patch for patch in range(patches)]
     tokens = [pick(held, ready * rows + patch, length, patches) for patch in order]
     normed = layer_norm(jnp.concatenate(tokens, axis=0), gain_ref[...])
-    if turn:
-        near = lax.broadcasted_iota(jnp.int32, (WIDTH, LANES), 1) < packed * length
-        for cut, own in projected(normed, proj_ref):
+
+    def project_part(cuts):
+        if not turn:
+            return project(normed, proj_ref, merged, cuts)
+        for cut, own in projected(normed, proj_ref, cuts):
+            near = lax.broadcasted_iota(jnp.int32, (cut.stop - cut.start, LANES), 1) < packed * length
             for tile in range(0, rows, LANES):
                 first, second = fields[0][cut, tile : tile + LANES], own[:, tile : tile + LANES]
                 merged[cut, 2 * tile : 2 * tile + LANES] = jnp.where(near, first, second)
                 merged[cut, 2 * tile + LANES : 2 * tile + 2 * LANES] = jnp.where(near, second, first)
-    else:
-        project(normed, proj_ref, merged)
-    attend(merged, scale_ref, mixed, *work, len(groups), packed, length)
+
+    project_part(QUERIES_KEYS)
+    attend(merged, scale_ref, mixed, *work, len(groups), packed, length, project_part)
     half = max(patches // 2, packed)
     for patch in range(patches):
         if patch % half == 0:
@@ -224,7 +232,7 @@
                 place = first + sender * piece
                 tokens[place : place + piece] = rows[frame * piece : (frame + 1) * piece]
     half = sides // 2 * side_patches
-    project(layer_norm(tokens[...], gain_ref[...]), proj_ref, fields)
+    project(layer_norm(tokens[...], gain_ref[...]), proj_ref, fields, QUERIES_KEYS + VALUES)
     attend_lanes(fields, scale_ref, mixed, *work, slice(half, 2 * half))
     stream = tokens[half:] + dot(mixed[...], out_ref[...], TN)
     for index, target in enumerate(pieces):

time: 67.6 us -> 67.6 us (level)
  no operation moved by 1% of the time
where the time goes in v8:
time: 67.6 us; the launch traced here: 67.4 us
  blocking collectives  25.1 us (37%)
  starting transfers between devices  17.2 us (25%)
  Pallas kernels  14.8 us (22%)
  waiting for transfers between devices  8.12 us (12%)
  local copies, waits for them, and re-layouts  1.93 us (3%)
    all_to_all x1, blocking collectives, per_device(): lax.all_to_all(stream.reshape(senders, rows // senders, width), ('tm', 'p...  25.1 us
    ppermute x12, starting transfers between devices, exchange(): return lax.ppermute(piece, axis, [(i, i ^ index) for i in range(size)])  17.2 us
    pallas_call x4, Pallas kernels, call(): pl.pallas_call(kernel, out_shape=[jax.ShapeDtypeStruct(*shape) for shape...  10.8 us
    ppermute x12, waiting for transfers between devices, exchange(): return lax.ppermute(piece, axis, [(i, i ^ index) for i in range(size)])  8.12 us
    pallas_call x3, Pallas kernels, place(): pl.pallas_call(functools.partial(place_kernel, places), out_shape=jax.Sha...  2.14 us
    pallas_call x1, Pallas kernels, project_early(): pl.pallas_call(functools.partial(fields_kernel, patches), out_shape=jax.S...  1.5 us
  transfers between devices with their start and end apart: 12, of which 5 were waited for; matrix products, arithmetic and copies ran while one was open for 1% of the time, Pallas kernels for 11%

profile of v8, /device:TPU:0, one launch (start us, length us, event | category | flops | bytes accessed | tf_op | source)
XLA Modules:
  0.0 67.4 jit_solution(9136018655162743226)
XLA Ops:
  0.0 1.1 %copy-done.1 = bf16[8,64,768]{2,1,0:T(8,128)(2,1)S(1)} copy-done((bf16[8,64,768]{2,1,0:T(8,128)(2,1)S(1)}, bf16[8,64,768]{2,1,0:T(8,128)(2,1)}, u32[]{:S(2)}) %copy-start.1) | copy-done | bytes 786456
  1.1 0.3 shard_map.92
  1.4 3.1 %collective-permute-start = (bf16[64,768]{1,0:T(8,128)(2,1)S(1)}, bf16[64,768]{1,0:T(8,128)(2,1)S(1)}, u32[]{:S(2)}, u32[]{:S(2)}) collective-permute-start(bf16[64,768]{1,0:T(8,128)(2,1)S(1)} %get-tuple-element.32), channel_id=1, source_target_pairs={{0,8},{4,12},{8,0},{12,4},{16,24},{20,28},{24,16},{28,20},{1,9},{5... | collective-permute-start | bytes 294920 | tf_op jit(solution)/shard_map/ppermute | solution.py:363
  4.5 2.6 %collective-permute-start.1 = (bf16[64,768]{1,0:T(8,128)(2,1)S(1)}, bf16[64,768]{1,0:T(8,128)(2,1)S(1)}, u32[]{:S(2)}, u32[]{:S(2)}) collective-permute-start(bf16[64,768]{1,0:T(8,128)(2,1)S(1)} %get-tuple-element.33), channel_id=1, source_target_pairs={{0,16},{4,20},{8,24},{12,28},{16,0},{20,4},{24,8},{28,12},{1,17},{... | collective-permute-start | bytes 294920 | tf_op jit(solution)/shard_map/ppermute | solution.py:363
  7.1 1.3 %collective-permute-start.2 = (bf16[64,768]{1,0:T(8,128)(2,1)S(1)}, bf16[64,768]{1,0:T(8,128)(2,1)S(1)}, u32[]{:S(2)}, u32[]{:S(2)}) collective-permute-start(bf16[64,768]{1,0:T(8,128)(2,1)S(1)} %get-tuple-element.34), channel_id=1, source_target_pairs={{0,20},{4,16},{8,28},{12,24},{16,4},{20,0},{24,12},{28,8},{1,21},{... | collective-permute-start | bytes 294920 | tf_op jit(solution)/shard_map/ppermute | solution.py:363
  8.4 2.5 %collective-permute-start.3 = (bf16[64,768]{1,0:T(8,128)(2,1)S(1)}, bf16[64,768]{1,0:T(8,128)(2,1)S(1)}, u32[]{:S(2)}, u32[]{:S(2)}) collective-permute-start(bf16[64,768]{1,0:T(8,128)(2,1)S(1)} %get-tuple-element.35), channel_id=1, source_target_pairs={{0,24},{4,28},{8,16},{12,20},{16,8},{20,12},{24,0},{28,4},{1,25},{... | collective-permute-start | bytes 294920 | tf_op jit(solution)/shard_map/ppermute | solution.py:363
  10.9 1.3 %collective-permute-start.4 = (bf16[64,768]{1,0:T(8,128)(2,1)S(1)}, bf16[64,768]{1,0:T(8,128)(2,1)S(1)}, u32[]{:S(2)}, u32[]{:S(2)}) collective-permute-start(bf16[64,768]{1,0:T(8,128)(2,1)S(1)} %get-tuple-element.36), channel_id=1, source_target_pairs={{0,28},{4,24},{8,20},{12,16},{16,12},{20,8},{24,4},{28,0},{1,29},{... | collective-permute-start | bytes 294920 | tf_op jit(solution)/shard_map/ppermute | solution.py:363
  12.2 0.8 %concatenate.3 = f32[1560]{0:T(1024)S(1)} concatenate(f32[768]{0:T(1024)} %param.10, f32[768]{0:T(1024)} %param.14, f32[12]{0:T(128)} %param.13, f32[12]{0:T(128)} %param.17), dimensions={0} | concatenate | bytes 12480 | tf_op jit(solution)/shard_map/concatenate | solution.py:302
  13.0 0.1 shard_map.91
  13.1 0.0 collective-permute-done.refs_1_.refs_2_
  13.1 0.4 collective-permute-start.5
  13.4 4.5 %collective-permute-done.1.refs_2_.refs_3_ = bf16[64,768]{1,0:T(8,128)(2,1)S(1)} collective-permute-done((bf16[64,768]{1,0:T(8,128)(2,1)S(1)}, bf16[64,768]{1,0:T(8,128)(2,1)S(1)}, u32[]{:S(2)}, u32[]{:S(2)}) %collective-permute-start.1) | collective-permute-done | bytes 98336 | tf_op jit(solution)/shard_map/ppermute | solution.py:363
  18.0 2.2 %collective-permute-start.6 = (bf16[64,768]{1,0:T(8,128)(2,1)S(1)}, bf16[64,768]{1,0:T(8,128)(2,1)S(1)}, u32[]{:S(2)}, u32[]{:S(2)}) collective-permute-start(bf16[64,768]{1,0:T(8,128)(2,1)S(1)} %get-tuple-element.38), channel_id=1, source_target_pairs={{0,4},{4,0},{8,12},{12,8},{16,20},{20,16},{24,28},{28,24},{1,5},{5... | collective-permute-start | bytes 294920 | tf_op jit(solution)/shard_map/ppermute | solution.py:363
  20.2 1.7 %collective-permute-done.2.refs_3_.refs_4_ = bf16[64,768]{1,0:T(8,128)(2,1)S(1)} collective-permute-done((bf16[64,768]{1,0:T(8,128)(2,1)S(1)}, bf16[64,768]{1,0:T(8,128)(2,1)S(1)}, u32[]{:S(2)}, u32[]{:S(2)}) %collective-permute-start.2) | collective-permute-done | bytes 98336 | tf_op jit(solution)/shard_map/ppermute | solution.py:363
  22.0 1.5 %shard_map.93.refs_0_ = bf16[2304,256]{1,0:T(8,128)(2,1)S(1)} custom-call(f32[1,768]{1,0:T(1,128)S(1)} %get-tuple-element.30.gain_ref, bf16[768,2304]{1,0:T(8,128)(2,1)S(1)} %copy-done.2, bf16[64,768]{1,0:T(8,128)(2,1)S(1)} %get-tuple-element.31.refs_0_.refs_1_, bf16[64,768]{1,0:T(8,128)(2,1)S(1)} %collective-permute-done.refs_1_.refs_2_, ...), custom_call_target="tpu_custom_call" | custom-call | flops 5000000000 | bytes 7000000 | tf_op jit(solution)/shard_map/pallas_call | solution.py:321
  23.5 0.0 collective-permute-done.5.refs_7_
  23.5 0.5 collective-permute-done.6.refs_8_
  24.0 4.0 %shard_map.94 = bf16[512,768]{1,0:T(8,128)(2,1)S(1)} custom-call(f32[12,128]{1,0:T(8,128)S(1)} %get-tuple-element.29.scale_ref, f32[1,768]{1,0:T(1,128)S(1)} %get-tuple-element.30.gain_ref, bf16[768,2304]{1,0:T(8,128)(2,1)S(1)} %copy-done.2, bf16[768,768]{1,0:T(8,128)(2,1)S(1)} %copy-done.4, bf16[2304,256]{1,0:T(8,128)(2,1)S(1)} %shard_map.93.refs_0_, ...), custom_call_target="tpu_custom_call" | custom-call | flops 10000000000 | bytes 10000000 | tf_op jit(solution)/shard_map/pallas_call | solution.py:307
  28.0 0.0 copy-start
  28.0 25.1 %all_to_all.5 = bf16[32,16,768]{2,1,0:T(8,128)(2,1)S(1)} all-to-all(bf16[32,16,768]{2,1,0:T(8,128)(2,1)S(1)} %bitcast.8), channel_id=1, replica_groups=mesh['tm'=8,'patch'=4] {'tm','patch'}, dimensions={0} | all-to-all | bytes 1572864 | tf_op jit(solution)/shard_map/all_to_all | solution.py:411
  53.1 2.3 %shard_map.96 = (bf16[64,768]{1,0:T(8,128)(2,1)S(1)}, bf16[64,768]{1,0:T(8,128)(2,1)S(1)}, bf16[2304,256]{1,0:T(8,128)(2,1)S(1)}, f32[128,768]{1,0:T(8,128)S(1)}) custom-call(f32[12,128]{1,0:T(8,128)S(1)} %get-tuple-element.27.scale_ref, f32[1,768]{1,0:T(1,128)S(1)} %get-tuple-element.28.gain_ref, bf16[768,2304]{1,0:T(8,128)(2,1)S(1)} %copy-done.3, ...), custom_call_target="tpu_custom_call" | custom-call | flops 10000000000 | bytes 10000000 | tf_op jit(solution)/shard_map/pallas_call | solution.py:307
  55.4 1.5 %collective-permute-start.10 = (bf16[1,64,768]{2,1,0:T(8,128)(2,1)S(1)}, bf16[1,64,768]{2,1,0:T(8,128)(2,1)S(1)}, u32[]{:S(2)}, u32[]{:S(2)}) collective-permute-start(bf16[1,64,768]{2,1,0:T(8,128)(2,1)S(1)} %bitcast.12), channel_id=1, source_target_pairs={{0,2},{1,3},{2,0},{3,1},{4,6},{5,7},{6,4},{7,5},{8,10},{9,11},{10,... | collective-permute-start | bytes 294920 | tf_op jit(solution)/shard_map/ppermute | solution.py:363
  57.0 2.3 %shard_map.95 = (bf16[64,768]{1,0:T(8,128)(2,1)S(1)}, bf16[64,768]{1,0:T(8,128)(2,1)S(1)}, bf16[2304,256]{1,0:T(8,128)(2,1)S(1)}, f32[128,768]{1,0:T(8,128)S(1)}) custom-call(f32[12,128]{1,0:T(8,128)S(1)} %get-tuple-element.27.scale_ref, f32[1,768]{1,0:T(1,128)S(1)} %get-tuple-element.28.gain_ref, bf16[768,2304]{1,0:T(8,128)(2,1)S(1)} %copy-done.3, ...), custom_call_target="tpu_custom_call" | custom-call | flops 10000000000 | bytes 10000000 | tf_op jit(solution)/shard_map/pallas_call | solution.py:307
  59.3 1.6 %collective-permute-start.7 = (bf16[1,64,768]{2,1,0:T(8,128)(2,1)S(1)}, bf16[1,64,768]{2,1,0:T(8,128)(2,1)S(1)}, u32[]{:S(2)}, u32[]{:S(2)}) collective-permute-start(bf16[1,64,768]{2,1,0:T(8,128)(2,1)S(1)} %bitcast.10), channel_id=1, source_target_pairs={{0,2},{1,3},{2,0},{3,1},{4,6},{5,7},{6,4},{7,5},{8,10},{9,11},{10,... | collective-permute-start | bytes 294920 | tf_op jit(solution)/shard_map/ppermute | solution.py:363
  60.9 0.5 collective-permute-start.8
  61.4 2.1 %shard_map.97 = (bf16[2,64,768]{2,1,0:T(8,128)(2,1)S(1)}, bf16[2,64,768]{2,1,0:T(8,128)(2,1)S(1)}) custom-call(f32[12,128]{1,0:T(8,128)S(1)} %get-tuple-element.27.scale_ref, bf16[768,768]{1,0:T(8,128)(2,1)S(1)} %copy-done, bf16[2304,256]{1,0:T(8,128)(2,1)S(1)} %get-tuple-element.41.refs_0_, f32[128,768]{1,0:T(8,128)S(1)} %get-tuple-element.42.refs_1_, ...), custom_call_target="tpu_custom_call" | custom-call | flops 1000000 | bytes 1000 | tf_op jit(solution)/shard_map/pallas_call | solution.py:307
  63.5 0.2 collective-permute-start.9
  63.7 0.7 %shard_map.98.refs_2_ = bf16[8,64,768]{2,1,0:T(8,128)(2,1)} custom-call(bf16[1,64,768]{2,1,0:T(8,128)(2,1)S(1)} %collective-permute-done.10.refs_0_, bf16[1,64,768]{2,1,0:T(8,128)(2,1)S(1)} %collective-permute-done.11.refs_1_), custom_call_target="tpu_custom_call" | custom-call | flops 10000000000 | bytes 1000000 | tf_op jit(solution)/shard_map/pallas_call | solution.py:349
  64.4 0.6 collective-permute-done.9.refs_1_
  65.0 0.8 %shard_map.99.refs_2_ = bf16[8,64,768]{2,1,0:T(8,128)(2,1)} custom-call(bf16[2,64,768]{2,1,0:T(8,128)(2,1)S(1)} %get-tuple-element.45.refs_0_, bf16[2,64,768]{2,1,0:T(8,128)(2,1)S(1)} %collective-permute-done.9.refs_1_, bf16[8,64,768]{2,1,0:T(8,128)(2,1)} %shard_map.98.refs_2_), custom_call_target="tpu_custom_call", output_to_operand_aliasing={{}: (2, {})} | custom-call | flops 1000000 | bytes 100 | tf_op jit(solution)/shard_map/pallas_call | solution.py:349
  65.8 0.7 %collective-permute-done.8.refs_1_ = bf16[1,64,768]{2,1,0:T(8,128)(2,1)S(1)} collective-permute-done((bf16[1,64,768]{2,1,0:T(8,128)(2,1)S(1)}, bf16[1,64,768]{2,1,0:T(8,128)(2,1)S(1)}, u32[]{:S(2)}, u32[]{:S(2)}) %collective-permute-start.8) | collective-permute-done | bytes 98336 | tf_op jit(solution)/shard_map/ppermute | solution.py:363
  66.5 0.7 %shard_map.100 = bf16[8,64,768]{2,1,0:T(8,128)(2,1)} custom-call(bf16[1,64,768]{2,1,0:T(8,128)(2,1)S(1)} %collective-permute-done.7.refs_0_, bf16[1,64,768]{2,1,0:T(8,128)(2,1)S(1)} %collective-permute-done.8.refs_1_, bf16[8,64,768]{2,1,0:T(8,128)(2,1)} %shard_map.99.refs_2_), custom_call_target="tpu_custom_call", output_to_operand_aliasing={{}: (2, {})} | custom-call | flops 10000000000 | bytes 1000000 | tf_op jit(solution)/shard_map/pallas_call | solution.py:349
  (15 shorter events, 0.0 us)
Async XLA Ops:
  0.0 1.1 %copy-start.1 = (bf16[8,64,768]{2,1,0:T(8,128)(2,1)S(1)}, bf16[8,64,768]{2,1,0:T(8,128)(2,1)}, u32[]{:S(2)}) copy-start(bf16[8,64,768]{2,1,0:T(8,128)(2,1)} %tokens_ref.1) | copy-start | bytes 2359300
  1.4 11.6 %collective-permute-start = (bf16[64,768]{1,0:T(8,128)(2,1)S(1)}, bf16[64,768]{1,0:T(8,128)(2,1)S(1)}, u32[]{:S(2)}, u32[]{:S(2)}) collective-permute-start(bf16[64,768]{1,0:T(8,128)(2,1)S(1)} %get-tuple-element.32), channel_id=1, source_target_pairs={{0,8},{4,12},{8,0},{12,4},{16,24},{20,28},{24,16},{28,20},{1,9},{5... | collective-permute-start | bytes 294920 | tf_op jit(solution)/shard_map/ppermute | solution.py:363
  4.5 13.5 %collective-permute-start.1 = (bf16[64,768]{1,0:T(8,128)(2,1)S(1)}, bf16[64,768]{1,0:T(8,128)(2,1)S(1)}, u32[]{:S(2)}, u32[]{:S(2)}) collective-permute-start(bf16[64,768]{1,0:T(8,128)(2,1)S(1)} %get-tuple-element.33), channel_id=1, source_target_pairs={{0,16},{4,20},{8,24},{12,28},{16,0},{20,4},{24,8},{28,12},{1,17},{... | collective-permute-start | bytes 294920 | tf_op jit(solution)/shard_map/ppermute | solution.py:363
  7.1 14.8 %collective-permute-start.2 = (bf16[64,768]{1,0:T(8,128)(2,1)S(1)}, bf16[64,768]{1,0:T(8,128)(2,1)S(1)}, u32[]{:S(2)}, u32[]{:S(2)}) collective-permute-start(bf16[64,768]{1,0:T(8,128)(2,1)S(1)} %get-tuple-element.34), channel_id=1, source_target_pairs={{0,20},{4,16},{8,28},{12,24},{16,4},{20,0},{24,12},{28,8},{1,21},{... | collective-permute-start | bytes 294920 | tf_op jit(solution)/shard_map/ppermute | solution.py:363
  8.4 15.0 %collective-permute-start.3 = (bf16[64,768]{1,0:T(8,128)(2,1)S(1)}, bf16[64,768]{1,0:T(8,128)(2,1)S(1)}, u32[]{:S(2)}, u32[]{:S(2)}) collective-permute-start(bf16[64,768]{1,0:T(8,128)(2,1)S(1)} %get-tuple-element.35), channel_id=1, source_target_pairs={{0,24},{4,28},{8,16},{12,20},{16,8},{20,12},{24,0},{28,4},{1,25},{... | collective-permute-start | bytes 294920 | tf_op jit(solution)/shard_map/ppermute | solution.py:363
  10.9 12.6 %collective-permute-start.4 = (bf16[64,768]{1,0:T(8,128)(2,1)S(1)}, bf16[64,768]{1,0:T(8,128)(2,1)S(1)}, u32[]{:S(2)}, u32[]{:S(2)}) collective-permute-start(bf16[64,768]{1,0:T(8,128)(2,1)S(1)} %get-tuple-element.36), channel_id=1, source_target_pairs={{0,28},{4,24},{8,20},{12,16},{16,12},{20,8},{24,4},{28,0},{1,29},{... | collective-permute-start | bytes 294920 | tf_op jit(solution)/shard_map/ppermute | solution.py:363
  13.0 9.0 %copy-start.2 = (bf16[768,2304]{1,0:T(8,128)(2,1)S(1)}, bf16[768,2304]{1,0:T(8,128)(2,1)}, u32[]{:S(2)}) copy-start(bf16[768,2304]{1,0:T(8,128)(2,1)} %proj_ref.5) | copy-start | bytes 10616836
  13.1 10.4 %collective-permute-start.5 = (bf16[64,768]{1,0:T(8,128)(2,1)S(1)}, bf16[64,768]{1,0:T(8,128)(2,1)S(1)}, u32[]{:S(2)}, u32[]{:S(2)}) collective-permute-start(bf16[64,768]{1,0:T(8,128)(2,1)S(1)} %get-tuple-element.37), channel_id=1, source_target_pairs={{0,12},{4,8},{8,4},{12,0},{16,28},{20,24},{24,20},{28,16},{1,13},{... | collective-permute-start | bytes 294920 | tf_op jit(solution)/shard_map/ppermute | solution.py:363
  18.0 6.0 %collective-permute-start.6 = (bf16[64,768]{1,0:T(8,128)(2,1)S(1)}, bf16[64,768]{1,0:T(8,128)(2,1)S(1)}, u32[]{:S(2)}, u32[]{:S(2)}) collective-permute-start(bf16[64,768]{1,0:T(8,128)(2,1)S(1)} %get-tuple-element.38), channel_id=1, source_target_pairs={{0,4},{4,0},{8,12},{12,8},{16,20},{20,16},{24,28},{28,24},{1,5},{5... | collective-permute-start | bytes 294920 | tf_op jit(solution)/shard_map/ppermute | solution.py:363
  22.0 2.1 %copy-start.4 = (bf16[768,768]{1,0:T(8,128)(2,1)S(1)}, bf16[768,768]{1,0:T(8,128)(2,1)}, u32[]{:S(2)}) copy-start(bf16[768,768]{1,0:T(8,128)(2,1)} %out_ref.4) | copy-start | bytes 3538948
  24.0 29.1 %copy-start.3 = (bf16[768,2304]{1,0:T(8,128)(2,1)S(1)}, bf16[768,2304]{1,0:T(8,128)(2,1)}, u32[]{:S(2)}) copy-start(bf16[768,2304]{1,0:T(8,128)(2,1)} %proj_ref.7) | copy-start | bytes 10616836
  28.0 25.1 %copy-start = (bf16[768,768]{1,0:T(8,128)(2,1)S(1)}, bf16[768,768]{1,0:T(8,128)(2,1)}, u32[]{:S(2)}) copy-start(bf16[768,768]{1,0:T(8,128)(2,1)} %out_ref.7) | copy-start | bytes 3538948
  55.4 8.3 %collective-permute-start.10 = (bf16[1,64,768]{2,1,0:T(8,128)(2,1)S(1)}, bf16[1,64,768]{2,1,0:T(8,128)(2,1)S(1)}, u32[]{:S(2)}, u32[]{:S(2)}) collective-permute-start(bf16[1,64,768]{2,1,0:T(8,128)(2,1)S(1)} %bitcast.12), channel_id=1, source_target_pairs={{0,2},{1,3},{2,0},{3,1},{4,6},{5,7},{6,4},{7,5},{8,10},{9,11},{10,... | collective-permute-start | bytes 294920 | tf_op jit(solution)/shard_map/ppermute | solution.py:363
  57.0 6.8 %collective-permute-start.11 = (bf16[1,64,768]{2,1,0:T(8,128)(2,1)S(1)}, bf16[1,64,768]{2,1,0:T(8,128)(2,1)S(1)}, u32[]{:S(2)}, u32[]{:S(2)}) collective-permute-start(bf16[1,64,768]{2,1,0:T(8,128)(2,1)S(1)} %bitcast.11), channel_id=1, source_target_pairs={{0,3},{1,2},{2,1},{3,0},{4,7},{5,6},{6,5},{7,4},{8,11},{9,10},{10,... | collective-permute-start | bytes 294920 | tf_op jit(solution)/shard_map/ppermute | solution.py:363
  59.3 6.5 %collective-permute-start.7 = (bf16[1,64,768]{2,1,0:T(8,128)(2,1)S(1)}, bf16[1,64,768]{2,1,0:T(8,128)(2,1)S(1)}, u32[]{:S(2)}, u32[]{:S(2)}) collective-permute-start(bf16[1,64,768]{2,1,0:T(8,128)(2,1)S(1)} %bitcast.10), channel_id=1, source_target_pairs={{0,2},{1,3},{2,0},{3,1},{4,6},{5,7},{6,4},{7,5},{8,10},{9,11},{10,... | collective-permute-start | bytes 294920 | tf_op jit(solution)/shard_map/ppermute | solution.py:363
  60.9 5.7 %collective-permute-start.8 = (bf16[1,64,768]{2,1,0:T(8,128)(2,1)S(1)}, bf16[1,64,768]{2,1,0:T(8,128)(2,1)S(1)}, u32[]{:S(2)}, u32[]{:S(2)}) collective-permute-start(bf16[1,64,768]{2,1,0:T(8,128)(2,1)S(1)} %bitcast.9), channel_id=1, source_target_pairs={{0,3},{1,2},{2,1},{3,0},{4,7},{5,6},{6,5},{7,4},{8,11},{9,10},{10,... | collective-permute-start | bytes 294920 | tf_op jit(solution)/shard_map/ppermute | solution.py:363
  63.5 1.5 %collective-permute-start.9 = (bf16[2,64,768]{2,1,0:T(8,128)(2,1)S(1)}, bf16[2,64,768]{2,1,0:T(8,128)(2,1)S(1)}, u32[]{:S(2)}, u32[]{:S(2)}) collective-permute-start(bf16[2,64,768]{2,1,0:T(8,128)(2,1)S(1)} %get-tuple-element.46), channel_id=1, source_target_pairs={{0,1},{1,0},{2,3},{3,2},{4,5},{5,4},{6,7},{7,6},{8,9},{9,8},{10,11... | collective-permute-start | bytes 589832 | tf_op jit(solution)/shard_map/ppermute | solution.py:363

commit v9 on v8

--- a/solution.py
+++ b/solution.py
@@ -237,7 +237,7 @@
     stream = tokens[half:] + dot(mixed[...], out_ref[...], TN)
     for index, target in enumerate(pieces):
         target[...] = stream[index * side_patches : (index + 1) * side_patches].astype(jnp.bfloat16)
-    kept[...] = tokens[:half]
+    kept[...] = tokens[:half].astype(jnp.bfloat16)
 
 
 def near_kernel(frames, scale_ref, out_ref, *refs):
@@ -246,7 +246,7 @@
     for frame in range(frames):
         fields, kept = refs[2 * frame : 2 * frame + 2]
         attend_lanes(fields, scale_ref, mixed, *work, slice(0, kept.shape[0]))
-        stream = kept[...] + dot(mixed[...], out_ref[...], TN)
+        stream = kept[...].astype(jnp.float32) + dot(mixed[...], out_ref[...], TN)
         for index, target in enumerate(pieces):
             target[frame] = stream[index * side_patches : (index + 1) * side_patches].astype(jnp.bfloat16)
 
@@ -425,7 +425,7 @@
         *pieces, fields, tokens_near = call(
             functools.partial(space_kernel, frame, senders, sides, own_frames),
             [(piece, jnp.bfloat16)] * half
-            + [((3 * width, columns), jnp.bfloat16), ((near_rows, width), jnp.float32)],
+            + [((3 * width, columns), jnp.bfloat16), ((near_rows, width), jnp.bfloat16)],
             [held, pltpu.VMEM((columns, width), jnp.float32)] + work,
             10**10,
             space_scale, space_gain, space_proj, space_out, stream,

time: 67.6 us -> 67.6 us (level)
  no operation moved by 1% of the time
where the time goes in v9:
time: 67.6 us; the launch traced here: 67.4 us
  blocking collectives  25.1 us (37%)
  starting transfers between devices  17.2 us (25%)
  Pallas kernels  14.8 us (22%)
  waiting for transfers between devices  8.12 us (12%)
  local copies, waits for them, and re-layouts  1.93 us (3%)
    all_to_all x1, blocking collectives, per_device(): lax.all_to_all(stream.reshape(senders, rows // senders, width), ('tm', 'p...  25.1 us
    ppermute x12, starting transfers between devices, exchange(): return lax.ppermute(piece, axis, [(i, i ^ index) for i in range(size)])  17.2 us
    pallas_call x4, Pallas kernels, call(): pl.pallas_call(kernel, out_shape=[jax.ShapeDtypeStruct(*shape) for shape...  10.8 us
    ppermute x12, waiting for transfers between devices, exchange(): return lax.ppermute(piece, axis, [(i, i ^ index) for i in range(size)])  8.12 us
    pallas_call x3, Pallas kernels, place(): pl.pallas_call(functools.partial(place_kernel, places), out_shape=jax.Sha...  2.14 us
    pallas_call x1, Pallas kernels, project_early(): pl.pallas_call(functools.partial(fields_kernel, patches), out_shape=jax.S...  1.5 us
  transfers between devices with their start and end apart: 12, of which 5 were waited for; matrix products, arithmetic and copies ran while one was open for 1% of the time, Pallas kernels for 11%

profile of v9, /device:TPU:0, one launch (start us, length us, event | category | flops | bytes accessed | tf_op | source)
XLA Modules:
  0.0 67.4 jit_solution(7598011970795232779)
XLA Ops:
  0.0 1.1 %copy-done.1 = bf16[8,64,768]{2,1,0:T(8,128)(2,1)S(1)} copy-done((bf16[8,64,768]{2,1,0:T(8,128)(2,1)S(1)}, bf16[8,64,768]{2,1,0:T(8,128)(2,1)}, u32[]{:S(2)}) %copy-start.1) | copy-done | bytes 786456
  1.1 0.3 shard_map.92
  1.4 3.1 %collective-permute-start = (bf16[64,768]{1,0:T(8,128)(2,1)S(1)}, bf16[64,768]{1,0:T(8,128)(2,1)S(1)}, u32[]{:S(2)}, u32[]{:S(2)}) collective-permute-start(bf16[64,768]{1,0:T(8,128)(2,1)S(1)} %get-tuple-element.32), channel_id=1, source_target_pairs={{0,8},{4,12},{8,0},{12,4},{16,24},{20,28},{24,16},{28,20},{1,9},{5... | collective-permute-start | bytes 294920 | tf_op jit(solution)/shard_map/ppermute | solution.py:363
  4.5 2.6 %collective-permute-start.1 = (bf16[64,768]{1,0:T(8,128)(2,1)S(1)}, bf16[64,768]{1,0:T(8,128)(2,1)S(1)}, u32[]{:S(2)}, u32[]{:S(2)}) collective-permute-start(bf16[64,768]{1,0:T(8,128)(2,1)S(1)} %get-tuple-element.33), channel_id=1, source_target_pairs={{0,16},{4,20},{8,24},{12,28},{16,0},{20,4},{24,8},{28,12},{1,17},{... | collective-permute-start | bytes 294920 | tf_op jit(solution)/shard_map/ppermute | solution.py:363
  7.1 1.3 %collective-permute-start.2 = (bf16[64,768]{1,0:T(8,128)(2,1)S(1)}, bf16[64,768]{1,0:T(8,128)(2,1)S(1)}, u32[]{:S(2)}, u32[]{:S(2)}) collective-permute-start(bf16[64,768]{1,0:T(8,128)(2,1)S(1)} %get-tuple-element.34), channel_id=1, source_target_pairs={{0,20},{4,16},{8,28},{12,24},{16,4},{20,0},{24,12},{28,8},{1,21},{... | collective-permute-start | bytes 294920 | tf_op jit(solution)/shard_map/ppermute | solution.py:363
  8.4 2.5 %collective-permute-start.3 = (bf16[64,768]{1,0:T(8,128)(2,1)S(1)}, bf16[64,768]{1,0:T(8,128)(2,1)S(1)}, u32[]{:S(2)}, u32[]{:S(2)}) collective-permute-start(bf16[64,768]{1,0:T(8,128)(2,1)S(1)} %get-tuple-element.35), channel_id=1, source_target_pairs={{0,24},{4,28},{8,16},{12,20},{16,8},{20,12},{24,0},{28,4},{1,25},{... | collective-permute-start | bytes 294920 | tf_op jit(solution)/shard_map/ppermute | solution.py:363
  10.9 1.3 %collective-permute-start.4 = (bf16[64,768]{1,0:T(8,128)(2,1)S(1)}, bf16[64,768]{1,0:T(8,128)(2,1)S(1)}, u32[]{:S(2)}, u32[]{:S(2)}) collective-permute-start(bf16[64,768]{1,0:T(8,128)(2,1)S(1)} %get-tuple-element.36), channel_id=1, source_target_pairs={{0,28},{4,24},{8,20},{12,16},{16,12},{20,8},{24,4},{28,0},{1,29},{... | collective-permute-start | bytes 294920 | tf_op jit(solution)/shard_map/ppermute | solution.py:363
  12.2 0.8 %concatenate.3 = f32[1560]{0:T(1024)S(1)} concatenate(f32[768]{0:T(1024)} %param.10, f32[768]{0:T(1024)} %param.14, f32[12]{0:T(128)} %param.13, f32[12]{0:T(128)} %param.17), dimensions={0} | concatenate | bytes 12480 | tf_op jit(solution)/shard_map/concatenate | solution.py:302
  13.0 0.1 shard_map.91
  13.1 0.0 collective-permute-done.refs_1_.refs_2_
  13.1 0.4 collective-permute-start.5
  13.4 4.5 %collective-permute-done.1.refs_2_.refs_3_ = bf16[64,768]{1,0:T(8,128)(2,1)S(1)} collective-permute-done((bf16[64,768]{1,0:T(8,128)(2,1)S(1)}, bf16[64,768]{1,0:T(8,128)(2,1)S(1)}, u32[]{:S(2)}, u32[]{:S(2)}) %collective-permute-start.1) | collective-permute-done | bytes 98336 | tf_op jit(solution)/shard_map/ppermute | solution.py:363
  18.0 2.2 %collective-permute-start.6 = (bf16[64,768]{1,0:T(8,128)(2,1)S(1)}, bf16[64,768]{1,0:T(8,128)(2,1)S(1)}, u32[]{:S(2)}, u32[]{:S(2)}) collective-permute-start(bf16[64,768]{1,0:T(8,128)(2,1)S(1)} %get-tuple-element.38), channel_id=1, source_target_pairs={{0,4},{4,0},{8,12},{12,8},{16,20},{20,16},{24,28},{28,24},{1,5},{5... | collective-permute-start | bytes 294920 | tf_op jit(solution)/shard_map/ppermute | solution.py:363
  20.2 1.7 %collective-permute-done.2.refs_3_.refs_4_ = bf16[64,768]{1,0:T(8,128)(2,1)S(1)} collective-permute-done((bf16[64,768]{1,0:T(8,128)(2,1)S(1)}, bf16[64,768]{1,0:T(8,128)(2,1)S(1)}, u32[]{:S(2)}, u32[]{:S(2)}) %collective-permute-start.2) | collective-permute-done | bytes 98336 | tf_op jit(solution)/shard_map/ppermute | solution.py:363
  22.0 1.5 %shard_map.93.refs_0_ = bf16[2304,256]{1,0:T(8,128)(2,1)S(1)} custom-call(f32[1,768]{1,0:T(1,128)S(1)} %get-tuple-element.30.gain_ref, bf16[768,2304]{1,0:T(8,128)(2,1)S(1)} %copy-done.2, bf16[64,768]{1,0:T(8,128)(2,1)S(1)} %get-tuple-element.31.refs_0_.refs_1_, bf16[64,768]{1,0:T(8,128)(2,1)S(1)} %collective-permute-done.refs_1_.refs_2_, ...), custom_call_target="tpu_custom_call" | custom-call | flops 5000000000 | bytes 7000000 | tf_op jit(solution)/shard_map/pallas_call | solution.py:321
  23.5 0.0 collective-permute-done.3.refs_5_
  23.5 0.5 collective-permute-done.6.refs_8_
  24.0 4.0 %shard_map.94 = bf16[512,768]{1,0:T(8,128)(2,1)S(1)} custom-call(f32[12,128]{1,0:T(8,128)S(1)} %get-tuple-element.29.scale_ref, f32[1,768]{1,0:T(1,128)S(1)} %get-tuple-element.30.gain_ref, bf16[768,2304]{1,0:T(8,128)(2,1)S(1)} %copy-done.2, bf16[768,768]{1,0:T(8,128)(2,1)S(1)} %copy-done.4, bf16[2304,256]{1,0:T(8,128)(2,1)S(1)} %shard_map.93.refs_0_, ...), custom_call_target="tpu_custom_call" | custom-call | flops 10000000000 | bytes 10000000 | tf_op jit(solution)/shard_map/pallas_call | solution.py:307
  28.0 0.0 copy-start
  28.0 25.1 %all_to_all.5 = bf16[32,16,768]{2,1,0:T(8,128)(2,1)S(1)} all-to-all(bf16[32,16,768]{2,1,0:T(8,128)(2,1)S(1)} %bitcast.8), channel_id=1, replica_groups=mesh['tm'=8,'patch'=4] {'tm','patch'}, dimensions={0} | all-to-all | bytes 1572864 | tf_op jit(solution)/shard_map/all_to_all | solution.py:411
  53.1 2.3 %shard_map.96 = (bf16[64,768]{1,0:T(8,128)(2,1)S(1)}, bf16[64,768]{1,0:T(8,128)(2,1)S(1)}, bf16[2304,256]{1,0:T(8,128)(2,1)S(1)}, bf16[128,768]{1,0:T(8,128)(2,1)S(1)}) custom-call(f32[12,128]{1,0:T(8,128)S(1)} %get-tuple-element.27.scale_ref, f32[1,768]{1,0:T(1,128)S(1)} %get-tuple-element.28.gain_ref, bf16[768,2304]{1,0:T(8,128)(2,1)S(1)} %copy-done.3, ...), custom_call_target="tpu_custom_call" | custom-call | flops 10000000000 | bytes 10000000 | tf_op jit(solution)/shard_map/pallas_call | solution.py:307
  55.4 1.5 %collective-permute-start.10 = (bf16[1,64,768]{2,1,0:T(8,128)(2,1)S(1)}, bf16[1,64,768]{2,1,0:T(8,128)(2,1)S(1)}, u32[]{:S(2)}, u32[]{:S(2)}) collective-permute-start(bf16[1,64,768]{2,1,0:T(8,128)(2,1)S(1)} %bitcast.12), channel_id=1, source_target_pairs={{0,2},{1,3},{2,0},{3,1},{4,6},{5,7},{6,4},{7,5},{8,10},{9,11},{10,... | collective-permute-start | bytes 294920 | tf_op jit(solution)/shard_map/ppermute | solution.py:363
  57.0 2.3 %shard_map.95 = (bf16[64,768]{1,0:T(8,128)(2,1)S(1)}, bf16[64,768]{1,0:T(8,128)(2,1)S(1)}, bf16[2304,256]{1,0:T(8,128)(2,1)S(1)}, bf16[128,768]{1,0:T(8,128)(2,1)S(1)}) custom-call(f32[12,128]{1,0:T(8,128)S(1)} %get-tuple-element.27.scale_ref, f32[1,768]{1,0:T(1,128)S(1)} %get-tuple-element.28.gain_ref, bf16[768,2304]{1,0:T(8,128)(2,1)S(1)} %copy-done.3, ...), custom_call_target="tpu_custom_call" | custom-call | flops 10000000000 | bytes 10000000 | tf_op jit(solution)/shard_map/pallas_call | solution.py:307
  59.3 1.6 %collective-permute-start.7 = (bf16[1,64,768]{2,1,0:T(8,128)(2,1)S(1)}, bf16[1,64,768]{2,1,0:T(8,128)(2,1)S(1)}, u32[]{:S(2)}, u32[]{:S(2)}) collective-permute-start(bf16[1,64,768]{2,1,0:T(8,128)(2,1)S(1)} %bitcast.10), channel_id=1, source_target_pairs={{0,2},{1,3},{2,0},{3,1},{4,6},{5,7},{6,4},{7,5},{8,10},{9,11},{10,... | collective-permute-start | bytes 294920 | tf_op jit(solution)/shard_map/ppermute | solution.py:363
  60.9 0.5 collective-permute-start.8
  61.4 2.1 %shard_map.97 = (bf16[2,64,768]{2,1,0:T(8,128)(2,1)S(1)}, bf16[2,64,768]{2,1,0:T(8,128)(2,1)S(1)}) custom-call(f32[12,128]{1,0:T(8,128)S(1)} %get-tuple-element.27.scale_ref, bf16[768,768]{1,0:T(8,128)(2,1)S(1)} %copy-done, bf16[2304,256]{1,0:T(8,128)(2,1)S(1)} %get-tuple-element.41.refs_0_, bf16[128,768]{1,0:T(8,128)(2,1)S(1)} %get-tuple-element.42.refs_1_, ...), custom_call_target="tpu_custom_call" | custom-call | flops 1000000 | bytes 1000 | tf_op jit(solution)/shard_map/pallas_call | solution.py:307
  63.5 0.2 collective-permute-start.9
  63.8 0.7 %shard_map.98.refs_2_ = bf16[8,64,768]{2,1,0:T(8,128)(2,1)} custom-call(bf16[1,64,768]{2,1,0:T(8,128)(2,1)S(1)} %collective-permute-done.10.refs_0_, bf16[1,64,768]{2,1,0:T(8,128)(2,1)S(1)} %collective-permute-done.11.refs_1_), custom_call_target="tpu_custom_call" | custom-call | flops 10000000000 | bytes 1000000 | tf_op jit(solution)/shard_map/pallas_call | solution.py:349
  64.5 0.6 collective-permute-done.9.refs_1_
  65.1 0.8 %shard_map.99.refs_2_ = bf16[8,64,768]{2,1,0:T(8,128)(2,1)} custom-call(bf16[2,64,768]{2,1,0:T(8,128)(2,1)S(1)} %get-tuple-element.45.refs_0_, bf16[2,64,768]{2,1,0:T(8,128)(2,1)S(1)} %collective-permute-done.9.refs_1_, bf16[8,64,768]{2,1,0:T(8,128)(2,1)} %shard_map.98.refs_2_), custom_call_target="tpu_custom_call", output_to_operand_aliasing={{}: (2, {})} | custom-call | flops 1000000 | bytes 100 | tf_op jit(solution)/shard_map/pallas_call | solution.py:349
  65.8 0.7 %collective-permute-done.8.refs_1_ = bf16[1,64,768]{2,1,0:T(8,128)(2,1)S(1)} collective-permute-done((bf16[1,64,768]{2,1,0:T(8,128)(2,1)S(1)}, bf16[1,64,768]{2,1,0:T(8,128)(2,1)S(1)}, u32[]{:S(2)}, u32[]{:S(2)}) %collective-permute-start.8) | collective-permute-done | bytes 98336 | tf_op jit(solution)/shard_map/ppermute | solution.py:363
  66.6 0.7 %shard_map.100 = bf16[8,64,768]{2,1,0:T(8,128)(2,1)} custom-call(bf16[1,64,768]{2,1,0:T(8,128)(2,1)S(1)} %collective-permute-done.7.refs_0_, bf16[1,64,768]{2,1,0:T(8,128)(2,1)S(1)} %collective-permute-done.8.refs_1_, bf16[8,64,768]{2,1,0:T(8,128)(2,1)} %shard_map.99.refs_2_), custom_call_target="tpu_custom_call", output_to_operand_aliasing={{}: (2, {})} | custom-call | flops 10000000000 | bytes 1000000 | tf_op jit(solution)/shard_map/pallas_call | solution.py:349
  (15 shorter events, 0.0 us)
Async XLA Ops:
  0.0 1.1 %copy-start.1 = (bf16[8,64,768]{2,1,0:T(8,128)(2,1)S(1)}, bf16[8,64,768]{2,1,0:T(8,128)(2,1)}, u32[]{:S(2)}) copy-start(bf16[8,64,768]{2,1,0:T(8,128)(2,1)} %tokens_ref.1) | copy-start | bytes 2359300
  1.4 11.6 %collective-permute-start = (bf16[64,768]{1,0:T(8,128)(2,1)S(1)}, bf16[64,768]{1,0:T(8,128)(2,1)S(1)}, u32[]{:S(2)}, u32[]{:S(2)}) collective-permute-start(bf16[64,768]{1,0:T(8,128)(2,1)S(1)} %get-tuple-element.32), channel_id=1, source_target_pairs={{0,8},{4,12},{8,0},{12,4},{16,24},{20,28},{24,16},{28,20},{1,9},{5... | collective-permute-start | bytes 294920 | tf_op jit(solution)/shard_map/ppermute | solution.py:363
  4.5 13.5 %collective-permute-start.1 = (bf16[64,768]{1,0:T(8,128)(2,1)S(1)}, bf16[64,768]{1,0:T(8,128)(2,1)S(1)}, u32[]{:S(2)}, u32[]{:S(2)}) collective-permute-start(bf16[64,768]{1,0:T(8,128)(2,1)S(1)} %get-tuple-element.33), channel_id=1, source_target_pairs={{0,16},{4,20},{8,24},{12,28},{16,0},{20,4},{24,8},{28,12},{1,17},{... | collective-permute-start | bytes 294920 | tf_op jit(solution)/shard_map/ppermute | solution.py:363
  7.1 14.8 %collective-permute-start.2 = (bf16[64,768]{1,0:T(8,128)(2,1)S(1)}, bf16[64,768]{1,0:T(8,128)(2,1)S(1)}, u32[]{:S(2)}, u32[]{:S(2)}) collective-permute-start(bf16[64,768]{1,0:T(8,128)(2,1)S(1)} %get-tuple-element.34), channel_id=1, source_target_pairs={{0,20},{4,16},{8,28},{12,24},{16,4},{20,0},{24,12},{28,8},{1,21},{... | collective-permute-start | bytes 294920 | tf_op jit(solution)/shard_map/ppermute | solution.py:363
  8.4 15.0 %collective-permute-start.3 = (bf16[64,768]{1,0:T(8,128)(2,1)S(1)}, bf16[64,768]{1,0:T(8,128)(2,1)S(1)}, u32[]{:S(2)}, u32[]{:S(2)}) collective-permute-start(bf16[64,768]{1,0:T(8,128)(2,1)S(1)} %get-tuple-element.35), channel_id=1, source_target_pairs={{0,24},{4,28},{8,16},{12,20},{16,8},{20,12},{24,0},{28,4},{1,25},{... | collective-permute-start | bytes 294920 | tf_op jit(solution)/shard_map/ppermute | solution.py:363
  10.9 12.6 %collective-permute-start.4 = (bf16[64,768]{1,0:T(8,128)(2,1)S(1)}, bf16[64,768]{1,0:T(8,128)(2,1)S(1)}, u32[]{:S(2)}, u32[]{:S(2)}) collective-permute-start(bf16[64,768]{1,0:T(8,128)(2,1)S(1)} %get-tuple-element.36), channel_id=1, source_target_pairs={{0,28},{4,24},{8,20},{12,16},{16,12},{20,8},{24,4},{28,0},{1,29},{... | collective-permute-start | bytes 294920 | tf_op jit(solution)/shard_map/ppermute | solution.py:363
  13.0 9.0 %copy-start.2 = (bf16[768,2304]{1,0:T(8,128)(2,1)S(1)}, bf16[768,2304]{1,0:T(8,128)(2,1)}, u32[]{:S(2)}) copy-start(bf16[768,2304]{1,0:T(8,128)(2,1)} %proj_ref.5) | copy-start | bytes 10616836
  13.1 10.4 %collective-permute-start.5 = (bf16[64,768]{1,0:T(8,128)(2,1)S(1)}, bf16[64,768]{1,0:T(8,128)(2,1)S(1)}, u32[]{:S(2)}, u32[]{:S(2)}) collective-permute-start(bf16[64,768]{1,0:T(8,128)(2,1)S(1)} %get-tuple-element.37), channel_id=1, source_target_pairs={{0,12},{4,8},{8,4},{12,0},{16,28},{20,24},{24,20},{28,16},{1,13},{... | collective-permute-start | bytes 294920 | tf_op jit(solution)/shard_map/ppermute | solution.py:363
  18.0 6.0 %collective-permute-start.6 = (bf16[64,768]{1,0:T(8,128)(2,1)S(1)}, bf16[64,768]{1,0:T(8,128)(2,1)S(1)}, u32[]{:S(2)}, u32[]{:S(2)}) collective-permute-start(bf16[64,768]{1,0:T(8,128)(2,1)S(1)} %get-tuple-element.38), channel_id=1, source_target_pairs={{0,4},{4,0},{8,12},{12,8},{16,20},{20,16},{24,28},{28,24},{1,5},{5... | collective-permute-start | bytes 294920 | tf_op jit(solution)/shard_map/ppermute | solution.py:363
  22.0 2.1 %copy-start.4 = (bf16[768,768]{1,0:T(8,128)(2,1)S(1)}, bf16[768,768]{1,0:T(8,128)(2,1)}, u32[]{:S(2)}) copy-start(bf16[768,768]{1,0:T(8,128)(2,1)} %out_ref.4) | copy-start | bytes 3538948
  24.0 29.1 %copy-start.3 = (bf16[768,2304]{1,0:T(8,128)(2,1)S(1)}, bf16[768,2304]{1,0:T(8,128)(2,1)}, u32[]{:S(2)}) copy-start(bf16[768,2304]{1,0:T(8,128)(2,1)} %proj_ref.7) | copy-start | bytes 10616836
  28.0 25.1 %copy-start = (bf16[768,768]{1,0:T(8,128)(2,1)S(1)}, bf16[768,768]{1,0:T(8,128)(2,1)}, u32[]{:S(2)}) copy-start(bf16[768,768]{1,0:T(8,128)(2,1)} %out_ref.7) | copy-start | bytes 3538948
  55.4 8.3 %collective-permute-start.10 = (bf16[1,64,768]{2,1,0:T(8,128)(2,1)S(1)}, bf16[1,64,768]{2,1,0:T(8,128)(2,1)S(1)}, u32[]{:S(2)}, u32[]{:S(2)}) collective-permute-start(bf16[1,64,768]{2,1,0:T(8,128)(2,1)S(1)} %bitcast.12), channel_id=1, source_target_pairs={{0,2},{1,3},{2,0},{3,1},{4,6},{5,7},{6,4},{7,5},{8,10},{9,11},{10,... | collective-permute-start | bytes 294920 | tf_op jit(solution)/shard_map/ppermute | solution.py:363
  57.0 6.8 %collective-permute-start.11 = (bf16[1,64,768]{2,1,0:T(8,128)(2,1)S(1)}, bf16[1,64,768]{2,1,0:T(8,128)(2,1)S(1)}, u32[]{:S(2)}, u32[]{:S(2)}) collective-permute-start(bf16[1,64,768]{2,1,0:T(8,128)(2,1)S(1)} %bitcast.11), channel_id=1, source_target_pairs={{0,3},{1,2},{2,1},{3,0},{4,7},{5,6},{6,5},{7,4},{8,11},{9,10},{10,... | collective-permute-start | bytes 294920 | tf_op jit(solution)/shard_map/ppermute | solution.py:363
  59.3 6.5 %collective-permute-start.7 = (bf16[1,64,768]{2,1,0:T(8,128)(2,1)S(1)}, bf16[1,64,768]{2,1,0:T(8,128)(2,1)S(1)}, u32[]{:S(2)}, u32[]{:S(2)}) collective-permute-start(bf16[1,64,768]{2,1,0:T(8,128)(2,1)S(1)} %bitcast.10), channel_id=1, source_target_pairs={{0,2},{1,3},{2,0},{3,1},{4,6},{5,7},{6,4},{7,5},{8,10},{9,11},{10,... | collective-permute-start | bytes 294920 | tf_op jit(solution)/shard_map/ppermute | solution.py:363
  60.9 5.7 %collective-permute-start.8 = (bf16[1,64,768]{2,1,0:T(8,128)(2,1)S(1)}, bf16[1,64,768]{2,1,0:T(8,128)(2,1)S(1)}, u32[]{:S(2)}, u32[]{:S(2)}) collective-permute-start(bf16[1,64,768]{2,1,0:T(8,128)(2,1)S(1)} %bitcast.9), channel_id=1, source_target_pairs={{0,3},{1,2},{2,1},{3,0},{4,7},{5,6},{6,5},{7,4},{8,11},{9,10},{10,... | collective-permute-start | bytes 294920 | tf_op jit(solution)/shard_map/ppermute | solution.py:363
  63.5 1.5 %collective-permute-start.9 = (bf16[2,64,768]{2,1,0:T(8,128)(2,1)S(1)}, bf16[2,64,768]{2,1,0:T(8,128)(2,1)S(1)}, u32[]{:S(2)}, u32[]{:S(2)}) collective-permute-start(bf16[2,64,768]{2,1,0:T(8,128)(2,1)S(1)} %get-tuple-element.46), channel_id=1, source_target_pairs={{0,1},{1,0},{2,3},{3,2},{4,5},{5,4},{6,7},{7,6},{8,9},{9,8},{10,11... | collective-permute-start | bytes 589832 | tf_op jit(solution)/shard_map/ppermute | solution.py:363

commit v10 on v8

--- a/solution.py
+++ b/solution.py
@@ -14,7 +14,7 @@
 EPSILON = 1e-06
 LOG2_E = math.log2(math.e)
 LANES = 128
-AHEAD = 12
+AHEAD = 24
 VMEM_BYTES = 24 * 1024 * 1024
 
 TN = (((0,), (0,)), ((), ()))

time: 67.6 us -> 67.5 us (level)
  no operation moved by 1% of the time
where the time goes in v10:
time: 67.5 us; the launch traced here: 67.3 us
  blocking collectives  25.1 us (37%)
  starting transfers between devices  17.2 us (25%)
  Pallas kernels  14.7 us (22%)
  waiting for transfers between devices  8.12 us (12%)
  local copies, waits for them, and re-layouts  1.93 us (3%)
    all_to_all x1, blocking collectives, per_device(): lax.all_to_all(stream.reshape(senders, rows // senders, width), ('tm', 'p...  25.1 us
    ppermute x12, starting transfers between devices, exchange(): return lax.ppermute(piece, axis, [(i, i ^ index) for i in range(size)])  17.2 us
    pallas_call x4, Pallas kernels, call(): pl.pallas_call(kernel, out_shape=[jax.ShapeDtypeStruct(*shape) for shape...  10.7 us
    ppermute x12, waiting for transfers between devices, exchange(): return lax.ppermute(piece, axis, [(i, i ^ index) for i in range(size)])  8.12 us
    pallas_call x3, Pallas kernels, place(): pl.pallas_call(functools.partial(place_kernel, places), out_shape=jax.Sha...  2.14 us
    pallas_call x1, Pallas kernels, project_early(): pl.pallas_call(functools.partial(fields_kernel, patches), out_shape=jax.S...  1.5 us
  transfers between devices with their start and end apart: 12, of which 5 were waited for; matrix products, arithmetic and copies ran while one was open for 1% of the time, Pallas kernels for 11%

profile of v10, /device:TPU:0, one launch (start us, length us, event | category | flops | bytes accessed | tf_op | source)
XLA Modules:
  0.0 67.3 jit_solution(1443174820183462391)
XLA Ops:
  0.0 1.1 %copy-done.1 = bf16[8,64,768]{2,1,0:T(8,128)(2,1)S(1)} copy-done((bf16[8,64,768]{2,1,0:T(8,128)(2,1)S(1)}, bf16[8,64,768]{2,1,0:T(8,128)(2,1)}, u32[]{:S(2)}) %copy-start.1) | copy-done | bytes 786456
  1.1 0.3 shard_map.92
  1.4 3.1 %collective-permute-start = (bf16[64,768]{1,0:T(8,128)(2,1)S(1)}, bf16[64,768]{1,0:T(8,128)(2,1)S(1)}, u32[]{:S(2)}, u32[]{:S(2)}) collective-permute-start(bf16[64,768]{1,0:T(8,128)(2,1)S(1)} %get-tuple-element.32), channel_id=1, source_target_pairs={{0,8},{4,12},{8,0},{12,4},{16,24},{20,28},{24,16},{28,20},{1,9},{5... | collective-permute-start | bytes 294920 | tf_op jit(solution)/shard_map/ppermute | solution.py:363
  4.5 2.6 %collective-permute-start.1 = (bf16[64,768]{1,0:T(8,128)(2,1)S(1)}, bf16[64,768]{1,0:T(8,128)(2,1)S(1)}, u32[]{:S(2)}, u32[]{:S(2)}) collective-permute-start(bf16[64,768]{1,0:T(8,128)(2,1)S(1)} %get-tuple-element.33), channel_id=1, source_target_pairs={{0,16},{4,20},{8,24},{12,28},{16,0},{20,4},{24,8},{28,12},{1,17},{... | collective-permute-start | bytes 294920 | tf_op jit(solution)/shard_map/ppermute | solution.py:363
  7.1 1.3 %collective-permute-start.2 = (bf16[64,768]{1,0:T(8,128)(2,1)S(1)}, bf16[64,768]{1,0:T(8,128)(2,1)S(1)}, u32[]{:S(2)}, u32[]{:S(2)}) collective-permute-start(bf16[64,768]{1,0:T(8,128)(2,1)S(1)} %get-tuple-element.34), channel_id=1, source_target_pairs={{0,20},{4,16},{8,28},{12,24},{16,4},{20,0},{24,12},{28,8},{1,21},{... | collective-permute-start | bytes 294920 | tf_op jit(solution)/shard_map/ppermute | solution.py:363
  8.4 2.5 %collective-permute-start.3 = (bf16[64,768]{1,0:T(8,128)(2,1)S(1)}, bf16[64,768]{1,0:T(8,128)(2,1)S(1)}, u32[]{:S(2)}, u32[]{:S(2)}) collective-permute-start(bf16[64,768]{1,0:T(8,128)(2,1)S(1)} %get-tuple-element.35), channel_id=1, source_target_pairs={{0,24},{4,28},{8,16},{12,20},{16,8},{20,12},{24,0},{28,4},{1,25},{... | collective-permute-start | bytes 294920 | tf_op jit(solution)/shard_map/ppermute | solution.py:363
  10.9 1.3 %collective-permute-start.4 = (bf16[64,768]{1,0:T(8,128)(2,1)S(1)}, bf16[64,768]{1,0:T(8,128)(2,1)S(1)}, u32[]{:S(2)}, u32[]{:S(2)}) collective-permute-start(bf16[64,768]{1,0:T(8,128)(2,1)S(1)} %get-tuple-element.36), channel_id=1, source_target_pairs={{0,28},{4,24},{8,20},{12,16},{16,12},{20,8},{24,4},{28,0},{1,29},{... | collective-permute-start | bytes 294920 | tf_op jit(solution)/shard_map/ppermute | solution.py:363
  12.2 0.8 %concatenate.3 = f32[1560]{0:T(1024)S(1)} concatenate(f32[768]{0:T(1024)} %param.10, f32[768]{0:T(1024)} %param.14, f32[12]{0:T(128)} %param.13, f32[12]{0:T(128)} %param.17), dimensions={0} | concatenate | bytes 12480 | tf_op jit(solution)/shard_map/concatenate | solution.py:302
  13.0 0.1 shard_map.91
  13.1 0.4 collective-permute-start.5
  13.4 4.5 %collective-permute-done.1.refs_2_.refs_3_ = bf16[64,768]{1,0:T(8,128)(2,1)S(1)} collective-permute-done((bf16[64,768]{1,0:T(8,128)(2,1)S(1)}, bf16[64,768]{1,0:T(8,128)(2,1)S(1)}, u32[]{:S(2)}, u32[]{:S(2)}) %collective-permute-start.1) | collective-permute-done | bytes 98336 | tf_op jit(solution)/shard_map/ppermute | solution.py:363
  18.0 2.2 %collective-permute-start.6 = (bf16[64,768]{1,0:T(8,128)(2,1)S(1)}, bf16[64,768]{1,0:T(8,128)(2,1)S(1)}, u32[]{:S(2)}, u32[]{:S(2)}) collective-permute-start(bf16[64,768]{1,0:T(8,128)(2,1)S(1)} %get-tuple-element.38), channel_id=1, source_target_pairs={{0,4},{4,0},{8,12},{12,8},{16,20},{20,16},{24,28},{28,24},{1,5},{5... | collective-permute-start | bytes 294920 | tf_op jit(solution)/shard_map/ppermute | solution.py:363
  20.2 1.7 %collective-permute-done.2.refs_3_.refs_4_ = bf16[64,768]{1,0:T(8,128)(2,1)S(1)} collective-permute-done((bf16[64,768]{1,0:T(8,128)(2,1)S(1)}, bf16[64,768]{1,0:T(8,128)(2,1)S(1)}, u32[]{:S(2)}, u32[]{:S(2)}) %collective-permute-start.2) | collective-permute-done | bytes 98336 | tf_op jit(solution)/shard_map/ppermute | solution.py:363
  22.0 1.5 %shard_map.93.refs_0_ = bf16[2304,256]{1,0:T(8,128)(2,1)S(1)} custom-call(f32[1,768]{1,0:T(1,128)S(1)} %get-tuple-element.30.gain_ref, bf16[768,2304]{1,0:T(8,128)(2,1)S(1)} %copy-done.2, bf16[64,768]{1,0:T(8,128)(2,1)S(1)} %get-tuple-element.31.refs_0_.refs_1_, bf16[64,768]{1,0:T(8,128)(2,1)S(1)} %collective-permute-done.refs_1_.refs_2_, ...), custom_call_target="tpu_custom_call" | custom-call | flops 5000000000 | bytes 7000000 | tf_op jit(solution)/shard_map/pallas_call | solution.py:321
  23.5 0.0 collective-permute-done.4.refs_6_
  23.5 0.0 collective-permute-done.5.refs_7_
  23.5 0.5 collective-permute-done.6.refs_8_
  24.0 3.9 %shard_map.94 = bf16[512,768]{1,0:T(8,128)(2,1)S(1)} custom-call(f32[12,128]{1,0:T(8,128)S(1)} %get-tuple-element.29.scale_ref, f32[1,768]{1,0:T(1,128)S(1)} %get-tuple-element.30.gain_ref, bf16[768,2304]{1,0:T(8,128)(2,1)S(1)} %copy-done.2, bf16[768,768]{1,0:T(8,128)(2,1)S(1)} %copy-done.4, bf16[2304,256]{1,0:T(8,128)(2,1)S(1)} %shard_map.93.refs_0_, ...), custom_call_target="tpu_custom_call" | custom-call | flops 10000000000 | bytes 10000000 | tf_op jit(solution)/shard_map/pallas_call | solution.py:307
  27.9 0.0 copy-start
  27.9 25.1 %all_to_all.5 = bf16[32,16,768]{2,1,0:T(8,128)(2,1)S(1)} all-to-all(bf16[32,16,768]{2,1,0:T(8,128)(2,1)S(1)} %bitcast.8), channel_id=1, replica_groups=mesh['tm'=8,'patch'=4] {'tm','patch'}, dimensions={0} | all-to-all | bytes 1572864 | tf_op jit(solution)/shard_map/all_to_all | solution.py:411
  53.0 2.3 %shard_map.96 = (bf16[64,768]{1,0:T(8,128)(2,1)S(1)}, bf16[64,768]{1,0:T(8,128)(2,1)S(1)}, bf16[2304,256]{1,0:T(8,128)(2,1)S(1)}, f32[128,768]{1,0:T(8,128)S(1)}) custom-call(f32[12,128]{1,0:T(8,128)S(1)} %get-tuple-element.27.scale_ref, f32[1,768]{1,0:T(1,128)S(1)} %get-tuple-element.28.gain_ref, bf16[768,2304]{1,0:T(8,128)(2,1)S(1)} %copy-done.3, ...), custom_call_target="tpu_custom_call" | custom-call | flops 10000000000 | bytes 10000000 | tf_op jit(solution)/shard_map/pallas_call | solution.py:307
  55.3 1.5 %collective-permute-start.10 = (bf16[1,64,768]{2,1,0:T(8,128)(2,1)S(1)}, bf16[1,64,768]{2,1,0:T(8,128)(2,1)S(1)}, u32[]{:S(2)}, u32[]{:S(2)}) collective-permute-start(bf16[1,64,768]{2,1,0:T(8,128)(2,1)S(1)} %bitcast.12), channel_id=1, source_target_pairs={{0,2},{1,3},{2,0},{3,1},{4,6},{5,7},{6,4},{7,5},{8,10},{9,11},{10,... | collective-permute-start | bytes 294920 | tf_op jit(solution)/shard_map/ppermute | solution.py:363
  56.9 2.3 %shard_map.95 = (bf16[64,768]{1,0:T(8,128)(2,1)S(1)}, bf16[64,768]{1,0:T(8,128)(2,1)S(1)}, bf16[2304,256]{1,0:T(8,128)(2,1)S(1)}, f32[128,768]{1,0:T(8,128)S(1)}) custom-call(f32[12,128]{1,0:T(8,128)S(1)} %get-tuple-element.27.scale_ref, f32[1,768]{1,0:T(1,128)S(1)} %get-tuple-element.28.gain_ref, bf16[768,2304]{1,0:T(8,128)(2,1)S(1)} %copy-done.3, ...), custom_call_target="tpu_custom_call" | custom-call | flops 10000000000 | bytes 10000000 | tf_op jit(solution)/shard_map/pallas_call | solution.py:307
  59.2 1.6 %collective-permute-start.7 = (bf16[1,64,768]{2,1,0:T(8,128)(2,1)S(1)}, bf16[1,64,768]{2,1,0:T(8,128)(2,1)S(1)}, u32[]{:S(2)}, u32[]{:S(2)}) collective-permute-start(bf16[1,64,768]{2,1,0:T(8,128)(2,1)S(1)} %bitcast.10), channel_id=1, source_target_pairs={{0,2},{1,3},{2,0},{3,1},{4,6},{5,7},{6,4},{7,5},{8,10},{9,11},{10,... | collective-permute-start | bytes 294920 | tf_op jit(solution)/shard_map/ppermute | solution.py:363
  60.8 0.5 collective-permute-start.8
  61.3 2.1 %shard_map.97 = (bf16[2,64,768]{2,1,0:T(8,128)(2,1)S(1)}, bf16[2,64,768]{2,1,0:T(8,128)(2,1)S(1)}) custom-call(f32[12,128]{1,0:T(8,128)S(1)} %get-tuple-element.27.scale_ref, bf16[768,768]{1,0:T(8,128)(2,1)S(1)} %copy-done, bf16[2304,256]{1,0:T(8,128)(2,1)S(1)} %get-tuple-element.41.refs_0_, f32[128,768]{1,0:T(8,128)S(1)} %get-tuple-element.42.refs_1_, ...), custom_call_target="tpu_custom_call" | custom-call | flops 1000000 | bytes 1000 | tf_op jit(solution)/shard_map/pallas_call | solution.py:307
  63.4 0.2 collective-permute-start.9
  63.6 0.7 %shard_map.98.refs_2_ = bf16[8,64,768]{2,1,0:T(8,128)(2,1)} custom-call(bf16[1,64,768]{2,1,0:T(8,128)(2,1)S(1)} %collective-permute-done.10.refs_0_, bf16[1,64,768]{2,1,0:T(8,128)(2,1)S(1)} %collective-permute-done.11.refs_1_), custom_call_target="tpu_custom_call" | custom-call | flops 10000000000 | bytes 1000000 | tf_op jit(solution)/shard_map/pallas_call | solution.py:349
  64.3 0.6 collective-permute-done.9.refs_1_
  64.9 0.8 %shard_map.99.refs_2_ = bf16[8,64,768]{2,1,0:T(8,128)(2,1)} custom-call(bf16[2,64,768]{2,1,0:T(8,128)(2,1)S(1)} %get-tuple-element.45.refs_0_, bf16[2,64,768]{2,1,0:T(8,128)(2,1)S(1)} %collective-permute-done.9.refs_1_, bf16[8,64,768]{2,1,0:T(8,128)(2,1)} %shard_map.98.refs_2_), custom_call_target="tpu_custom_call", output_to_operand_aliasing={{}: (2, {})} | custom-call | flops 1000000 | bytes 100 | tf_op jit(solution)/shard_map/pallas_call | solution.py:349
  65.7 0.7 %collective-permute-done.8.refs_1_ = bf16[1,64,768]{2,1,0:T(8,128)(2,1)S(1)} collective-permute-done((bf16[1,64,768]{2,1,0:T(8,128)(2,1)S(1)}, bf16[1,64,768]{2,1,0:T(8,128)(2,1)S(1)}, u32[]{:S(2)}, u32[]{:S(2)}) %collective-permute-start.8) | collective-permute-done | bytes 98336 | tf_op jit(solution)/shard_map/ppermute | solution.py:363
  66.4 0.7 %shard_map.100 = bf16[8,64,768]{2,1,0:T(8,128)(2,1)} custom-call(bf16[1,64,768]{2,1,0:T(8,128)(2,1)S(1)} %collective-permute-done.7.refs_0_, bf16[1,64,768]{2,1,0:T(8,128)(2,1)S(1)} %collective-permute-done.8.refs_1_, bf16[8,64,768]{2,1,0:T(8,128)(2,1)} %shard_map.99.refs_2_), custom_call_target="tpu_custom_call", output_to_operand_aliasing={{}: (2, {})} | custom-call | flops 10000000000 | bytes 1000000 | tf_op jit(solution)/shard_map/pallas_call | solution.py:349
  (15 shorter events, 0.0 us)
Async XLA Ops:
  0.0 1.1 %copy-start.1 = (bf16[8,64,768]{2,1,0:T(8,128)(2,1)S(1)}, bf16[8,64,768]{2,1,0:T(8,128)(2,1)}, u32[]{:S(2)}) copy-start(bf16[8,64,768]{2,1,0:T(8,128)(2,1)} %tokens_ref.1) | copy-start | bytes 2359300
  1.4 11.6 %collective-permute-start = (bf16[64,768]{1,0:T(8,128)(2,1)S(1)}, bf16[64,768]{1,0:T(8,128)(2,1)S(1)}, u32[]{:S(2)}, u32[]{:S(2)}) collective-permute-start(bf16[64,768]{1,0:T(8,128)(2,1)S(1)} %get-tuple-element.32), channel_id=1, source_target_pairs={{0,8},{4,12},{8,0},{12,4},{16,24},{20,28},{24,16},{28,20},{1,9},{5... | collective-permute-start | bytes 294920 | tf_op jit(solution)/shard_map/ppermute | solution.py:363
  4.5 13.5 %collective-permute-start.1 = (bf16[64,768]{1,0:T(8,128)(2,1)S(1)}, bf16[64,768]{1,0:T(8,128)(2,1)S(1)}, u32[]{:S(2)}, u32[]{:S(2)}) collective-permute-start(bf16[64,768]{1,0:T(8,128)(2,1)S(1)} %get-tuple-element.33), channel_id=1, source_target_pairs={{0,16},{4,20},{8,24},{12,28},{16,0},{20,4},{24,8},{28,12},{1,17},{... | collective-permute-start | bytes 294920 | tf_op jit(solution)/shard_map/ppermute | solution.py:363
  7.1 14.8 %collective-permute-start.2 = (bf16[64,768]{1,0:T(8,128)(2,1)S(1)}, bf16[64,768]{1,0:T(8,128)(2,1)S(1)}, u32[]{:S(2)}, u32[]{:S(2)}) collective-permute-start(bf16[64,768]{1,0:T(8,128)(2,1)S(1)} %get-tuple-element.34), channel_id=1, source_target_pairs={{0,20},{4,16},{8,28},{12,24},{16,4},{20,0},{24,12},{28,8},{1,21},{... | collective-permute-start | bytes 294920 | tf_op jit(solution)/shard_map/ppermute | solution.py:363
  8.4 15.0 %collective-permute-start.3 = (bf16[64,768]{1,0:T(8,128)(2,1)S(1)}, bf16[64,768]{1,0:T(8,128)(2,1)S(1)}, u32[]{:S(2)}, u32[]{:S(2)}) collective-permute-start(bf16[64,768]{1,0:T(8,128)(2,1)S(1)} %get-tuple-element.35), channel_id=1, source_target_pairs={{0,24},{4,28},{8,16},{12,20},{16,8},{20,12},{24,0},{28,4},{1,25},{... | collective-permute-start | bytes 294920 | tf_op jit(solution)/shard_map/ppermute | solution.py:363
  10.9 12.6 %collective-permute-start.4 = (bf16[64,768]{1,0:T(8,128)(2,1)S(1)}, bf16[64,768]{1,0:T(8,128)(2,1)S(1)}, u32[]{:S(2)}, u32[]{:S(2)}) collective-permute-start(bf16[64,768]{1,0:T(8,128)(2,1)S(1)} %get-tuple-element.36), channel_id=1, source_target_pairs={{0,28},{4,24},{8,20},{12,16},{16,12},{20,8},{24,4},{28,0},{1,29},{... | collective-permute-start | bytes 294920 | tf_op jit(solution)/shard_map/ppermute | solution.py:363
  13.0 9.0 %copy-start.2 = (bf16[768,2304]{1,0:T(8,128)(2,1)S(1)}, bf16[768,2304]{1,0:T(8,128)(2,1)}, u32[]{:S(2)}) copy-start(bf16[768,2304]{1,0:T(8,128)(2,1)} %proj_ref.5) | copy-start | bytes 10616836
  13.1 10.4 %collective-permute-start.5 = (bf16[64,768]{1,0:T(8,128)(2,1)S(1)}, bf16[64,768]{1,0:T(8,128)(2,1)S(1)}, u32[]{:S(2)}, u32[]{:S(2)}) collective-permute-start(bf16[64,768]{1,0:T(8,128)(2,1)S(1)} %get-tuple-element.37), channel_id=1, source_target_pairs={{0,12},{4,8},{8,4},{12,0},{16,28},{20,24},{24,20},{28,16},{1,13},{... | collective-permute-start | bytes 294920 | tf_op jit(solution)/shard_map/ppermute | solution.py:363
  18.0 6.0 %collective-permute-start.6 = (bf16[64,768]{1,0:T(8,128)(2,1)S(1)}, bf16[64,768]{1,0:T(8,128)(2,1)S(1)}, u32[]{:S(2)}, u32[]{:S(2)}) collective-permute-start(bf16[64,768]{1,0:T(8,128)(2,1)S(1)} %get-tuple-element.38), channel_id=1, source_target_pairs={{0,4},{4,0},{8,12},{12,8},{16,20},{20,16},{24,28},{28,24},{1,5},{5... | collective-permute-start | bytes 294920 | tf_op jit(solution)/shard_map/ppermute | solution.py:363
  22.0 2.1 %copy-start.4 = (bf16[768,768]{1,0:T(8,128)(2,1)S(1)}, bf16[768,768]{1,0:T(8,128)(2,1)}, u32[]{:S(2)}) copy-start(bf16[768,768]{1,0:T(8,128)(2,1)} %out_ref.4) | copy-start | bytes 3538948
  24.0 29.0 %copy-start.3 = (bf16[768,2304]{1,0:T(8,128)(2,1)S(1)}, bf16[768,2304]{1,0:T(8,128)(2,1)}, u32[]{:S(2)}) copy-start(bf16[768,2304]{1,0:T(8,128)(2,1)} %proj_ref.7) | copy-start | bytes 10616836
  27.9 25.1 %copy-start = (bf16[768,768]{1,0:T(8,128)(2,1)S(1)}, bf16[768,768]{1,0:T(8,128)(2,1)}, u32[]{:S(2)}) copy-start(bf16[768,768]{1,0:T(8,128)(2,1)} %out_ref.7) | copy-start | bytes 3538948
  55.3 8.3 %collective-permute-start.10 = (bf16[1,64,768]{2,1,0:T(8,128)(2,1)S(1)}, bf16[1,64,768]{2,1,0:T(8,128)(2,1)S(1)}, u32[]{:S(2)}, u32[]{:S(2)}) collective-permute-start(bf16[1,64,768]{2,1,0:T(8,128)(2,1)S(1)} %bitcast.12), channel_id=1, source_target_pairs={{0,2},{1,3},{2,0},{3,1},{4,6},{5,7},{6,4},{7,5},{8,10},{9,11},{10,... | collective-permute-start | bytes 294920 | tf_op jit(solution)/shard_map/ppermute | solution.py:363
  56.9 6.8 %collective-permute-start.11 = (bf16[1,64,768]{2,1,0:T(8,128)(2,1)S(1)}, bf16[1,64,768]{2,1,0:T(8,128)(2,1)S(1)}, u32[]{:S(2)}, u32[]{:S(2)}) collective-permute-start(bf16[1,64,768]{2,1,0:T(8,128)(2,1)S(1)} %bitcast.11), channel_id=1, source_target_pairs={{0,3},{1,2},{2,1},{3,0},{4,7},{5,6},{6,5},{7,4},{8,11},{9,10},{10,... | collective-permute-start | bytes 294920 | tf_op jit(solution)/shard_map/ppermute | solution.py:363
  59.2 6.5 %collective-permute-start.7 = (bf16[1,64,768]{2,1,0:T(8,128)(2,1)S(1)}, bf16[1,64,768]{2,1,0:T(8,128)(2,1)S(1)}, u32[]{:S(2)}, u32[]{:S(2)}) collective-permute-start(bf16[1,64,768]{2,1,0:T(8,128)(2,1)S(1)} %bitcast.10), channel_id=1, source_target_pairs={{0,2},{1,3},{2,0},{3,1},{4,6},{5,7},{6,4},{7,5},{8,10},{9,11},{10,... | collective-permute-start | bytes 294920 | tf_op jit(solution)/shard_map/ppermute | solution.py:363
  60.8 5.7 %collective-permute-start.8 = (bf16[1,64,768]{2,1,0:T(8,128)(2,1)S(1)}, bf16[1,64,768]{2,1,0:T(8,128)(2,1)S(1)}, u32[]{:S(2)}, u32[]{:S(2)}) collective-permute-start(bf16[1,64,768]{2,1,0:T(8,128)(2,1)S(1)} %bitcast.9), channel_id=1, source_target_pairs={{0,3},{1,2},{2,1},{3,0},{4,7},{5,6},{6,5},{7,4},{8,11},{9,10},{10,... | collective-permute-start | bytes 294920 | tf_op jit(solution)/shard_map/ppermute | solution.py:363
  63.4 1.5 %collective-permute-start.9 = (bf16[2,64,768]{2,1,0:T(8,128)(2,1)S(1)}, bf16[2,64,768]{2,1,0:T(8,128)(2,1)S(1)}, u32[]{:S(2)}, u32[]{:S(2)}) collective-permute-start(bf16[2,64,768]{2,1,0:T(8,128)(2,1)S(1)} %get-tuple-element.46), channel_id=1, source_target_pairs={{0,1},{1,0},{2,3},{3,2},{4,5},{5,4},{6,7},{7,6},{8,9},{9,8},{10,11... | collective-permute-start | bytes 589832 | tf_op jit(solution)/shard_map/ppermute | solution.py:363
